TPU v7x, 256 devices: a whole 4x4x8 slice. The times are simulated.
256 devices in a mesh: col: 32 (over y, z), dom: 8 (over x, core).
Axes of the slice: x: 4, y: 4, z: 8, core: 2. Of those that a mesh axis runs over, the one named last changes fastest.
Arguments:
- source_feats: bfloat16 [65536, 128], P(('col', 'dom')), may hold values from -6 to 6
- source_scale: float32 [65536], P(('col', 'dom')), may hold values from 0.3 to 1
- dest_scale: float32 [32768], P(('col', 'dom')), may hold values from 0.01 to 0.1
- weight: bfloat16 [128, 256], replicated, may hold values from -0.5 to 0.5
- layer_bias: float32 [256], replicated, may hold values from -3 to 3
- tile_rows: int32 [40960], P(('col', 'dom')), may hold values from 0 to 31
- tile_cols: int32 [40960], P(('col', 'dom')), may hold values from 0 to 15
- tile_mask: int32 [40960, 128, 128], P(('col', 'dom')), may hold values 0 or 1
- targets: int32 [8192], P(('col', 'dom')), may hold values from 0 to 127
- upstream: bfloat16 [8192, 256], P(('col', 'dom')), may hold values from -6 to 6
Outputs:
- hidden: bfloat16 [32768, 256], P(('col', 'dom'))
- weight_grad: float32 [128, 256], replicated
- bias_grad: float32 [256], replicated
- input_grad: float32 [65536, 128], P(('col', 'dom'))
Inputs may be any that keep to these rules, and one draw needn't show every extreme that they name: `tile_rows`: block of the tile among the 32 blocks of its destination partition; some blocks are named far more often than others. `tile_cols`: block of the tile among the 16 blocks of its source group. `targets`: a row of the device's own 128 destination rows; a row may be named more than once.
All inputs are finite; a program needn't handle non-finite values. No bound on the sum of `tile_mask` on one device may be relied on, other than what follows from the above.
Results may differ from a plain program's by a relative error of at most 0.03.
Values may be sent and summed in bfloat16 or wider, within the bound.
No kernel may reach another device: no remote copies, remote signals or barrier semaphores. Data moves between devices by JAX's collectives and lax.ppermute only.
A program may use at most 128 MiB of HBM per device.

v0:
```python
import jax
import jax.numpy as jnp
from jax import lax
from jax.sharding import PartitionSpec as P


def silu_slope(values):
    sigma = jax.nn.sigmoid(values)
    return sigma * (1.0 + values * (1.0 - sigma))


def body(
    source_feats,
    source_scale,
    dest_scale,
    weight,
    layer_bias,
    tile_rows,
    tile_cols,
    tile_mask,
    targets,
    upstream,
):
    column_count = lax.axis_size("col")
    domain_count = lax.axis_size("dom")
    block_size = tile_mask.shape[1]
    features = source_feats.shape[1]
    own_rows = dest_scale.shape[0]
    source_rows = source_feats.shape[0]
    row_blocks = column_count * own_rows // block_size
    col_blocks = domain_count * source_rows // block_size
    scaled = (source_feats.astype(jnp.float32) * source_scale[:, None]).astype(jnp.bfloat16)
    sources = lax.all_gather(scaled, "dom", axis=0, tiled=True).reshape(
        col_blocks, block_size, features
    )
    edge_masks = tile_mask.astype(jnp.bfloat16)
    col_hot = (tile_cols[:, None] == jnp.arange(col_blocks, dtype=jnp.int32)[None, :]).astype(
        jnp.float32
    )
    picked = sources[tile_cols]
    product = jnp.einsum("tij,tjf->tif", edge_masks, picked, preferred_element_type=jnp.float32)
    row_hot = (tile_rows[:, None] == jnp.arange(row_blocks, dtype=jnp.int32)[None, :]).astype(
        jnp.float32
    )
    partial_value = jnp.einsum("tr,tif->rif", row_hot, product, precision=lax.Precision.HIGHEST)
    partial_value = partial_value.reshape(row_blocks * block_size, features)
    summed = lax.psum_scatter(
        partial_value.astype(jnp.bfloat16), "col", scatter_dimension=0, tiled=True
    ).astype(jnp.float32)
    aggregated = (summed * dest_scale[:, None]).astype(jnp.bfloat16)
    preact = jnp.dot(aggregated, weight, preferred_element_type=jnp.float32) + layer_bias[None, :]
    hidden = jax.nn.silu(preact).astype(jnp.bfloat16)
    slope_grad = (upstream.astype(jnp.float32) * silu_slope(preact[targets])).astype(jnp.bfloat16)
    weight_part = jnp.dot(aggregated[targets].T, slope_grad, preferred_element_type=jnp.float32)
    bias_part = jnp.sum(slope_grad.astype(jnp.float32), axis=0)
    weight_grad, bias_grad = lax.psum((weight_part, bias_part), ("col", "dom"))
    returned_term = jnp.dot(slope_grad, weight.T, preferred_element_type=jnp.float32)
    collected = jnp.zeros((own_rows, features), jnp.float32).at[targets].add(returned_term)
    local_rows = (collected * dest_scale[:, None]).astype(jnp.bfloat16)
    returned = lax.all_gather(local_rows, "col", axis=0, tiled=True)
    picked_back = returned.reshape(row_blocks, block_size, features)[tile_rows]
    back_product = jnp.einsum(
        "tij,tif->tjf", edge_masks, picked_back, preferred_element_type=jnp.float32
    )
    source_partial = jnp.einsum(
        "tc,tjf->cjf", col_hot, back_product, precision=lax.Precision.HIGHEST
    )
    source_partial = source_partial.reshape(col_blocks * block_size, features)
    source_total = lax.psum_scatter(
        source_partial.astype(jnp.bfloat16), "dom", scatter_dimension=0, tiled=True
    ).astype(jnp.float32)
    input_grad = source_total * source_scale[:, None]
    return (hidden, weight_grad, bias_grad, input_grad)


def solution(mesh):
    placed = (
        P(("col", "dom"), None),
        P(("col", "dom")),
        P(("col", "dom")),
        P(),
        P(),
        P(("col", "dom")),
        P(("col", "dom")),
        P(("col", "dom"), None, None),
        P(("col", "dom")),
        P(("col", "dom"), None),
    )
    return jax.shard_map(
        body,
        mesh=mesh,
        in_specs=placed,
        out_specs=(P(("col", "dom"), None), P(), P(), P(("col", "dom"), None)),
        check_vma=False,
    )
```

profile of v0, /device:TPU:1, one launch (start us, length us, event | category | flops | bytes accessed | tf_op | source)
XLA Modules:
  0.0 721.4 jit_solution(14913614556258641829)
XLA Ops:
  7.2 0.0 reduce-scatter.3.cloned.1.call-start
  7.2 0.7 compare_select_fusion.1
  7.9 0.9 multiply_convert_fusion.1
  8.9 16.2 %all_gather.6 = bf16[2048,128]{1,0:T(8,128)(2,1)S(1)} all-gather(bf16[256,128]{1,0:T(8,128)(2,1)S(1)} %multiply_convert_fusion.1), channel_id=1, replica_groups=mesh['col'=32,'dom'=8] {'dom'}, dimensions={0}, use_global_device_ids=true | all-gather | bytes 589824 | tf_op jit(solution)/shard_map/all_gather | solution.py:33
  25.1 7.7 %gather_fusion = bf16[160,128,128]{2,1,0:T(8,128)(2,1)} fusion(bf16[16,128,128]{2,1,0:T(8,128)(2,1)S(1)} %bitcast.28, s32[1024]{0:T(1024)S(1)} %pad_clamp_fusion.2), kind=kCustom, calls=%fused_computation | custom fusion | bytes 10486400 | tf_op jit(solution)/shard_map/gather | solution.py:40
  32.8 13.3 %fusion.6 = f32[160,128,128]{2,1,0:T(8,128)} fusion(bf16[160,128,128]{2,1,0:T(8,128)(2,1)} %gather_fusion, s32[160,128,128]{2,1,0:T(8,128)} %param.17), kind=kOutput, calls=%fused_computation.11 | convolution fusion | flops 673710080 | bytes 26214400 | tf_op jit(solution)/shard_map/tij,tjf->tif/dot_general | solution.py:41
  46.1 11.5 %copy.16 = f32[160,128,128]{1,0,2:T(8,128)} copy(f32[160,128,128]{2,1,0:T(8,128)} %fusion.6) | data formatting | bytes 20971520 | tf_op jit(solution)/shard_map/tij,tjf->tif/dot_general | solution.py:41
  57.7 7.9 %fusion.8 = bf16[32,128,128]{2,0,1:T(8,128)(2,1)S(1)} fusion(f32[160,128,128]{1,0,2:T(8,128)} %copy.16, s32[160]{0:T(256)S(1)} %copy-done.3), kind=kOutput, calls=%fused_computation.13 | convolution fusion | flops 1007162368 | bytes 11534976 | tf_op jit(solution)/shard_map/tr,tif->rif/dot_general | solution.py:45
  65.5 1.4 copy.14
  66.9 0.0 all-gather.2.cloned.1.call-start
  67.0 209.5 %reduce-scatter.3.cloned.1.call-done = bf16[128,128]{1,0:T(8,128)(2,1)} async-done(((bf16[4096,128]{1,0:T(8,128)(2,1)}), bf16[128,128]{1,0:T(8,128)(2,1)}) %reduce-scatter.3.cloned.1.call-update) | async-done | bytes 32784 | tf_op jit(solution)/shard_map/reduce_scatter | solution.py:47
  276.5 0.8 multiply_convert_fusion.3
  277.4 0.8 multiply_convert_fusion
  278.2 0.6 gather_fusion.2
  278.9 0.1 fusion.23
  279.0 0.7 scatter_custom_fusion
  279.7 0.7 multiply_convert_fusion.2
  280.5 0.2 reduce-scatter.5.cloned.1.call-start
  280.7 75.4 %all-gather.2.cloned.1.call-done = bf16[4096,128]{1,0:T(8,128)(2,1)} async-done(((bf16[128,128]{1,0:T(8,128)(2,1)}), bf16[4096,128]{1,0:T(8,128)(2,1)}) %all-gather.2.cloned.1.call-update) | async-done | bytes 1048592 | tf_op jit(solution)/shard_map/all_gather | solution.py:60
  356.1 9.0 %gather_fusion.3 = bf16[160,128,128]{2,1,0:T(8,128)(2,1)} fusion(bf16[32,128,128]{2,1,0:T(8,128)(2,1)} %bitcast.29, s32[1024]{0:T(1024)S(1)} %pad_clamp_fusion), kind=kCustom, calls=%fused_computation.3 | custom fusion | bytes 10486400 | tf_op jit(solution)/shard_map/gather | solution.py:61
  365.1 11.4 %fusion.4 = f32[160,128,128]{2,1,0:T(8,128)} fusion(bf16[160,128,128]{2,1,0:T(8,128)(2,1)} %gather_fusion.3, s32[160,128,128]{2,1,0:T(8,128)} %param.17), kind=kOutput, calls=%fused_computation.9 | convolution fusion | flops 673710080 | bytes 26214400 | tf_op jit(solution)/shard_map/tij,tif->tjf/dot_general | solution.py:62
  376.5 11.5 %copy.17 = f32[160,128,128]{1,0,2:T(8,128)} copy(f32[160,128,128]{2,1,0:T(8,128)} %fusion.4) | data formatting | bytes 20971520 | tf_op jit(solution)/shard_map/tij,tif->tjf/dot_general | solution.py:62
  388.0 7.4 %fusion.11 = bf16[16,128,128]{2,0,1:T(8,128)(2,1)S(1)} fusion(f32[160,128,128]{1,0,2:T(8,128)} %copy.17, s32[160]{0:T(256)S(1)} %copy-done.4), kind=kOutput, calls=%fused_computation.14 | convolution fusion | flops 503581184 | bytes 11010688 | tf_op jit(solution)/shard_map/tc,tjf->cjf/dot_general | solution.py:65
  395.3 0.9 copy.15
  396.3 0.0 all-reduce.2.cloned.1.call-start
  396.3 0.6 gather_fusion.1
  396.9 79.0 %psum.15 = f32[256]{0:T(256)} all-reduce(f32[256]{0:T(256)S(1)} %get-tuple-element.4), channel_id=1, replica_groups=mesh['col'=32,'dom'=8] {'col','dom'}, use_global_device_ids=true, to_apply=%region_3.4 | all-reduce | flops 256 | bytes 2048 | tf_op jit(solution)/shard_map/psum | solution.py:56
  475.9 0.9 fusion.22
  476.8 0.0 reduce-scatter.5.cloned.1.call-done
  476.9 1.6 convert_multiply_fusion
  478.4 234.8 %all-reduce.2.cloned.1.call-done = f32[128,256]{1,0:T(8,128)} async-done(((f32[128,256]{1,0:T(8,128)}), f32[128,256]{1,0:T(8,128)}) %all-reduce.2.cloned.1.call-update) | async-done | bytes 131088 | tf_op jit(solution)/shard_map/psum | solution.py:56
  713.3 1.6 copy.19
  (26 shorter events, 0.2 us)
Async XLA Ops:
  7.2 270.2 %copy-start = (bf16[128,256]{1,0:T(8,128)(2,1)S(1)}, bf16[128,256]{1,0:T(8,128)(2,1)}, u32[]{:S(2)}) copy-start(bf16[128,256]{1,0:T(8,128)(2,1)} %param.13) | copy-start | bytes 196612
  7.2 269.4 %reduce-scatter.3.cloned.1.call-start = ((), (), s32[]{:S(2)}) async-start(), calls=%async_computation.2 | async-start | bytes 1081344 | tf_op jit(solution)/shard_map/reduce_scatter | solution.py:47
  46.1 11.5 %copy-start.3 = (s32[160]{0:T(256)S(1)}, s32[160]{0:T(256)}, u32[]{:S(2)}) copy-start(s32[160]{0:T(256)} %param.15) | copy-start | bytes 1924
  57.6 9.4 %copy-start.7 = (s32[32]{0:T(128)S(1)}, s32[32]{0:T(128)}, u32[]{:S(2)}) copy-start(s32[32]{0:T(128)} %param.18) | copy-start | bytes 388
  57.6 218.9 %copy-start.5 = (f32[128]{0:T(128)S(1)}, f32[128]{0:T(128)}, u32[]{:S(2)}) copy-start(f32[128]{0:T(128)} %param.12) | copy-start | bytes 1540
  57.6 219.8 %copy-start.6 = (f32[256]{0:T(256)S(1)}, f32[256]{0:T(256)}, u32[]{:S(2)}) copy-start(f32[256]{0:T(256)} %param.14) | copy-start | bytes 3076
  57.6 221.2 %copy-start.1 = (bf16[32,256]{1,0:T(8,128)(2,1)S(1)}, bf16[32,256]{1,0:T(8,128)(2,1)}, u32[]{:S(2)}) copy-start(bf16[32,256]{1,0:T(8,128)(2,1)} %param.19) | copy-start | bytes 49156
  66.9 289.2 %all-gather.2.cloned.1.call-start = ((), (), s32[]{:S(2)}) async-start(), calls=%async_computation.4 | async-start | bytes 1081344 | tf_op jit(solution)/shard_map/all_gather | solution.py:60
  280.5 196.4 %reduce-scatter.5.cloned.1.call-start = ((), (), s32[]{:S(2)}) async-start(), calls=%async_computation.5 | async-start | bytes 589824 | tf_op jit(solution)/shard_map/reduce_scatter | solution.py:69
  376.5 11.5 %copy-start.4 = (s32[160]{0:T(256)S(1)}, s32[160]{0:T(256)}, u32[]{:S(2)}) copy-start(s32[160]{0:T(256)} %param.16) | copy-start | bytes 1924
  388.0 88.9 %copy-start.2 = (f32[256]{0:T(256)S(1)}, f32[256]{0:T(256)}, u32[]{:S(2)}) copy-start(f32[256]{0:T(256)} %param.11) | copy-start | bytes 3076
  396.3 317.0 %all-reduce.2.cloned.1.call-start = ((), (), s32[]{:S(2)}) async-start(), calls=%async_computation.3 | async-start | bytes 262144 | tf_op jit(solution)/shard_map/psum | solution.py:56
Sparse Core Ops, SparseCore 0:
  67.0 209.4 reduce-scatter.2
  280.6 75.4 all-gather.1
  396.4 33.3 reduce-scatter.4
  476.9 236.2 all-reduce.1
where the time goes:
time: 722 us; the launch traced here: 721 us
  waiting for transfers between devices  520 us (72%)
  blocking collectives  95.2 us (13%)
  local copies, waits for them, and re-layouts  44.8 us (6%)
  matrix products  41.7 us (6%)
  between operations  13.9 us (2%)
    psum x1, waiting for transfers between devices, body(): weight_grad, bias_grad = lax.psum((weight_part, bias_part), ('col', 'dom'))  235 us
    reduce_scatter x1, waiting for transfers between devices, body(): lax.psum_scatter(partial_value.astype(jnp.bfloat16), 'col', scatter_dimen...  210 us
    psum x1, blocking collectives, body(): weight_grad, bias_grad = lax.psum((weight_part, bias_part), ('col', 'dom'))  79 us
    all_gather x1, waiting for transfers between devices, body(): returned = lax.all_gather(local_rows, 'col', axis=0, tiled=True)  75.4 us
    all_gather x1, blocking collectives, body(): lax.all_gather(scaled, 'dom', axis=0, tiled=True)  16.2 us
  transfers between devices with their start and end apart: 4, of which 3 were waited for; matrix products, arithmetic and copies ran while one was open for 0% of the time, Pallas kernels for 0%

commit v1 on v0

v1 whole, which is shorter than its diff:
```python
import jax
import jax.numpy as jnp
from jax import lax
from jax.experimental import pallas as pl
from jax.experimental.pallas import tpu as pltpu
from jax.sharding import PartitionSpec as P

NY, NZ, NX, NCORE = 4, 8, 4, 2
COL, DOM = NY * NZ, NX * NCORE
BLK = 128
F = 128
HID = 256
TGT = 32
VMEM = pl.BlockSpec(memory_space=pltpu.VMEM)
SMEM = pl.BlockSpec(memory_space=pltpu.SMEM)
PARAMS = pltpu.CompilerParams(vmem_limit_bytes=48 * 1024 * 1024)
F32, BF16 = jnp.float32, jnp.bfloat16
EXTRA = 32


def call(kernel, outs, ins, scratch=(), flops=0, moved=0):
    return pl.pallas_call(
        kernel,
        out_shape=outs,
        in_specs=ins,
        out_specs=[VMEM] * len(outs),
        scratch_shapes=list(scratch),
        compiler_params=PARAMS,
        cost_estimate=pl.CostEstimate(flops=flops, bytes_accessed=moved, transcendentals=0),
    )


def sds(shape, dtype):
    return jax.ShapeDtypeStruct(shape, dtype)


def exchange_dom(value, distance):
    pairs = [(i, i ^ distance) for i in range(DOM)]
    return lax.ppermute(value, "dom", pairs)


def exchange_y(value, distance):
    pairs = [(i, (((i // NZ) ^ distance) * NZ) + i % NZ) for i in range(COL)]
    return lax.ppermute(value, "col", pairs)


def forward_kernel(place, rows, cols, mask, *refs):
    pieces, outs = refs[:DOM], refs[DOM : DOM + NY]
    sources, totals = refs[DOM + NY :]
    my_y, my_dom = place[0], place[1]
    for k in range(DOM):
        at = my_dom ^ k
        sources[2 * at] = pieces[k][0:BLK, :]
        sources[2 * at + 1] = pieces[k][BLK:, :]
    totals[...] = jnp.zeros_like(totals)
    tiles = mask.shape[0]
    step = 4

    def tile_step(i, carry):
        products = []
        for u in range(step):
            t = i * step + u
            edges = mask[t].astype(F32).astype(BF16)
            products.append(
                jnp.dot(edges, sources[cols[t]], preferred_element_type=F32)
            )
        for u in range(step):
            r = rows[i * step + u]
            totals[r] = totals[r] + products[u]
        return carry

    lax.fori_loop(0, tiles // step, tile_step, 0)
    for k in range(NY):
        base = (my_y ^ k) * NZ
        for z in range(NZ):
            outs[k][z * BLK : (z + 1) * BLK, :] = totals[base + z].astype(BF16)


def y_sum_kernel(own, a, b, c, out):
    total = (own[...].astype(F32) + a[...].astype(F32)) + (b[...].astype(F32) + c[...].astype(F32))
    out[...] = total.astype(BF16)


def column(row):
    return jnp.transpose(jnp.broadcast_to(row, (BLK, BLK)))


def sigmoid(v):
    return 1.0 / (1.0 + jnp.exp(-v))


def dense_kernel(parts, dest_scale, weight, bias, targets, upstream, hidden, packed):
    summed = parts[0].astype(F32)
    for z in range(1, NZ):
        summed = summed + parts[z].astype(F32)
    scale = column(dest_scale[...])
    aggregated = (summed * scale).astype(BF16)
    w = weight[...]
    preact = jnp.dot(aggregated, w, preferred_element_type=F32) + bias[...]
    hidden[...] = (preact * sigmoid(preact)).astype(BF16)
    wanted = targets[...]
    row_ids = lax.broadcasted_iota(jnp.int32, (BLK, TGT), 0)
    chosen = (row_ids == wanted).astype(F32)
    chosen_b = chosen.astype(BF16)
    agg_t = lax.dot_general(
        chosen_b, aggregated, (((0,), (0,)), ((), ())), preferred_element_type=F32
    ).astype(BF16)
    pre_t = jnp.dot(agg_t, w, preferred_element_type=F32) + bias[...]
    s = sigmoid(pre_t)
    slope = (upstream[...].astype(F32) * (s * (1.0 + pre_t * (1.0 - s)))).astype(BF16)
    weight_part = lax.dot_general(
        agg_t, slope, (((0,), (0,)), ((), ())), preferred_element_type=F32
    )
    bias_part = jnp.sum(slope.astype(F32), axis=0, keepdims=True)
    term = lax.dot_general(
        slope, w, (((1,), (1,)), ((), ())), preferred_element_type=F32
    )
    same = lax.dot_general(
        chosen_b, chosen_b, (((0,), (0,)), ((), ())), preferred_element_type=F32
    )
    collected = jnp.dot(
        same, term, preferred_element_type=F32, precision=lax.Precision.HIGHEST
    )
    scale_t = lax.dot_general(
        chosen, scale, (((0,), (0,)), ((), ())), preferred_element_type=F32,
        precision=lax.Precision.HIGHEST,
    )
    k_row = lax.broadcasted_iota(jnp.int32, (TGT, TGT), 0)
    k_col = lax.broadcasted_iota(jnp.int32, (TGT, TGT), 1)
    earlier = jnp.sum(jnp.where(k_col < k_row, same, 0.0), axis=1, keepdims=True)
    returned = jnp.where(earlier > 0.0, 0.0, collected * scale_t).astype(BF16)
    names = jnp.concatenate([wanted.astype(F32), jnp.zeros((1, BLK - TGT), F32)], axis=1)
    bias_hi = bias_part.astype(BF16).astype(F32)
    bias_lo = bias_part - bias_hi
    sundry = jnp.concatenate(
        [
            names,
            bias_hi[:, :BLK],
            bias_hi[:, BLK:],
            bias_lo[:, :BLK],
            bias_lo[:, BLK:],
            jnp.zeros((3, BLK), F32),
        ],
        axis=0,
    )
    for c in range(COL):
        at, side = 8 * (c // 2), BLK * (c % 2)
        packed[c, 0:TGT, :] = returned
        chunk = weight_part[at : at + 8, side : side + BLK]
        packed[c, TGT : TGT + 16, :] = jnp.concatenate([chunk, sundry], axis=0).astype(BF16)


def split(value):
    high = value.astype(BF16)
    low = (value - high.astype(F32)).astype(BF16)
    return high, low


def joined(high, low):
    return high.astype(F32) + low.astype(F32)


def backward_kernel(place, rows, cols, mask, packed, own, other, returned, totals):
    my_core = place[2]
    row_ids = lax.broadcasted_iota(jnp.int32, (BLK, TGT), 0)

    def unpack(c, grads):
        extra = packed[c, TGT : TGT + 16, :].astype(F32)
        wanted = extra[8:9, :TGT].astype(jnp.int32)
        chosen = (row_ids == wanted).astype(BF16)
        returned[c] = lax.dot_general(
            packed[c, 0:TGT, :], chosen, (((0,), (1,)), ((), ())), preferred_element_type=F32
        ).astype(BF16)
        return grads + extra

    grads = lax.fori_loop(0, COL, unpack, jnp.zeros((16, BLK), F32))
    high, low = split(grads)
    for ref in (own, other):
        ref[NX * 256 : NX * 256 + 16, :] = high
        ref[NX * 256 + 16 :, :] = low
    totals[...] = jnp.zeros_like(totals)
    tiles = mask.shape[0]
    step = 4

    def tile_step(i, carry):
        products = []
        for u in range(step):
            t = i * step + u
            edges = mask[t].astype(F32).astype(BF16)
            products.append(
                jnp.dot(returned[rows[t]], edges, preferred_element_type=F32)
            )
        for u in range(step):
            c = cols[i * step + u]
            totals[c] = totals[c] + products[u]
        return carry

    lax.fori_loop(0, tiles // step, tile_step, 0)
    for x in range(NX):
        for half in range(2):
            rows_at = pl.ds(x * 256 + half * BLK, BLK)
            for ref, core in ((own, my_core), (other, 1 - my_core)):
                block = (x * NCORE + core) * 2 + half
                ref[rows_at, :] = jnp.transpose(totals[block]).astype(BF16)


def core_sum_kernel(place, own, got, *outs):
    my_x = place[3]
    at = NX * 256
    grads = joined(own[at : at + 16, :], own[at + 16 :, :]) + joined(
        got[at : at + 16, :], got[at + 16 :, :]
    )
    high, low = split(grads)
    for k in range(NX):
        rows_at = pl.ds(pl.multiple_of((my_x ^ k) * 256, 256), 256)
        total = own[rows_at, :].astype(F32) + got[rows_at, :].astype(F32)
        outs[k][0:256, :] = total.astype(BF16)
        outs[k][256:272, :] = high
        outs[k][272:, :] = low


def finish_kernel(a, b, c, d, source_scale, grad, chunks, bias):
    for half in range(2):
        at = slice(half * BLK, (half + 1) * BLK)
        total = (a[at, :].astype(F32) + b[at, :].astype(F32)) + (
            c[at, :].astype(F32) + d[at, :].astype(F32)
        )
        grad[at, :] = total * column(source_scale[:, at])
    parts = [joined(ref[256:272, :], ref[272:, :]) for ref in (a, b, c, d)]
    grads = (parts[0] + parts[1]) + (parts[2] + parts[3])
    for i in range(COL):
        chunks[i] = grads[0:8, :]
    bias[:, :BLK] = grads[9:10, :] + grads[11:12, :]
    bias[:, BLK:] = grads[10:11, :] + grads[12:13, :]


def body(
    source_feats,
    source_scale,
    dest_scale,
    weight,
    layer_bias,
    tile_rows,
    tile_cols,
    tile_mask,
    targets,
    upstream,
):
    my_col, my_dom = lax.axis_index("col"), lax.axis_index("dom")
    place = jnp.stack([my_col >> 3, my_dom, my_dom & 1, my_dom >> 1]).astype(jnp.int32)
    tiles = tile_mask.shape[0]
    scaled = (source_feats.astype(F32) * source_scale[:, None]).astype(BF16)
    pieces = [scaled] + [exchange_dom(scaled, k) for k in range(1, DOM)]
    partials = call(
        forward_kernel,
        [sds((NZ * BLK, F), BF16)] * NY,
        [SMEM] * 3 + [VMEM] * (1 + DOM),
        [pltpu.VMEM((DOM * 2, BLK, F), BF16), pltpu.VMEM((COL, BLK, F), F32)],
        flops=2 * tiles * BLK**3,
        moved=tiles * BLK * BLK * 4,
    )(place, tile_rows, tile_cols, tile_mask, *pieces)
    arrived = [exchange_y(partials[k], k) for k in range(1, NY)]
    (line,) = call(
        y_sum_kernel, [sds((NZ * BLK, F), BF16)], [VMEM] * NY, moved=5 * NZ * BLK * F * 2
    )(partials[0], *arrived)
    groups = [[y * NZ + z for z in range(NZ)] for y in range(NY)]
    parts = lax.all_to_all(
        line.reshape(NZ, BLK, F), "col", 0, 0, axis_index_groups=groups, tiled=True
    )
    hidden, packed = call(
        dense_kernel,
        [sds((BLK, HID), BF16), sds((COL, TGT + 16, F), BF16)],
        [VMEM] * 6,
    )(
        parts,
        dest_scale.reshape(1, BLK),
        weight,
        layer_bias.reshape(1, HID),
        targets.reshape(1, TGT),
        upstream,
    )
    gathered = lax.all_to_all(packed, "col", 0, 0, tiled=True)
    own, other = call(
        backward_kernel,
        [sds((NX * 256 + EXTRA, F), BF16)] * 2,
        [SMEM] * 3 + [VMEM] * 2,
        [pltpu.VMEM((COL, F, BLK), BF16), pltpu.VMEM((DOM * 2, F, BLK), F32)],
        flops=2 * tiles * BLK**3,
        moved=tiles * BLK * BLK * 4,
    )(place, tile_rows, tile_cols, tile_mask, gathered)
    got = exchange_dom(other, 1)
    by_x = call(
        core_sum_kernel, [sds((256 + EXTRA, F), BF16)] * NX, [SMEM, VMEM, VMEM]
    )(place, own, got)
    from_x = [exchange_dom(by_x[k], 2 * k) for k in range(1, NX)]
    input_grad, chunks, bias_grad = call(
        finish_kernel,
        [sds((256, F), F32), sds((COL, 8, BLK), F32), sds((1, HID), F32)],
        [VMEM] * 5,
    )(by_x[0], *from_x, source_scale.reshape(1, 256))
    spread = lax.all_to_all(chunks, "col", 0, 0, tiled=True)
    weight_grad = spread.reshape(F // 8, 2, 8, BLK).transpose(0, 2, 1, 3).reshape(F, HID)
    return hidden, weight_grad, bias_grad.reshape(HID), input_grad


def solution(mesh):
    placed = (
        P(("col", "dom"), None),
        P(("col", "dom")),
        P(("col", "dom")),
        P(),
        P(),
        P(("col", "dom")),
        P(("col", "dom")),
        P(("col", "dom"), None, None),
        P(("col", "dom")),
        P(("col", "dom"), None),
    )
    return jax.shard_map(
        body,
        mesh=mesh,
        in_specs=placed,
        out_specs=(P(("col", "dom"), None), P(), P(), P(("col", "dom"), None)),
        check_vma=False,
    )
```

time: 722 us -> 127 us (0.18)
  waiting for transfers between devices: 520 us -> 21.7 us
  blocking collectives: 95.2 us -> 43.9 us
  local copies, waits for them, and re-layouts: 44.8 us -> 2.05 us
  matrix products: 41.7 us -> 0 us
  Pallas kernels: 0 us -> 31.6 us
  starting transfers between devices: 0.34 us -> 24.8 us
  between operations: 13.9 us -> 0.76 us
    psum x1 -> x0, waiting for transfers between devices: 235 us -> none  [body(): weight_grad, bias_grad = lax.psum((weight_part, bias_part), ('col', 'dom'))]
    reduce_scatter x2 -> x0, waiting for transfers between devices: 210 us -> none  [the longest x1 210 us: body(): lax.psum_scatter(partial_value.astype(jnp.bfloat16), 'col', scatter_dimen...]
    psum x1 -> x0, blocking collectives: 79 us -> none  [body(): weight_grad, bias_grad = lax.psum((weight_part, bias_part), ('col', 'dom'))]
    all_gather x1 -> x0, waiting for transfers between devices: 75.4 us -> none  [body(): returned = lax.all_gather(local_rows, 'col', axis=0, tiled=True)]
    all_to_all x0 -> x3, blocking collectives: none -> 43.9 us  [the longest x1 17.4 us: body(): lax.all_to_all(line.reshape(NZ, BLK, F), 'col', 0, 0, axis_index_groups=g...]
    dot_general x7 -> x0, matrix products: 41.7 us -> none  [the longest x1 13.3 us: body(): jnp.einsum('tij,tjf->tif', edge_masks, picked, preferred_element_type=jnp...]
    pallas_call x0 -> x6, Pallas kernels: none -> 31.6 us  [the longest x1 17.5 us: body(): call(backward_kernel, [sds((NX * 256 + EXTRA, F), BF16)] * 2, [SMEM] * 3...]
    ppermute x0 -> x14, starting transfers between devices: none -> 24.8 us  [the longest x11 20.8 us: exchange_dom(): return lax.ppermute(value, 'dom', pairs)]
  transfers between devices with their start and end apart: 4 -> 14, of which waited for: 3 -> 9; matrix products, arithmetic and copies ran while one was open for 0% -> 0% of each run, Pallas kernels for 0% -> 0%
where the time goes in v1:
time: 127 us; the launch traced here: 126 us
  blocking collectives  43.9 us (35%)
  Pallas kernels  31.6 us (25%)
  starting transfers between devices  24.8 us (20%)
  waiting for transfers between devices  21.7 us (17%)
  local copies, waits for them, and re-layouts  2.05 us (2%)
    ppermute x11, starting transfers between devices, exchange_dom(): return lax.ppermute(value, 'dom', pairs)  20.8 us
    pallas_call x1, Pallas kernels, body(): call(backward_kernel, [sds((NX * 256 + EXTRA, F), BF16)] * 2, [SMEM] * 3...  17.5 us
    all_to_all x1, blocking collectives, body(): lax.all_to_all(line.reshape(NZ, BLK, F), 'col', 0, 0, axis_index_groups=g...  17.4 us
    all_to_all x1, blocking collectives, body(): gathered = lax.all_to_all(packed, 'col', 0, 0, tiled=True)  13.3 us
    all_to_all x1, blocking collectives, body(): spread = lax.all_to_all(chunks, 'col', 0, 0, tiled=True)  13.1 us
    ppermute x3, waiting for transfers between devices, exchange_y(): return lax.ppermute(value, 'col', pairs)  12.9 us
    pallas_call x1, Pallas kernels, body(): call(forward_kernel, [sds((NZ * BLK, F), BF16)] * NY, [SMEM] * 3 + [VMEM]...  11.7 us
    ppermute x11, waiting for transfers between devices, exchange_dom(): return lax.ppermute(value, 'dom', pairs)  8.85 us
  transfers between devices with their start and end apart: 14, of which 9 were waited for; matrix products, arithmetic and copies ran while one was open for 0% of the time, Pallas kernels for 0%

profile of v1, /device:TPU:1, one launch (start us, length us, event | category | flops | bytes accessed | tf_op | source)
XLA Modules:
  0.0 125.8 jit_solution(10160584927276568625)
XLA Ops:
  0.7 1.0 multiply_convert_fusion.refs_0_
  1.7 4.0 %collective-permute-start.6 = (bf16[256,128]{1,0:T(8,128)(2,1)S(1)}, bf16[256,128]{1,0:T(8,128)(2,1)S(1)}, u32[]{:S(2)}, u32[]{:S(2)}) collective-permute-start(bf16[256,128]{1,0:T(8,128)(2,1)S(1)} %multiply_convert_fusion.refs_0_), channel_id=1, source_target_pairs={{0,7},{1,6},{2,5},{3,4},{4,3},{5,2},{6,1},{7,0},{8,15},{9,14},{10,... | collective-permute-start | bytes 196616 | tf_op jit(solution)/shard_map/ppermute | solution.py:39
  5.7 1.9 %collective-permute-start.5 = (bf16[256,128]{1,0:T(8,128)(2,1)S(1)}, bf16[256,128]{1,0:T(8,128)(2,1)S(1)}, u32[]{:S(2)}, u32[]{:S(2)}) collective-permute-start(bf16[256,128]{1,0:T(8,128)(2,1)S(1)} %multiply_convert_fusion.refs_0_), channel_id=1, source_target_pairs={{0,6},{1,7},{2,4},{3,5},{4,2},{5,3},{6,0},{7,1},{8,14},{9,15},{10,... | collective-permute-start | bytes 196616 | tf_op jit(solution)/shard_map/ppermute | solution.py:39
  7.6 1.4 %collective-permute-start.3 = (bf16[256,128]{1,0:T(8,128)(2,1)S(1)}, bf16[256,128]{1,0:T(8,128)(2,1)S(1)}, u32[]{:S(2)}, u32[]{:S(2)}) collective-permute-start(bf16[256,128]{1,0:T(8,128)(2,1)S(1)} %multiply_convert_fusion.refs_0_), channel_id=1, source_target_pairs={{0,4},{1,5},{2,6},{3,7},{4,0},{5,1},{6,2},{7,3},{8,12},{9,13},{10,... | collective-permute-start | bytes 196616 | tf_op jit(solution)/shard_map/ppermute | solution.py:39
  9.0 0.4 collective-permute-start.2
  9.4 3.2 %collective-permute-start.1 = (bf16[256,128]{1,0:T(8,128)(2,1)S(1)}, bf16[256,128]{1,0:T(8,128)(2,1)S(1)}, u32[]{:S(2)}, u32[]{:S(2)}) collective-permute-start(bf16[256,128]{1,0:T(8,128)(2,1)S(1)} %multiply_convert_fusion.refs_0_), channel_id=1, source_target_pairs={{0,2},{1,3},{2,0},{3,1},{4,6},{5,7},{6,4},{7,5},{8,10},{9,11},{10,... | collective-permute-start | bytes 196616 | tf_op jit(solution)/shard_map/ppermute | solution.py:39
  12.7 0.3 collective-permute-done.4.refs_5_
  13.0 0.7 collective-permute-done.2.refs_3_
  13.7 2.1 %collective-permute-done.1.refs_2_ = bf16[256,128]{1,0:T(8,128)(2,1)S(1)} collective-permute-done((bf16[256,128]{1,0:T(8,128)(2,1)S(1)}, bf16[256,128]{1,0:T(8,128)(2,1)S(1)}, u32[]{:S(2)}, u32[]{:S(2)}) %collective-permute-start.1) | collective-permute-done | bytes 65568 | tf_op jit(solution)/shard_map/ppermute | solution.py:39
  15.8 0.7 copy-done.2
  16.5 0.7 copy-done.4
  17.2 11.7 %shard_map.129 = (bf16[1024,128]{1,0:T(8,128)(2,1)S(1)}, bf16[1024,128]{1,0:T(8,128)(2,1)S(1)}, bf16[1024,128]{1,0:T(8,128)(2,1)S(1)}, bf16[1024,128]{1,0:T(8,128)(2,1)S(1)}) custom-call(s32[4]{0:T(128)S(1)} %pad_add_fusion.place, s32[160]{0:T(256)S(1)} %copy-done.2, s32[160]{0:T(256)S(1)} %copy-done.4, s32[160,128,128]{2,1,0:T(8,128)} %mask.3, ...), custom_call_target="tpu_custom_call" | custom-call | flops 671088640 | bytes 10485760 | tf_op jit(solution)/shard_map/pallas_call | solution.py:254
  28.8 0.8 collective-permute-start.7
  29.6 2.6 %collective-permute-start.8 = (bf16[1024,128]{1,0:T(8,128)(2,1)S(1)}, bf16[1024,128]{1,0:T(8,128)(2,1)S(1)}, u32[]{:S(2)}, u32[]{:S(2)}) collective-permute-start(bf16[1024,128]{1,0:T(8,128)(2,1)S(1)} %get-tuple-element.21), channel_id=1, source_target_pairs={{0,128},{8,136},{16,144},{24,152},{32,160},{40,168},{48,176},{56,1... | collective-permute-start | bytes 786440 | tf_op jit(solution)/shard_map/ppermute | solution.py:44
  32.3 0.5 collective-permute-start.9
  32.8 3.6 %collective-permute-done.7.a = bf16[1024,128]{1,0:T(8,128)(2,1)S(1)} collective-permute-done((bf16[1024,128]{1,0:T(8,128)(2,1)S(1)}, bf16[1024,128]{1,0:T(8,128)(2,1)S(1)}, u32[]{:S(2)}, u32[]{:S(2)}) %collective-permute-start.7) | collective-permute-done | bytes 262176 | tf_op jit(solution)/shard_map/ppermute | solution.py:44
  36.4 6.9 %collective-permute-done.8.b = bf16[1024,128]{1,0:T(8,128)(2,1)S(1)} collective-permute-done((bf16[1024,128]{1,0:T(8,128)(2,1)S(1)}, bf16[1024,128]{1,0:T(8,128)(2,1)S(1)}, u32[]{:S(2)}, u32[]{:S(2)}) %collective-permute-start.8) | collective-permute-done | bytes 262176 | tf_op jit(solution)/shard_map/ppermute | solution.py:44
  43.3 2.3 %collective-permute-done.9.c = bf16[1024,128]{1,0:T(8,128)(2,1)S(1)} collective-permute-done((bf16[1024,128]{1,0:T(8,128)(2,1)S(1)}, bf16[1024,128]{1,0:T(8,128)(2,1)S(1)}, u32[]{:S(2)}, u32[]{:S(2)}) %collective-permute-start.9) | collective-permute-done | bytes 262176 | tf_op jit(solution)/shard_map/ppermute | solution.py:44
  45.8 17.4 %all_to_all.15.parts = bf16[8,128,128]{2,1,0:T(8,128)(2,1)S(1)} all-to-all(bf16[8,128,128]{2,1,0:T(8,128)(2,1)S(1)} %bitcast.15), channel_id=1, replica_groups={{0,8,16,24,32,40,48,56},{64,72,80,88,96,104,112,120},{128,136,144,152,1..., dimensions={0} | all-to-all | bytes 524288 | tf_op jit(solution)/shard_map/all_to_all | solution.py:267
  63.2 0.9 shard_map.131
  64.1 13.3 %all_to_all.16.packed = bf16[32,48,128]{2,1,0:T(8,128)(2,1)S(1)} all-to-all(bf16[32,48,128]{2,1,0:T(8,128)(2,1)S(1)} %get-tuple-element.24), channel_id=1, replica_groups=mesh['col'=32,'dom'=8] {'col'}, dimensions={0} | all-to-all | bytes 786432 | tf_op jit(solution)/shard_map/all_to_all | solution.py:282
  77.4 17.5 %shard_map.132 = (bf16[1056,128]{1,0:T(8,128)(2,1)S(1)}, bf16[1056,128]{1,0:T(8,128)(2,1)S(1)}) custom-call(s32[4]{0:T(128)S(1)} %pad_add_fusion.place, s32[160]{0:T(256)S(1)} %copy-done.3, s32[160]{0:T(256)S(1)} %copy-done.5, s32[160,128,128]{2,1,0:T(8,128)} %mask.3, bf16[32,48,128]{2,1,0:T(8,128)(2,1)S(1)} %all_to_all.16.packed), custom_call_target="tpu_custom_call" | custom-call | flops 671088640 | bytes 10485760 | tf_op jit(solution)/shard_map/pallas_call | solution.py:283
  94.9 6.0 %collective-permute-start.10 = (bf16[1056,128]{1,0:T(8,128)(2,1)S(1)}, bf16[1056,128]{1,0:T(8,128)(2,1)S(1)}, u32[]{:S(2)}, u32[]{:S(2)}) collective-permute-start(bf16[1056,128]{1,0:T(8,128)(2,1)S(1)} %get-tuple-element.26), channel_id=1, source_target_pairs={{0,1},{1,0},{2,3},{3,2},{4,5},{5,4},{6,7},{7,6},{8,9},{9,8},{10,11... | collective-permute-start | bytes 811016 | tf_op jit(solution)/shard_map/ppermute | solution.py:39
  100.9 1.2 collective-permute-done.10.got
  102.1 0.6 shard_map.133
  102.9 3.4 %collective-permute-start.12 = (bf16[288,128]{1,0:T(8,128)(2,1)S(1)}, bf16[288,128]{1,0:T(8,128)(2,1)S(1)}, u32[]{:S(2)}, u32[]{:S(2)}) collective-permute-start(bf16[288,128]{1,0:T(8,128)(2,1)S(1)} %get-tuple-element.29), channel_id=1, source_target_pairs={{0,4},{1,5},{2,6},{3,7},{4,0},{5,1},{6,2},{7,3},{8,12},{9,13},{10,... | collective-permute-start | bytes 221192 | tf_op jit(solution)/shard_map/ppermute | solution.py:39
  106.3 0.3 collective-permute-start.13
  106.7 3.0 %collective-permute-done.12.c = bf16[288,128]{1,0:T(8,128)(2,1)S(1)} collective-permute-done((bf16[288,128]{1,0:T(8,128)(2,1)S(1)}, bf16[288,128]{1,0:T(8,128)(2,1)S(1)}, u32[]{:S(2)}, u32[]{:S(2)}) %collective-permute-start.12) | collective-permute-done | bytes 73760 | tf_op jit(solution)/shard_map/ppermute | solution.py:39
  109.6 1.6 %collective-permute-done.13.d = bf16[288,128]{1,0:T(8,128)(2,1)S(1)} collective-permute-done((bf16[288,128]{1,0:T(8,128)(2,1)S(1)}, bf16[288,128]{1,0:T(8,128)(2,1)S(1)}, u32[]{:S(2)}, u32[]{:S(2)}) %collective-permute-start.13) | collective-permute-done | bytes 73760 | tf_op jit(solution)/shard_map/ppermute | solution.py:39
  111.2 0.8 shard_map.134
  112.0 13.1 %all_to_all.17 = f32[32,8,128]{2,1,0:T(8,128)S(1)} all-to-all(f32[32,8,128]{2,1,0:T(8,128)S(1)} %get-tuple-element.31), channel_id=1, replica_groups=mesh['col'=32,'dom'=8] {'col'}, dimensions={0} | all-to-all | bytes 262144 | tf_op jit(solution)/shard_map/all_to_all | solution.py:301
  125.1 0.7 copy.15
  (28 shorter events, 0.4 us)
Async XLA Ops:
  0.6 76.8 %copy-start.5 = (s32[160]{0:T(256)S(1)}, s32[160]{0:T(256)}, u32[]{:S(2)}) copy-start(s32[160]{0:T(256)} %cols.3) | copy-start | bytes 1924
  0.6 76.8 %copy-start.3 = (s32[160]{0:T(256)S(1)}, s32[160]{0:T(256)}, u32[]{:S(2)}) copy-start(s32[160]{0:T(256)} %rows.3) | copy-start | bytes 1924
  0.7 62.5 %copy-start.1 = (bf16[32,256]{1,0:T(8,128)(2,1)S(1)}, bf16[32,256]{1,0:T(8,128)(2,1)}, u32[]{:S(2)}) copy-start(bf16[32,256]{1,0:T(8,128)(2,1)} %upstream.1) | copy-start | bytes 49156
  0.7 62.5 %copy-start.9 = (s32[32]{0:T(128)S(1)}, s32[32]{0:T(128)}, u32[]{:S(2)}) copy-start(s32[32]{0:T(128)} %param.18) | copy-start | bytes 388
  0.7 62.5 %copy-start.7 = (f32[256]{0:T(256)S(1)}, f32[256]{0:T(256)}, u32[]{:S(2)}) copy-start(f32[256]{0:T(256)} %param.14) | copy-start | bytes 3076
  0.7 62.5 %copy-start = (bf16[128,256]{1,0:T(8,128)(2,1)S(1)}, bf16[128,256]{1,0:T(8,128)(2,1)}, u32[]{:S(2)}) copy-start(bf16[128,256]{1,0:T(8,128)(2,1)} %weight.1) | copy-start | bytes 196612
  0.7 62.5 %copy-start.8 = (f32[128]{0:T(128)S(1)}, f32[128]{0:T(128)}, u32[]{:S(2)}) copy-start(f32[128]{0:T(128)} %param.12) | copy-start | bytes 1540
  1.7 7.7 %collective-permute-start.6 = (bf16[256,128]{1,0:T(8,128)(2,1)S(1)}, bf16[256,128]{1,0:T(8,128)(2,1)S(1)}, u32[]{:S(2)}, u32[]{:S(2)}) collective-permute-start(bf16[256,128]{1,0:T(8,128)(2,1)S(1)} %multiply_convert_fusion.refs_0_), channel_id=1, source_target_pairs={{0,7},{1,6},{2,5},{3,4},{4,3},{5,2},{6,1},{7,0},{8,15},{9,14},{10,... | collective-permute-start | bytes 196616 | tf_op jit(solution)/shard_map/ppermute | solution.py:39
  5.7 6.9 %collective-permute-start.5 = (bf16[256,128]{1,0:T(8,128)(2,1)S(1)}, bf16[256,128]{1,0:T(8,128)(2,1)S(1)}, u32[]{:S(2)}, u32[]{:S(2)}) collective-permute-start(bf16[256,128]{1,0:T(8,128)(2,1)S(1)} %multiply_convert_fusion.refs_0_), channel_id=1, source_target_pairs={{0,6},{1,7},{2,4},{3,5},{4,2},{5,3},{6,0},{7,1},{8,14},{9,15},{10,... | collective-permute-start | bytes 196616 | tf_op jit(solution)/shard_map/ppermute | solution.py:39
  7.6 5.4 %collective-permute-start.4 = (bf16[256,128]{1,0:T(8,128)(2,1)S(1)}, bf16[256,128]{1,0:T(8,128)(2,1)S(1)}, u32[]{:S(2)}, u32[]{:S(2)}) collective-permute-start(bf16[256,128]{1,0:T(8,128)(2,1)S(1)} %multiply_convert_fusion.refs_0_), channel_id=1, source_target_pairs={{0,5},{1,4},{2,7},{3,6},{4,1},{5,0},{6,3},{7,2},{8,13},{9,12},{10,... | collective-permute-start | bytes 196616 | tf_op jit(solution)/shard_map/ppermute | solution.py:39
  7.6 5.4 %collective-permute-start.3 = (bf16[256,128]{1,0:T(8,128)(2,1)S(1)}, bf16[256,128]{1,0:T(8,128)(2,1)S(1)}, u32[]{:S(2)}, u32[]{:S(2)}) collective-permute-start(bf16[256,128]{1,0:T(8,128)(2,1)S(1)} %multiply_convert_fusion.refs_0_), channel_id=1, source_target_pairs={{0,4},{1,5},{2,6},{3,7},{4,0},{5,1},{6,2},{7,3},{8,12},{9,13},{10,... | collective-permute-start | bytes 196616 | tf_op jit(solution)/shard_map/ppermute | solution.py:39
  9.0 4.7 %collective-permute-start.2 = (bf16[256,128]{1,0:T(8,128)(2,1)S(1)}, bf16[256,128]{1,0:T(8,128)(2,1)S(1)}, u32[]{:S(2)}, u32[]{:S(2)}) collective-permute-start(bf16[256,128]{1,0:T(8,128)(2,1)S(1)} %multiply_convert_fusion.refs_0_), channel_id=1, source_target_pairs={{0,3},{1,2},{2,1},{3,0},{4,7},{5,6},{6,5},{7,4},{8,11},{9,10},{10,... | collective-permute-start | bytes 196616 | tf_op jit(solution)/shard_map/ppermute | solution.py:39
  9.4 6.4 %collective-permute-start.1 = (bf16[256,128]{1,0:T(8,128)(2,1)S(1)}, bf16[256,128]{1,0:T(8,128)(2,1)S(1)}, u32[]{:S(2)}, u32[]{:S(2)}) collective-permute-start(bf16[256,128]{1,0:T(8,128)(2,1)S(1)} %multiply_convert_fusion.refs_0_), channel_id=1, source_target_pairs={{0,2},{1,3},{2,0},{3,1},{4,6},{5,7},{6,4},{7,5},{8,10},{9,11},{10,... | collective-permute-start | bytes 196616 | tf_op jit(solution)/shard_map/ppermute | solution.py:39
  12.6 3.2 %collective-permute-start = (bf16[256,128]{1,0:T(8,128)(2,1)S(1)}, bf16[256,128]{1,0:T(8,128)(2,1)S(1)}, u32[]{:S(2)}, u32[]{:S(2)}) collective-permute-start(bf16[256,128]{1,0:T(8,128)(2,1)S(1)} %multiply_convert_fusion.refs_0_), channel_id=1, source_target_pairs={{0,1},{1,0},{2,3},{3,2},{4,5},{5,4},{6,7},{7,6},{8,9},{9,8},{10,11... | collective-permute-start | bytes 196616 | tf_op jit(solution)/shard_map/ppermute | solution.py:39
  12.6 98.6 %copy-start.6 = (f32[256]{0:T(256)S(1)}, f32[256]{0:T(256)}, u32[]{:S(2)}) copy-start(f32[256]{0:T(256)} %param.11) | copy-start | bytes 3076
  15.8 0.7 copy-start.2
  16.5 0.7 copy-start.4
  28.8 7.6 %collective-permute-start.7 = (bf16[1024,128]{1,0:T(8,128)(2,1)S(1)}, bf16[1024,128]{1,0:T(8,128)(2,1)S(1)}, u32[]{:S(2)}, u32[]{:S(2)}) collective-permute-start(bf16[1024,128]{1,0:T(8,128)(2,1)S(1)} %get-tuple-element.20), channel_id=1, source_target_pairs={{0,64},{8,72},{16,80},{24,88},{32,96},{40,104},{48,112},{56,120},{... | collective-permute-start | bytes 786440 | tf_op jit(solution)/shard_map/ppermute | solution.py:44
  29.6 13.7 %collective-permute-start.8 = (bf16[1024,128]{1,0:T(8,128)(2,1)S(1)}, bf16[1024,128]{1,0:T(8,128)(2,1)S(1)}, u32[]{:S(2)}, u32[]{:S(2)}) collective-permute-start(bf16[1024,128]{1,0:T(8,128)(2,1)S(1)} %get-tuple-element.21), channel_id=1, source_target_pairs={{0,128},{8,136},{16,144},{24,152},{32,160},{40,168},{48,176},{56,1... | collective-permute-start | bytes 786440 | tf_op jit(solution)/shard_map/ppermute | solution.py:44
  32.3 13.4 %collective-permute-start.9 = (bf16[1024,128]{1,0:T(8,128)(2,1)S(1)}, bf16[1024,128]{1,0:T(8,128)(2,1)S(1)}, u32[]{:S(2)}, u32[]{:S(2)}) collective-permute-start(bf16[1024,128]{1,0:T(8,128)(2,1)S(1)} %get-tuple-element.22), channel_id=1, source_target_pairs={{0,192},{8,200},{16,208},{24,216},{32,224},{40,232},{48,240},{56,2... | collective-permute-start | bytes 786440 | tf_op jit(solution)/shard_map/ppermute | solution.py:44
  94.9 7.2 %collective-permute-start.10 = (bf16[1056,128]{1,0:T(8,128)(2,1)S(1)}, bf16[1056,128]{1,0:T(8,128)(2,1)S(1)}, u32[]{:S(2)}, u32[]{:S(2)}) collective-permute-start(bf16[1056,128]{1,0:T(8,128)(2,1)S(1)} %get-tuple-element.26), channel_id=1, source_target_pairs={{0,1},{1,0},{2,3},{3,2},{4,5},{5,4},{6,7},{7,6},{8,9},{9,8},{10,11... | collective-permute-start | bytes 811016 | tf_op jit(solution)/shard_map/ppermute | solution.py:39
  102.7 3.9 %collective-permute-start.11 = (bf16[288,128]{1,0:T(8,128)(2,1)S(1)}, bf16[288,128]{1,0:T(8,128)(2,1)S(1)}, u32[]{:S(2)}, u32[]{:S(2)}) collective-permute-start(bf16[288,128]{1,0:T(8,128)(2,1)S(1)} %get-tuple-element.28), channel_id=1, source_target_pairs={{0,2},{1,3},{2,0},{3,1},{4,6},{5,7},{6,4},{7,5},{8,10},{9,11},{10,... | collective-permute-start | bytes 221192 | tf_op jit(solution)/shard_map/ppermute | solution.py:39
  102.9 6.7 %collective-permute-start.12 = (bf16[288,128]{1,0:T(8,128)(2,1)S(1)}, bf16[288,128]{1,0:T(8,128)(2,1)S(1)}, u32[]{:S(2)}, u32[]{:S(2)}) collective-permute-start(bf16[288,128]{1,0:T(8,128)(2,1)S(1)} %get-tuple-element.29), channel_id=1, source_target_pairs={{0,4},{1,5},{2,6},{3,7},{4,0},{5,1},{6,2},{7,3},{8,12},{9,13},{10,... | collective-permute-start | bytes 221192 | tf_op jit(solution)/shard_map/ppermute | solution.py:39
  106.3 4.9 %collective-permute-start.13 = (bf16[288,128]{1,0:T(8,128)(2,1)S(1)}, bf16[288,128]{1,0:T(8,128)(2,1)S(1)}, u32[]{:S(2)}, u32[]{:S(2)}) collective-permute-start(bf16[288,128]{1,0:T(8,128)(2,1)S(1)} %get-tuple-element.30), channel_id=1, source_target_pairs={{0,6},{1,7},{2,4},{3,5},{4,2},{5,3},{6,0},{7,1},{8,14},{9,15},{10,... | collective-permute-start | bytes 221192 | tf_op jit(solution)/shard_map/ppermute | solution.py:39

commit v2 on v1

v2 whole, which is shorter than its diff:
```python
import jax
import jax.numpy as jnp
from jax import lax
from jax.experimental import pallas as pl
from jax.experimental.pallas import tpu as pltpu
from jax.sharding import PartitionSpec as P

NY, NZ, NX, NCORE = 4, 8, 4, 2
COL, DOM = NY * NZ, NX * NCORE
BLK = 128
F = 128
HID = 256
TGT = 32
VMEM = pl.BlockSpec(memory_space=pltpu.VMEM)
HBM = pl.BlockSpec(memory_space=pltpu.HBM)
SMEM = pl.BlockSpec(memory_space=pltpu.SMEM)
F32, BF16 = jnp.float32, jnp.bfloat16
PAIRS = 96
HALF_AT = 120
EMPTY = 160
STEP = 8
GRADS = HID + 16
PACK = TGT + 16
Y_GROUPS = [[y * NZ + z for y in range(NY)] for z in range(NZ)]
Z_GROUPS = [[y * NZ + z for z in range(NZ)] for y in range(NY)]
X_GROUPS = [[x * NCORE + core for x in range(NX)] for core in range(NCORE)]


def call(kernel, outs, ins, scratch=(), flops=0, moved=0, limit=16):
    return pl.pallas_call(
        kernel,
        out_shape=outs,
        in_specs=ins,
        out_specs=[VMEM] * len(outs),
        scratch_shapes=list(scratch),
        compiler_params=pltpu.CompilerParams(vmem_limit_bytes=limit * 1024 * 1024),
        cost_estimate=pl.CostEstimate(flops=flops, bytes_accessed=moved, transcendentals=0),
    )


def sds(shape, dtype):
    return jax.ShapeDtypeStruct(shape, dtype)


def exchange_dom(value, distance):
    pairs = [(i, i ^ distance) for i in range(DOM)]
    return lax.ppermute(value, "dom", pairs)


def swap(value, axis, groups=None):
    return lax.all_to_all(value, axis, 0, 0, axis_index_groups=groups, tiled=True)


def pair_of(pairs, edges, n):
    word = pairs[n]
    both = jnp.concatenate([edges[word & 255], edges[(word >> 8) & 255]], axis=1)
    return both, (word >> 16) & 15, (word >> 20) & 15, word >> 24


def forward_kernel(ids, mask, *refs):
    pieces, (out, kept, pairs) = refs[:DOM], refs[DOM : DOM + 3]
    sources, totals, staged, edges, waiting, mask_sems, kept_sems = refs[DOM + 3 :]
    steps = mask.shape[0] // STEP

    def mask_copy(i):
        at = pl.ds(i * STEP, STEP)
        return pltpu.make_async_copy(mask.at[at], staged.at[at], mask_sems.at[i])

    def kept_copy(i):
        at = pl.ds(i * STEP, STEP)
        return pltpu.make_async_copy(edges.at[at], kept.at[at], kept_sems.at[i])

    for i in range(steps):
        mask_copy(i).start()
    my_dom = lax.axis_index("dom")
    for k in range(DOM):
        at = my_dom ^ k
        sources[2 * at] = pieces[k][0:BLK, :]
        sources[2 * at + 1] = pieces[k][BLK:, :]
    totals[...] = jnp.zeros_like(totals)
    edges[EMPTY:, :, :] = jnp.zeros((STEP, BLK, BLK), BF16)
    kept_copy(steps).start()
    for r in range(COL):
        waiting[r] = -1

    def step(i, n):
        mask_copy(i).wait()
        products = []
        for u in range(STEP):
            t = i * STEP + u
            r, c = ids[t] >> 4, ids[t] & 15
            tile = staged[t].astype(F32).astype(BF16)
            edges[t] = tile
            products.append((r, jnp.dot(tile, sources[c], preferred_element_type=F32)))
            first = waiting[r]
            paired = first >= 0
            pairs[n] = (first & 255) | (t << 8) | ((first >> 8) << 16) | (c << 20) | (r << 24)
            waiting[r] = jnp.where(paired, -1, t | (c << 8))
            n = n + jnp.where(paired, 1, 0)
        for r, product in products:
            totals[r] = totals[r] + product
        kept_copy(i).start()
        return n

    n = lax.fori_loop(0, steps // 2, step, 0)
    pairs[HALF_AT] = n
    n = lax.fori_loop(steps // 2, steps, step, n)
    for r in range(COL):
        first = waiting[r]
        pairs[n] = (first & 255) | (EMPTY << 8) | ((first >> 8) << 16) | (r << 24)
        n = n + jnp.where(first >= 0, 1, 0)

    def fill(at, carry):
        pairs[at] = EMPTY | (EMPTY << 8)
        return carry

    lax.fori_loop(n, PAIRS, fill, 0)
    for r in range(COL):
        out[r] = totals[r].astype(BF16)
    for i in range(steps + 1):
        kept_copy(i).wait()


def forward(ids, tile_mask, pieces):
    tiles = tile_mask.shape[0]
    steps = tiles // STEP
    return pl.pallas_call(
        forward_kernel,
        out_shape=[
            sds((COL, BLK, F), BF16),
            sds((tiles + STEP, BLK, BLK), BF16),
            sds((BLK,), jnp.int32),
        ],
        in_specs=[SMEM, HBM] + [VMEM] * DOM,
        out_specs=[VMEM, HBM, SMEM],
        scratch_shapes=[
            pltpu.VMEM((DOM * 2, BLK, F), BF16),
            pltpu.VMEM((COL, BLK, F), F32),
            pltpu.VMEM(tile_mask.shape, jnp.int32),
            pltpu.VMEM((tiles + STEP, BLK, BLK), BF16),
            pltpu.SMEM((COL,), jnp.int32),
            pltpu.SemaphoreType.DMA((steps,)),
            pltpu.SemaphoreType.DMA((steps + 1,)),
        ],
        compiler_params=pltpu.CompilerParams(vmem_limit_bytes=52 * 1024 * 1024),
        cost_estimate=pl.CostEstimate(
            flops=2 * tiles * BLK**3, bytes_accessed=tiles * BLK * BLK * 6, transcendentals=0
        ),
    )(ids, tile_mask, *pieces)


def column(row):
    return jnp.transpose(jnp.broadcast_to(row, (BLK, BLK)))


def sigmoid(v):
    return 1.0 / (1.0 + jnp.exp(-v))


def y_sum_kernel(parts, out):
    for z in range(NZ):
        total = (parts[0, z].astype(F32) + parts[1, z].astype(F32)) + (
            parts[2, z].astype(F32) + parts[3, z].astype(F32)
        )
        out[z] = total.astype(BF16)


def dense_kernel(parts, dest_scale, weight, bias, targets, upstream, hidden, packed):
    summed = parts[0].astype(F32)
    for z in range(1, NZ):
        summed = summed + parts[z].astype(F32)
    scale = column(dest_scale[...])
    aggregated = (summed * scale).astype(BF16)
    w = weight[...]
    preact = jnp.dot(aggregated, w, preferred_element_type=F32) + bias[...]
    hidden[...] = (preact * sigmoid(preact)).astype(BF16)
    wanted = targets[...]
    row_ids = lax.broadcasted_iota(jnp.int32, (BLK, TGT), 0)
    chosen = (row_ids == wanted).astype(F32)
    chosen_b = chosen.astype(BF16)
    agg_t = lax.dot_general(
        chosen_b, aggregated, (((0,), (0,)), ((), ())), preferred_element_type=F32
    ).astype(BF16)
    pre_t = jnp.dot(agg_t, w, preferred_element_type=F32) + bias[...]
    s = sigmoid(pre_t)
    slope = (upstream[...].astype(F32) * (s * (1.0 + pre_t * (1.0 - s)))).astype(BF16)
    weight_part = lax.dot_general(
        agg_t, slope, (((0,), (0,)), ((), ())), preferred_element_type=F32
    )
    bias_part = jnp.sum(slope.astype(F32), axis=0, keepdims=True)
    term = lax.dot_general(
        slope, w, (((1,), (1,)), ((), ())), preferred_element_type=F32
    )
    same = lax.dot_general(
        chosen_b, chosen_b, (((0,), (0,)), ((), ())), preferred_element_type=F32
    )
    collected = jnp.dot(
        same, term, preferred_element_type=F32, precision=lax.Precision.HIGHEST
    )
    scale_t = lax.dot_general(
        chosen, scale, (((0,), (0,)), ((), ())), preferred_element_type=F32,
        precision=lax.Precision.HIGHEST,
    )
    k_row = lax.broadcasted_iota(jnp.int32, (TGT, TGT), 0)
    k_col = lax.broadcasted_iota(jnp.int32, (TGT, TGT), 1)
    earlier = jnp.sum(jnp.where(k_col < k_row, same, 0.0), axis=1, keepdims=True)
    returned = jnp.where(earlier > 0.0, 0.0, collected * scale_t).astype(BF16)
    names = jnp.concatenate([wanted.astype(F32)] * (BLK // TGT), axis=1)
    lanes = lax.broadcasted_iota(jnp.int32, (1, BLK), 1)
    names = jnp.where(lanes // TGT == (lax.axis_index("col") & 3), names, -1.0)
    high = bias_part.astype(BF16).astype(F32)
    low = bias_part - high
    sundry = jnp.concatenate(
        [names, high[:, :BLK], high[:, BLK:], low[:, :BLK], low[:, BLK:], jnp.zeros((3, BLK), F32)],
        axis=0,
    )
    for c in range(COL):
        at, side = 8 * (c // 2), BLK * (c % 2)
        chunk = weight_part[at : at + 8, side : side + BLK]
        packed[c, 0:TGT, :] = returned
        packed[c, TGT:, :] = jnp.concatenate([chunk, sundry], axis=0).astype(BF16)


def gradient_kernel(packed, chunks, bias):
    total = packed[0, TGT:, :].astype(F32)
    for c in range(1, COL):
        total = total + packed[c, TGT:, :].astype(F32)
    for c in range(COL):
        chunks[c] = total[0:8, :]
    bias[...] = jnp.concatenate([total[9:10] + total[11:12], total[10:11] + total[12:13]], axis=1)


def unpack(packed, returned):
    row_ids = lax.broadcasted_iota(jnp.int32, (BLK, BLK), 0).astype(F32)
    quarters = BLK // TGT
    for g in range(COL // quarters):
        held = slice(g * quarters, (g + 1) * quarters)
        rows = jnp.transpose(packed[held, 0:TGT, :].reshape(BLK, F))
        for first in range(g * quarters, (g + 1) * quarters, 2):
            chosen = [
                (row_ids == packed[c, TGT:, :].astype(F32)[8:9, :]).astype(BF16)
                for c in (first, first + 1)
            ]
            placed = lax.dot_general(
                rows,
                jnp.concatenate(chosen, axis=0),
                (((1,), (1,)), ((), ())),
                preferred_element_type=F32,
            ).astype(BF16)
            returned[first] = placed[:, :BLK]
            returned[first + 1] = placed[:, BLK:]


def bias_rows(bias):
    high = bias.astype(BF16).astype(F32)
    low = bias - high
    return jnp.concatenate(
        [high[:, :BLK], high[:, BLK:], low[:, :BLK], low[:, BLK:], jnp.zeros((12, BLK), F32)],
        axis=0,
    ).astype(BF16)


def bias_of(rows):
    rows = rows.astype(F32)
    return jnp.concatenate([rows[0:1] + rows[2:3], rows[1:2] + rows[3:4]], axis=1)


def backward_kernel(pairs, kept, packed, bias, own, other, edges, returned, totals, sems):
    my_core = lax.axis_index("dom") & 1
    copies = []
    for i in range(kept.shape[0] // STEP):
        at = pl.ds(i * STEP, STEP)
        copies.append(pltpu.make_async_copy(kept.at[at], edges.at[at], sems.at[i]))
        copies[-1].start()
    for ref in (own, other):
        ref[NX * 256 :, :] = bias_rows(bias[...])
    unpack(packed, returned)
    totals[...] = jnp.zeros_like(totals)
    half = len(copies) // 2
    for copy in copies[:half]:
        copy.wait()
    unroll = 4

    def pair_step(i, carry):
        products = []
        for u in range(unroll):
            both, c1, c2, r = pair_of(pairs, edges, i * unroll + u)
            products.append((c1, c2, jnp.dot(returned[r], both, preferred_element_type=F32)))
        for c1, c2, product in products:
            totals[c1] = totals[c1] + product[:, :BLK]
            totals[c2] = totals[c2] + product[:, BLK:]
        return carry

    early = pairs[HALF_AT] // unroll
    lax.fori_loop(0, early, pair_step, 0)
    for copy in copies[half:]:
        copy.wait()
    lax.fori_loop(early, PAIRS // unroll, pair_step, 0)
    for x in range(NX):
        for half in range(2):
            rows_at = pl.ds(x * 256 + half * BLK, BLK)
            for ref, core in ((own, my_core), (other, 1 - my_core)):
                block = (x * NCORE + core) * 2 + half
                ref[rows_at, :] = jnp.transpose(totals[block]).astype(BF16)


def core_sum_kernel(own, got, grads, grads_got, out):
    at = NX * 256
    bias = bias_rows(bias_of(own[at:, :]) + bias_of(got[at:, :]))
    weight_sum = [(grads[c] + grads_got[c]).astype(BF16) for c in range(COL)]
    for x in range(NX):
        rows_at = slice(x * 256, (x + 1) * 256)
        total = own[rows_at, :].astype(F32) + got[rows_at, :].astype(F32)
        out[x, 0:256, :] = total.astype(BF16)
        for c in range(0, COL, 2):
            out[x, 256 + 8 * c : 272 + 8 * c, :] = jnp.concatenate(weight_sum[c : c + 2], axis=0)
        out[x, 256 + HID :, :] = bias


def finish_kernel(parts, source_scale, grad, weight_grad, bias_grad):
    def total(at):
        return (parts[0, at, :].astype(F32) + parts[1, at, :].astype(F32)) + (
            parts[2, at, :].astype(F32) + parts[3, at, :].astype(F32)
        )

    for half in range(2):
        at = slice(half * BLK, (half + 1) * BLK)
        grad[at, :] = total(at) * column(source_scale[:, at])
    for c in range(0, COL, 2):
        both = total(slice(256 + 8 * c, 272 + 8 * c))
        rows_at = slice(4 * c, 4 * c + 8)
        weight_grad[rows_at, :BLK] = both[0:8]
        weight_grad[rows_at, BLK:] = both[8:16]
    bias = [bias_of(parts[x, 256 + HID :, :]) for x in range(NX)]
    bias_grad[...] = (bias[0] + bias[1]) + (bias[2] + bias[3])


def body(
    source_feats,
    source_scale,
    dest_scale,
    weight,
    layer_bias,
    tile_rows,
    tile_cols,
    tile_mask,
    targets,
    upstream,
):
    scaled = (source_feats.astype(F32) * source_scale[:, None]).astype(BF16)
    pieces = [scaled] + [exchange_dom(scaled, k) for k in range(1, DOM)]
    products = 2 * tile_mask.shape[0] * BLK**3
    partials, kept, pairs = forward(tile_rows * 16 + tile_cols, tile_mask, pieces)
    parts = swap(partials.reshape(NY, NZ, BLK, F), "col", Y_GROUPS)
    (line,) = call(y_sum_kernel, [sds((NZ, BLK, F), BF16)], [VMEM])(parts)
    parts = swap(line, "col", Z_GROUPS)
    hidden, packed = call(
        dense_kernel,
        [sds((BLK, HID), BF16), sds((COL, PACK, F), BF16)],
        [VMEM] * 6,
    )(
        parts,
        dest_scale.reshape(1, BLK),
        weight,
        layer_bias.reshape(1, HID),
        targets.reshape(1, TGT),
        upstream,
    )
    gathered = swap(packed, "col")
    chunks, bias_sum = call(
        gradient_kernel, [sds((COL, 8, BLK), F32), sds((1, HID), F32)], [VMEM]
    )(gathered)
    grads = swap(chunks, "col")
    own, other = call(
        backward_kernel,
        [sds((NX * 256 + 16, F), BF16)] * 2,
        [SMEM, HBM, VMEM, VMEM],
        [
            pltpu.VMEM(kept.shape, BF16),
            pltpu.VMEM((COL, F, BLK), BF16),
            pltpu.VMEM((DOM * 2, F, BLK), F32),
            pltpu.SemaphoreType.DMA((kept.shape[0] // STEP,)),
        ],
        flops=products,
        limit=52,
    )(pairs, kept, gathered, bias_sum)
    got = exchange_dom(other, 1)
    grads_got = exchange_dom(grads, 1)
    (by_x,) = call(core_sum_kernel, [sds((NX, 256 + GRADS, F), BF16)], [VMEM] * 4)(
        own, got, grads, grads_got
    )
    input_grad, weight_grad, bias_grad = call(
        finish_kernel,
        [sds((256, F), F32), sds((F, HID), F32), sds((1, HID), F32)],
        [VMEM] * 2,
    )(swap(by_x, "dom", X_GROUPS), source_scale.reshape(1, 256))
    return hidden, weight_grad, bias_grad.reshape(HID), input_grad


def solution(mesh):
    placed = (
        P(("col", "dom"), None),
        P(("col", "dom")),
        P(("col", "dom")),
        P(),
        P(),
        P(("col", "dom")),
        P(("col", "dom")),
        P(("col", "dom"), None, None),
        P(("col", "dom")),
        P(("col", "dom"), None),
    )
    return jax.shard_map(
        body,
        mesh=mesh,
        in_specs=placed,
        out_specs=(P(("col", "dom"), None), P(), P(), P(("col", "dom"), None)),
        check_vma=False,
    )
```

time: 127 us -> 109 us (0.86)
  waiting for transfers between devices: 21.7 us -> 3.47 us
  blocking collectives: 43.9 us -> 60.7 us
  Pallas kernels: 31.6 us -> 19.1 us
  local copies, waits for them, and re-layouts: 2.05 us -> 0.02 us
  starting transfers between devices: 24.8 us -> 23 us
    all_to_all x3 -> x4, blocking collectives: 43.9 us -> 60.7 us  [swap(): lax.all_to_all(value, axis, 0, 0, axis_index_groups=groups, tiled=True)]
    ppermute x3 -> x0, waiting for transfers between devices: 12.9 us -> none  [exchange_y(): return lax.ppermute(value, 'col', pairs)]
    pallas_call x6 -> x7, Pallas kernels: 31.6 us -> 19.1 us  [the longest x1 8.59 us: body(): call(backward_kernel, [sds((NX * 256 + 16, F), BF16)] * 2, [SMEM, HBM, VM...]
    ppermute x11 -> x9, waiting for transfers between devices: 8.85 us -> 3.47 us  [exchange_dom(): return lax.ppermute(value, 'dom', pairs)]
    all_to_all x0 -> x1, starting transfers between devices: none -> 5.34 us  [swap(): lax.all_to_all(value, axis, 0, 0, axis_index_groups=groups, tiled=True)]
    ppermute x3 -> x0, starting transfers between devices: 3.95 us -> none  [exchange_y(): return lax.ppermute(value, 'col', pairs)]
    ppermute x11 -> x9, starting transfers between devices: 20.8 us -> 17.7 us  [exchange_dom(): return lax.ppermute(value, 'dom', pairs)]
    unnamed x21 -> x12, local copies, waits for them, and re-layouts: 2.05 us -> 0.02 us
  transfers between devices with their start and end apart: 14 -> 10, of which waited for: 9 -> 3; matrix products, arithmetic and copies ran while one was open for 0% -> 1% of each run, Pallas kernels for 0% -> 8%
where the time goes in v2:
time: 109 us
  blocking collectives  60.7 us (56%)
  starting transfers between devices  23 us (21%)
  Pallas kernels  19.1 us (18%)
  waiting for transfers between devices  3.47 us (3%)
  other arithmetic  1.68 us (2%)
    all_to_all x4, blocking collectives, swap(): lax.all_to_all(value, axis, 0, 0, axis_index_groups=groups, tiled=True)  60.7 us
    ppermute x9, starting transfers between devices, exchange_dom(): return lax.ppermute(value, 'dom', pairs)  17.7 us
    pallas_call x1, Pallas kernels, body(): call(backward_kernel, [sds((NX * 256 + 16, F), BF16)] * 2, [SMEM, HBM, VM...  8.59 us
    pallas_call x1, Pallas kernels, forward(): pl.pallas_call(forward_kernel, out_shape=[sds((COL, BLK, F), BF16), sds((...  7.87 us
    all_to_all x1, starting transfers between devices, swap(): lax.all_to_all(value, axis, 0, 0, axis_index_groups=groups, tiled=True)  5.34 us
    ppermute x9, waiting for transfers between devices, exchange_dom(): return lax.ppermute(value, 'dom', pairs)  3.47 us
  transfers between devices with their start and end apart: 10, of which 3 were waited for; matrix products, arithmetic and copies ran while one was open for 1% of the time, Pallas kernels for 8%

profile of v2, /device:TPU:1, one launch (start us, length us, event | category | flops | bytes accessed | tf_op | source)
XLA Modules:
  0.0 108.7 jit_solution(10646512476573491074)
XLA Ops:
  0.7 1.0 multiply_convert_fusion.refs_0_
  1.7 4.0 %collective-permute-start.6 = (bf16[256,128]{1,0:T(8,128)(2,1)S(1)}, bf16[256,128]{1,0:T(8,128)(2,1)S(1)}, u32[]{:S(2)}, u32[]{:S(2)}) collective-permute-start(bf16[256,128]{1,0:T(8,128)(2,1)S(1)} %multiply_convert_fusion.refs_0_), channel_id=1, source_target_pairs={{0,7},{1,6},{2,5},{3,4},{4,3},{5,2},{6,1},{7,0},{8,15},{9,14},{10,... | collective-permute-start | bytes 196616 | tf_op jit(solution)/shard_map/ppermute | solution.py:47
  5.6 1.9 %collective-permute-start.5 = (bf16[256,128]{1,0:T(8,128)(2,1)S(1)}, bf16[256,128]{1,0:T(8,128)(2,1)S(1)}, u32[]{:S(2)}, u32[]{:S(2)}) collective-permute-start(bf16[256,128]{1,0:T(8,128)(2,1)S(1)} %multiply_convert_fusion.refs_0_), channel_id=1, source_target_pairs={{0,6},{1,7},{2,4},{3,5},{4,2},{5,3},{6,0},{7,1},{8,14},{9,15},{10,... | collective-permute-start | bytes 196616 | tf_op jit(solution)/shard_map/ppermute | solution.py:47
  7.6 0.0 collective-permute-start.4
  7.6 1.4 %collective-permute-start.3 = (bf16[256,128]{1,0:T(8,128)(2,1)S(1)}, bf16[256,128]{1,0:T(8,128)(2,1)S(1)}, u32[]{:S(2)}, u32[]{:S(2)}) collective-permute-start(bf16[256,128]{1,0:T(8,128)(2,1)S(1)} %multiply_convert_fusion.refs_0_), channel_id=1, source_target_pairs={{0,4},{1,5},{2,6},{3,7},{4,0},{5,1},{6,2},{7,3},{8,12},{9,13},{10,... | collective-permute-start | bytes 196616 | tf_op jit(solution)/shard_map/ppermute | solution.py:47
  9.0 0.4 collective-permute-start.2
  9.4 0.0 collective-permute-done.6.refs_7_
  9.4 3.2 %collective-permute-start.1 = (bf16[256,128]{1,0:T(8,128)(2,1)S(1)}, bf16[256,128]{1,0:T(8,128)(2,1)S(1)}, u32[]{:S(2)}, u32[]{:S(2)}) collective-permute-start(bf16[256,128]{1,0:T(8,128)(2,1)S(1)} %multiply_convert_fusion.refs_0_), channel_id=1, source_target_pairs={{0,2},{1,3},{2,0},{3,1},{4,6},{5,7},{6,4},{7,5},{8,10},{9,11},{10,... | collective-permute-start | bytes 196616 | tf_op jit(solution)/shard_map/ppermute | solution.py:47
  12.6 0.0 collective-permute-done.5.refs_6_
  12.6 0.0 collective-permute-start
  12.6 0.7 multiply_add_fusion.ids
  13.3 0.0 collective-permute-done.4.refs_5_
  13.3 0.0 collective-permute-done.3.refs_4_
  13.3 0.4 collective-permute-done.2.refs_3_
  13.6 2.1 %collective-permute-done.1.refs_2_ = bf16[256,128]{1,0:T(8,128)(2,1)S(1)} collective-permute-done((bf16[256,128]{1,0:T(8,128)(2,1)S(1)}, bf16[256,128]{1,0:T(8,128)(2,1)S(1)}, u32[]{:S(2)}, u32[]{:S(2)}) %collective-permute-start.1) | collective-permute-done | bytes 65568 | tf_op jit(solution)/shard_map/ppermute | solution.py:47
  15.8 0.0 collective-permute-done.refs_1_
  15.8 7.9 %shard_map.129 = (bf16[32,128,128]{2,1,0:T(8,128)(2,1)S(1)}, bf16[168,128,128]{2,1,0:T(8,128)(2,1)}, s32[128]{0:T(128)S(1)}) custom-call(s32[160]{0:T(256)S(1)} %multiply_add_fusion.ids, s32[160,128,128]{2,1,0:T(8,128)} %mask.1, bf16[256,128]{1,0:T(8,128)(2,1)S(1)} %multiply_convert_fusion.refs_0_, bf16[256,128]{1,0:T(8,128)(2,1)S(1)} %collective-permute-done.refs_1_, ...), custom_call_target="tpu_custom_call" | custom-call | flops 671088640 | bytes 15728640 | tf_op jit(solution)/shard_map/pallas_call | solution.py:127
  23.6 17.0 %all_to_all.25.parts = bf16[4,8,128,128]{3,2,1,0:T(8,128)(2,1)S(1)} all-to-all(bf16[4,8,128,128]{3,2,1,0:T(8,128)(2,1)S(1)} %bitcast.6), channel_id=1, replica_groups={{0,64,128,192},{8,72,136,200},{16,80,144,208},{24,88,152,216},{32,96,16..., dimensions={0} | all-to-all | bytes 2097152 | tf_op jit(solution)/shard_map/all_to_all | solution.py:51
  40.7 0.1 shard_map.130
  40.8 17.4 %all_to_all.26.parts = bf16[8,128,128]{2,1,0:T(8,128)(2,1)S(1)} all-to-all(bf16[8,128,128]{2,1,0:T(8,128)(2,1)S(1)} %shard_map.130), channel_id=1, replica_groups={{0,8,16,24,32,40,48,56},{64,72,80,88,96,104,112,120},{128,136,144,152,1..., dimensions={0} | all-to-all | bytes 524288 | tf_op jit(solution)/shard_map/all_to_all | solution.py:51
  58.2 1.0 shard_map.131
  59.2 13.4 %all_to_all.27.packed = bf16[32,48,128]{2,1,0:T(8,128)(2,1)S(1)} all-to-all(bf16[32,48,128]{2,1,0:T(8,128)(2,1)S(1)} %get-tuple-element.20), channel_id=1, replica_groups=mesh['col'=32,'dom'=8] {'col'}, dimensions={0} | all-to-all | bytes 786432 | tf_op jit(solution)/shard_map/all_to_all | solution.py:51
  72.6 0.7 shard_map.132
  73.3 5.3 %all-to-all-start.3 = ((f32[32,8,128]{2,1,0:T(8,128)}), f32[32,8,128]{2,1,0:T(8,128)S(1)}, u32[]{:S(2)}, u32[]{:S(2)}) async-start(f32[32,8,128]{2,1,0:T(8,128)} %get-tuple-element.24), calls=%async_computation.3 | async-start | bytes 262144 | tf_op jit(solution)/shard_map/all_to_all | solution.py:51
  78.6 8.6 %shard_map.133 = (bf16[1040,128]{1,0:T(8,128)(2,1)S(1)}, bf16[1040,128]{1,0:T(8,128)(2,1)S(1)}) custom-call(s32[128]{0:T(128)S(1)} %get-tuple-element.18.pairs, bf16[168,128,128]{2,1,0:T(8,128)(2,1)} %get-tuple-element.19.kept, bf16[32,48,128]{2,1,0:T(8,128)(2,1)S(1)} %all_to_all.27.packed, f32[1,256]{1,0:T(1,128)S(1)} %get-tuple-element.21.bias), custom_call_target="tpu_custom_call" | custom-call | flops 671088640 | tf_op jit(solution)/shard_map/pallas_call | solution.py:374
  87.2 5.2 %collective-permute-start.7 = (bf16[1040,128]{1,0:T(8,128)(2,1)S(1)}, bf16[1040,128]{1,0:T(8,128)(2,1)S(1)}, u32[]{:S(2)}, u32[]{:S(2)}) collective-permute-start(bf16[1040,128]{1,0:T(8,128)(2,1)S(1)} %get-tuple-element.23), channel_id=1, source_target_pairs={{0,1},{1,0},{2,3},{3,2},{4,5},{5,4},{6,7},{7,6},{8,9},{9,8},{10,11... | collective-permute-start | bytes 798728 | tf_op jit(solution)/shard_map/ppermute | solution.py:47
  92.4 0.0 all-to-all-done.3.grads
  92.4 1.6 %collective-permute-start.8 = (f32[32,8,128]{2,1,0:T(8,128)S(1)}, f32[32,8,128]{2,1,0:T(8,128)S(1)}, u32[]{:S(2)}, u32[]{:S(2)}) collective-permute-start(f32[32,8,128]{2,1,0:T(8,128)S(1)} %all-to-all-done.3.grads), channel_id=1, source_target_pairs={{0,1},{1,0},{2,3},{3,2},{4,5},{5,4},{6,7},{7,6},{8,9},{9,8},{10,11... | collective-permute-start | bytes 393224 | tf_op jit(solution)/shard_map/ppermute | solution.py:47
  94.0 1.0 collective-permute-done.8.grads_got
  95.0 0.1 shard_map.134
  95.1 12.9 %all_to_all.28.parts = bf16[4,528,128]{2,1,0:T(8,128)(2,1)S(1)} all-to-all(bf16[4,528,128]{2,1,0:T(8,128)(2,1)S(1)} %shard_map.134), channel_id=1, replica_groups={{0,2,4,6},{1,3,5,7},{8,10,12,14},{9,11,13,15},{16,18,20,22},{17,19,21,2..., dimensions={0} | all-to-all | bytes 1081344 | tf_op jit(solution)/shard_map/all_to_all | solution.py:51
  108.0 0.8 shard_map.135
  (13 shorter events, 0.0 us)
Async XLA Ops:
  0.6 57.5 %copy-start.1 = (bf16[32,256]{1,0:T(8,128)(2,1)S(1)}, bf16[32,256]{1,0:T(8,128)(2,1)}, u32[]{:S(2)}) copy-start(bf16[32,256]{1,0:T(8,128)(2,1)} %upstream.1) | copy-start | bytes 49156
  0.6 57.5 %copy-start.5 = (s32[32]{0:T(128)S(1)}, s32[32]{0:T(128)}, u32[]{:S(2)}) copy-start(s32[32]{0:T(128)} %param.18) | copy-start | bytes 388
  0.7 57.5 %copy-start.3 = (f32[256]{0:T(256)S(1)}, f32[256]{0:T(256)}, u32[]{:S(2)}) copy-start(f32[256]{0:T(256)} %param.14) | copy-start | bytes 3076
  0.7 57.5 %copy-start = (bf16[128,256]{1,0:T(8,128)(2,1)S(1)}, bf16[128,256]{1,0:T(8,128)(2,1)}, u32[]{:S(2)}) copy-start(bf16[128,256]{1,0:T(8,128)(2,1)} %weight.1) | copy-start | bytes 196612
  0.7 57.5 %copy-start.4 = (f32[128]{0:T(128)S(1)}, f32[128]{0:T(128)}, u32[]{:S(2)}) copy-start(f32[128]{0:T(128)} %param.12) | copy-start | bytes 1540
  1.7 7.7 %collective-permute-start.6 = (bf16[256,128]{1,0:T(8,128)(2,1)S(1)}, bf16[256,128]{1,0:T(8,128)(2,1)S(1)}, u32[]{:S(2)}, u32[]{:S(2)}) collective-permute-start(bf16[256,128]{1,0:T(8,128)(2,1)S(1)} %multiply_convert_fusion.refs_0_), channel_id=1, source_target_pairs={{0,7},{1,6},{2,5},{3,4},{4,3},{5,2},{6,1},{7,0},{8,15},{9,14},{10,... | collective-permute-start | bytes 196616 | tf_op jit(solution)/shard_map/ppermute | solution.py:47
  5.6 6.9 %collective-permute-start.5 = (bf16[256,128]{1,0:T(8,128)(2,1)S(1)}, bf16[256,128]{1,0:T(8,128)(2,1)S(1)}, u32[]{:S(2)}, u32[]{:S(2)}) collective-permute-start(bf16[256,128]{1,0:T(8,128)(2,1)S(1)} %multiply_convert_fusion.refs_0_), channel_id=1, source_target_pairs={{0,6},{1,7},{2,4},{3,5},{4,2},{5,3},{6,0},{7,1},{8,14},{9,15},{10,... | collective-permute-start | bytes 196616 | tf_op jit(solution)/shard_map/ppermute | solution.py:47
  7.6 5.7 %collective-permute-start.4 = (bf16[256,128]{1,0:T(8,128)(2,1)S(1)}, bf16[256,128]{1,0:T(8,128)(2,1)S(1)}, u32[]{:S(2)}, u32[]{:S(2)}) collective-permute-start(bf16[256,128]{1,0:T(8,128)(2,1)S(1)} %multiply_convert_fusion.refs_0_), channel_id=1, source_target_pairs={{0,5},{1,4},{2,7},{3,6},{4,1},{5,0},{6,3},{7,2},{8,13},{9,12},{10,... | collective-permute-start | bytes 196616 | tf_op jit(solution)/shard_map/ppermute | solution.py:47
  7.6 5.7 %collective-permute-start.3 = (bf16[256,128]{1,0:T(8,128)(2,1)S(1)}, bf16[256,128]{1,0:T(8,128)(2,1)S(1)}, u32[]{:S(2)}, u32[]{:S(2)}) collective-permute-start(bf16[256,128]{1,0:T(8,128)(2,1)S(1)} %multiply_convert_fusion.refs_0_), channel_id=1, source_target_pairs={{0,4},{1,5},{2,6},{3,7},{4,0},{5,1},{6,2},{7,3},{8,12},{9,13},{10,... | collective-permute-start | bytes 196616 | tf_op jit(solution)/shard_map/ppermute | solution.py:47
  9.0 4.7 %collective-permute-start.2 = (bf16[256,128]{1,0:T(8,128)(2,1)S(1)}, bf16[256,128]{1,0:T(8,128)(2,1)S(1)}, u32[]{:S(2)}, u32[]{:S(2)}) collective-permute-start(bf16[256,128]{1,0:T(8,128)(2,1)S(1)} %multiply_convert_fusion.refs_0_), channel_id=1, source_target_pairs={{0,3},{1,2},{2,1},{3,0},{4,7},{5,6},{6,5},{7,4},{8,11},{9,10},{10,... | collective-permute-start | bytes 196616 | tf_op jit(solution)/shard_map/ppermute | solution.py:47
  9.4 6.4 %collective-permute-start.1 = (bf16[256,128]{1,0:T(8,128)(2,1)S(1)}, bf16[256,128]{1,0:T(8,128)(2,1)S(1)}, u32[]{:S(2)}, u32[]{:S(2)}) collective-permute-start(bf16[256,128]{1,0:T(8,128)(2,1)S(1)} %multiply_convert_fusion.refs_0_), channel_id=1, source_target_pairs={{0,2},{1,3},{2,0},{3,1},{4,6},{5,7},{6,4},{7,5},{8,10},{9,11},{10,... | collective-permute-start | bytes 196616 | tf_op jit(solution)/shard_map/ppermute | solution.py:47
  12.6 3.2 %collective-permute-start = (bf16[256,128]{1,0:T(8,128)(2,1)S(1)}, bf16[256,128]{1,0:T(8,128)(2,1)S(1)}, u32[]{:S(2)}, u32[]{:S(2)}) collective-permute-start(bf16[256,128]{1,0:T(8,128)(2,1)S(1)} %multiply_convert_fusion.refs_0_), channel_id=1, source_target_pairs={{0,1},{1,0},{2,3},{3,2},{4,5},{5,4},{6,7},{7,6},{8,9},{9,8},{10,11... | collective-permute-start | bytes 196616 | tf_op jit(solution)/shard_map/ppermute | solution.py:47
  13.3 94.7 %copy-start.2 = (f32[256]{0:T(256)S(1)}, f32[256]{0:T(256)}, u32[]{:S(2)}) copy-start(f32[256]{0:T(256)} %param.11) | copy-start | bytes 3076
  73.3 19.1 %all-to-all-start.3 = ((f32[32,8,128]{2,1,0:T(8,128)}), f32[32,8,128]{2,1,0:T(8,128)S(1)}, u32[]{:S(2)}, u32[]{:S(2)}) async-start(f32[32,8,128]{2,1,0:T(8,128)} %get-tuple-element.24), calls=%async_computation.3 | async-start | bytes 262144 | tf_op jit(solution)/shard_map/all_to_all | solution.py:51
  87.2 6.8 %collective-permute-start.7 = (bf16[1040,128]{1,0:T(8,128)(2,1)S(1)}, bf16[1040,128]{1,0:T(8,128)(2,1)S(1)}, u32[]{:S(2)}, u32[]{:S(2)}) collective-permute-start(bf16[1040,128]{1,0:T(8,128)(2,1)S(1)} %get-tuple-element.23), channel_id=1, source_target_pairs={{0,1},{1,0},{2,3},{3,2},{4,5},{5,4},{6,7},{7,6},{8,9},{9,8},{10,11... | collective-permute-start | bytes 798728 | tf_op jit(solution)/shard_map/ppermute | solution.py:47
  92.4 2.6 %collective-permute-start.8 = (f32[32,8,128]{2,1,0:T(8,128)S(1)}, f32[32,8,128]{2,1,0:T(8,128)S(1)}, u32[]{:S(2)}, u32[]{:S(2)}) collective-permute-start(f32[32,8,128]{2,1,0:T(8,128)S(1)} %all-to-all-done.3.grads), channel_id=1, source_target_pairs={{0,1},{1,0},{2,3},{3,2},{4,5},{5,4},{6,7},{7,6},{8,9},{9,8},{10,11... | collective-permute-start | bytes 393224 | tf_op jit(solution)/shard_map/ppermute | solution.py:47

commit v3 on v2

--- a/solution.py
+++ b/solution.py
@@ -16,12 +16,13 @@
 SMEM = pl.BlockSpec(memory_space=pltpu.SMEM)
 F32, BF16 = jnp.float32, jnp.bfloat16
 PAIRS = 96
-HALF_AT = 120
+UNROLL = 4
+PHASES = 4
+COUNT_AT = 112
 EMPTY = 160
 STEP = 8
 GRADS = HID + 16
 PACK = TGT + 16
-Y_GROUPS = [[y * NZ + z for y in range(NY)] for z in range(NZ)]
 Z_GROUPS = [[y * NZ + z for z in range(NZ)] for y in range(NY)]
 X_GROUPS = [[x * NCORE + core for x in range(NX)] for core in range(NCORE)]
 
@@ -58,8 +59,8 @@
 
 
 def forward_kernel(ids, mask, *refs):
-    pieces, (out, kept, pairs) = refs[:DOM], refs[DOM : DOM + 3]
-    sources, totals, staged, edges, waiting, mask_sems, kept_sems = refs[DOM + 3 :]
+    pieces, (kept, pairs), outs = refs[:DOM], refs[DOM : DOM + 2], refs[DOM + 2 : DOM + 9]
+    sources, totals, staged, edges, waiting, mask_sems, kept_sems = refs[DOM + 9 :]
     steps = mask.shape[0] // STEP
 
     def mask_copy(i):
@@ -85,26 +86,24 @@
 
     def step(i, n):
         mask_copy(i).wait()
-        products = []
         for u in range(STEP):
             t = i * STEP + u
             r, c = ids[t] >> 4, ids[t] & 15
             tile = staged[t].astype(F32).astype(BF16)
             edges[t] = tile
-            products.append((r, jnp.dot(tile, sources[c], preferred_element_type=F32)))
+            totals[r] = totals[r] + jnp.dot(tile, sources[c], preferred_element_type=F32)
             first = waiting[r]
             paired = first >= 0
             pairs[n] = (first & 255) | (t << 8) | ((first >> 8) << 16) | (c << 20) | (r << 24)
             waiting[r] = jnp.where(paired, -1, t | (c << 8))
             n = n + jnp.where(paired, 1, 0)
-        for r, product in products:
-            totals[r] = totals[r] + product
         kept_copy(i).start()
         return n
 
-    n = lax.fori_loop(0, steps // 2, step, 0)
-    pairs[HALF_AT] = n
-    n = lax.fori_loop(steps // 2, steps, step, n)
+    n = 0
+    for phase in range(PHASES):
+        n = lax.fori_loop(phase * steps // PHASES, (phase + 1) * steps // PHASES, step, n)
+        pairs[COUNT_AT + phase] = n // UNROLL
     for r in range(COL):
         first = waiting[r]
         pairs[n] = (first & 255) | (EMPTY << 8) | ((first >> 8) << 16) | (r << 24)
@@ -115,8 +114,21 @@
         return carry
 
     lax.fori_loop(n, PAIRS, fill, 0)
-    for r in range(COL):
-        out[r] = totals[r].astype(BF16)
+    pairs[COUNT_AT + PHASES] = (n + UNROLL - 1) // UNROLL
+    y = lax.axis_index("col") >> 3
+    half = NZ // 2
+    own, far_up, far_down, up_low, up_high, down_low, down_high = outs
+    for out, step_to, first, count in (
+        (far_up, 2, 0, half),
+        (far_down, 2, half, half),
+        (up_high, 1, half, half),
+        (down_low, 3, 0, half),
+        (up_low, 1, 0, half),
+        (down_high, 3, half, half),
+        (own, 0, 0, NZ),
+    ):
+        for z in range(count):
+            out[z] = totals[((y + step_to) & 3) * NZ + first + z].astype(BF16)
     for i in range(steps + 1):
         kept_copy(i).wait()
 
@@ -126,13 +138,11 @@
     steps = tiles // STEP
     return pl.pallas_call(
         forward_kernel,
-        out_shape=[
-            sds((COL, BLK, F), BF16),
-            sds((tiles + STEP, BLK, BLK), BF16),
-            sds((BLK,), jnp.int32),
-        ],
+        out_shape=[sds((tiles + STEP, BLK, BLK), BF16), sds((BLK,), jnp.int32)]
+        + [sds((NZ, BLK, F), BF16)]
+        + [sds((NZ // 2, BLK, F), BF16)] * 6,
         in_specs=[SMEM, HBM] + [VMEM] * DOM,
-        out_specs=[VMEM, HBM, SMEM],
+        out_specs=[HBM, SMEM] + [VMEM] * 7,
         scratch_shapes=[
             pltpu.VMEM((DOM * 2, BLK, F), BF16),
             pltpu.VMEM((COL, BLK, F), F32),
@@ -157,12 +167,24 @@
     return 1.0 / (1.0 + jnp.exp(-v))
 
 
-def y_sum_kernel(parts, out):
-    for z in range(NZ):
-        total = (parts[0, z].astype(F32) + parts[1, z].astype(F32)) + (
-            parts[2, z].astype(F32) + parts[3, z].astype(F32)
-        )
-        out[z] = total.astype(BF16)
+def relay_kernel(up, far_up, down, far_down, out_up, out_down):
+    for z in range(NZ // 2):
+        out_up[z] = (up[z].astype(F32) + far_up[z].astype(F32)).astype(BF16)
+        out_down[z] = (down[z].astype(F32) + far_down[z].astype(F32)).astype(BF16)
+
+
+def y_sum_kernel(own, low_above, low_below, high_below, high_above, out):
+    half = NZ // 2
+    for z in range(half):
+        low = low_above[z].astype(F32) + low_below[z].astype(F32)
+        out[z] = (own[z].astype(F32) + low).astype(BF16)
+        high = high_below[z].astype(F32) + high_above[z].astype(F32)
+        out[z + half] = (own[z + half].astype(F32) + high).astype(BF16)
+
+
+def step_y(value, step):
+    pairs = [(i, ((i // NZ + step) % NY) * NZ + i % NZ) for i in range(COL)]
+    return lax.ppermute(value, "col", pairs)
 
 
 def dense_kernel(parts, dest_scale, weight, bias, targets, upstream, hidden, packed):
@@ -267,35 +289,36 @@
 
 def backward_kernel(pairs, kept, packed, bias, own, other, edges, returned, totals, sems):
     my_core = lax.axis_index("dom") & 1
-    copies = []
-    for i in range(kept.shape[0] // STEP):
+    last = kept.shape[0] // STEP - 1
+
+    def kept_copy(i):
         at = pl.ds(i * STEP, STEP)
-        copies.append(pltpu.make_async_copy(kept.at[at], edges.at[at], sems.at[i]))
-        copies[-1].start()
+        return pltpu.make_async_copy(kept.at[at], edges.at[at], sems.at[i])
+
+    for i in range(last + 1):
+        kept_copy(i).start()
     for ref in (own, other):
         ref[NX * 256 :, :] = bias_rows(bias[...])
     unpack(packed, returned)
     totals[...] = jnp.zeros_like(totals)
-    half = len(copies) // 2
-    for copy in copies[:half]:
-        copy.wait()
-    unroll = 4
-
-    def pair_step(i, carry):
-        products = []
-        for u in range(unroll):
-            both, c1, c2, r = pair_of(pairs, edges, i * unroll + u)
-            products.append((c1, c2, jnp.dot(returned[r], both, preferred_element_type=F32)))
-        for c1, c2, product in products:
+
+    def step(g, carry):
+        for u in range(UNROLL):
+            both, c1, c2, r = pair_of(pairs, edges, g * UNROLL + u)
+            product = jnp.dot(returned[r], both, preferred_element_type=F32)
             totals[c1] = totals[c1] + product[:, :BLK]
             totals[c2] = totals[c2] + product[:, BLK:]
         return carry
 
-    early = pairs[HALF_AT] // unroll
-    lax.fori_loop(0, early, pair_step, 0)
-    for copy in copies[half:]:
-        copy.wait()
-    lax.fori_loop(early, PAIRS // unroll, pair_step, 0)
+    done = 0
+    for phase in range(PHASES):
+        for i in range(phase * last // PHASES, (phase + 1) * last // PHASES):
+            kept_copy(i).wait()
+        until = pairs[COUNT_AT + phase]
+        lax.fori_loop(done, until, step, 0)
+        done = until
+    kept_copy(last).wait()
+    lax.fori_loop(done, pairs[COUNT_AT + PHASES], step, 0)
     for x in range(NX):
         for half in range(2):
             rows_at = pl.ds(x * 256 + half * BLK, BLK)
@@ -348,11 +371,21 @@
     upstream,
 ):
     scaled = (source_feats.astype(F32) * source_scale[:, None]).astype(BF16)
-    pieces = [scaled] + [exchange_dom(scaled, k) for k in range(1, DOM)]
+    along_x = [scaled] + [exchange_dom(scaled, NCORE * k) for k in range(1, NX)]
+    pieces = [piece for held in along_x for piece in (held, exchange_dom(held, 1))]
     products = 2 * tile_mask.shape[0] * BLK**3
-    partials, kept, pairs = forward(tile_rows * 16 + tile_cols, tile_mask, pieces)
-    parts = swap(partials.reshape(NY, NZ, BLK, F), "col", Y_GROUPS)
-    (line,) = call(y_sum_kernel, [sds((NZ, BLK, F), BF16)], [VMEM])(parts)
+    kept, pairs, own, far_up, far_down, up_low, up_high, down_low, down_high = forward(
+        tile_rows * 16 + tile_cols, tile_mask, pieces
+    )
+    far_up, far_down = step_y(far_up, 1), step_y(far_down, -1)
+    high_below, low_above = step_y(up_high, 1), step_y(down_low, -1)
+    up, down = call(relay_kernel, [sds((NZ // 2, BLK, F), BF16)] * 2, [VMEM] * 4)(
+        up_low, far_up, down_high, far_down
+    )
+    low_below, high_above = step_y(up, 1), step_y(down, -1)
+    (line,) = call(y_sum_kernel, [sds((NZ, BLK, F), BF16)], [VMEM] * 5)(
+        own, low_above, low_below, high_below, high_above
+    )
     parts = swap(line, "col", Z_GROUPS)
     hidden, packed = call(
         dense_kernel,

time: 109 us -> 102 us (0.936)
  blocking collectives: 60.7 us -> 43.1 us
  starting transfers between devices: 23 us -> 31.2 us
  waiting for transfers between devices: 3.47 us -> 6.28 us
    all_to_all x4 -> x3, blocking collectives: 60.7 us -> 43.1 us  [swap(): lax.all_to_all(value, axis, 0, 0, axis_index_groups=groups, tiled=True)]
    ppermute x0 -> x6, starting transfers between devices: none -> 7.12 us  [step_y(): return lax.ppermute(value, 'col', pairs)]
    ppermute x0 -> x6, waiting for transfers between devices: none -> 4.98 us  [step_y(): return lax.ppermute(value, 'col', pairs)]
    ppermute x9, waiting for transfers between devices: 3.47 us -> 1.3 us  [exchange_dom(): return lax.ppermute(value, 'dom', pairs)]
    ppermute x9, starting transfers between devices: 17.7 us -> 18.9 us  [exchange_dom(): return lax.ppermute(value, 'dom', pairs)]
    pallas_call x2 -> x3, Pallas kernels: 8 us -> 7.99 us  [the longest x1 7.83 us: forward(): pl.pallas_call(forward_kernel, out_shape=[sds((tiles + STEP, BLK, BLK), B...]
  transfers between devices with their start and end apart: 10 -> 16, of which waited for: 3 -> 5; matrix products, arithmetic and copies ran while one was open for 1% -> 1% of each run, Pallas kernels for 8% -> 8%
where the time goes in v3:
time: 102 us
  blocking collectives  43.1 us (42%)
  starting transfers between devices  31.2 us (31%)
  Pallas kernels  18.5 us (18%)
  waiting for transfers between devices  6.28 us (6%)
  other arithmetic  1.68 us (2%)
    all_to_all x3, blocking collectives, swap(): lax.all_to_all(value, axis, 0, 0, axis_index_groups=groups, tiled=True)  43.1 us
    ppermute x9, starting transfers between devices, exchange_dom(): return lax.ppermute(value, 'dom', pairs)  18.9 us
    pallas_call x1, Pallas kernels, body(): call(backward_kernel, [sds((NX * 256 + 16, F), BF16)] * 2, [SMEM, HBM, VM...  7.97 us
    pallas_call x1, Pallas kernels, forward(): pl.pallas_call(forward_kernel, out_shape=[sds((tiles + STEP, BLK, BLK), B...  7.83 us
    ppermute x6, starting transfers between devices, step_y(): return lax.ppermute(value, 'col', pairs)  7.12 us
    all_to_all x1, starting transfers between devices, swap(): lax.all_to_all(value, axis, 0, 0, axis_index_groups=groups, tiled=True)  5.22 us
    ppermute x6, waiting for transfers between devices, step_y(): return lax.ppermute(value, 'col', pairs)  4.98 us
  transfers between devices with their start and end apart: 16, of which 5 were waited for; matrix products, arithmetic and copies ran while one was open for 1% of the time, Pallas kernels for 8%

profile of v3, /device:TPU:1, one launch (start us, length us, event | category | flops | bytes accessed | tf_op | source)
XLA Modules:
  0.0 101.5 jit_solution(14445187196796967433)
XLA Ops:
  0.7 1.0 multiply_convert_fusion.refs_0_
  1.7 3.4 %collective-permute-start.5 = (bf16[256,128]{1,0:T(8,128)(2,1)S(1)}, bf16[256,128]{1,0:T(8,128)(2,1)S(1)}, u32[]{:S(2)}, u32[]{:S(2)}) collective-permute-start(bf16[256,128]{1,0:T(8,128)(2,1)S(1)} %multiply_convert_fusion.refs_0_), channel_id=1, source_target_pairs={{0,6},{1,7},{2,4},{3,5},{4,2},{5,3},{6,0},{7,1},{8,14},{9,15},{10,... | collective-permute-start | bytes 196616 | tf_op jit(solution)/shard_map/ppermute | solution.py:48
  5.1 0.5 collective-permute-start.3
  5.6 0.2 collective-permute-start.1
  5.7 3.3 %collective-permute-start = (bf16[256,128]{1,0:T(8,128)(2,1)S(1)}, bf16[256,128]{1,0:T(8,128)(2,1)S(1)}, u32[]{:S(2)}, u32[]{:S(2)}) collective-permute-start(bf16[256,128]{1,0:T(8,128)(2,1)S(1)} %multiply_convert_fusion.refs_0_), channel_id=1, source_target_pairs={{0,1},{1,0},{2,3},{3,2},{4,5},{5,4},{6,7},{7,6},{8,9},{9,8},{10,11... | collective-permute-start | bytes 196616 | tf_op jit(solution)/shard_map/ppermute | solution.py:48
  9.1 2.0 %collective-permute-start.6 = (bf16[256,128]{1,0:T(8,128)(2,1)S(1)}, bf16[256,128]{1,0:T(8,128)(2,1)S(1)}, u32[]{:S(2)}, u32[]{:S(2)}) collective-permute-start(bf16[256,128]{1,0:T(8,128)(2,1)S(1)} %collective-permute-done.5.refs_6_), channel_id=1, source_target_pairs={{0,1},{1,0},{2,3},{3,2},{4,5},{5,4},{6,7},{7,6},{8,9},{9,8},{10,11... | collective-permute-start | bytes 196616 | tf_op jit(solution)/shard_map/ppermute | solution.py:48
  11.1 0.7 collective-permute-start.4
  11.8 0.2 collective-permute-start.2
  12.0 0.7 multiply_add_fusion.ids
  12.8 0.3 collective-permute-done.2.refs_3_
  13.1 7.8 %shard_map.129 = (bf16[168,128,128]{2,1,0:T(8,128)(2,1)}, s32[128]{0:T(128)S(1)}, bf16[8,128,128]{2,1,0:T(8,128)(2,1)S(1)}, bf16[4,128,128]{2,1,0:T(8,128)(2,1)S...) custom-call(s32[160]{0:T(256)S(1)} %multiply_add_fusion.ids, ...), custom_call_target="tpu_custom_call" | custom-call | flops 671088640 | bytes 15728640 | tf_op jit(solution)/shard_map/pallas_call | solution.py:139
  20.9 1.4 %collective-permute-start.8 = (bf16[4,128,128]{2,1,0:T(8,128)(2,1)S(1)}, bf16[4,128,128]{2,1,0:T(8,128)(2,1)S(1)}, u32[]{:S(2)}, u32[]{:S(2)}) collective-permute-start(bf16[4,128,128]{2,1,0:T(8,128)(2,1)S(1)} %get-tuple-element.27), channel_id=1, source_target_pairs={{0,64},{8,72},{16,80},{24,88},{32,96},{40,104},{48,112},{56,120},{... | collective-permute-start | bytes 393224 | tf_op jit(solution)/shard_map/ppermute | solution.py:187
  22.3 1.5 %collective-permute-start.9 = (bf16[4,128,128]{2,1,0:T(8,128)(2,1)S(1)}, bf16[4,128,128]{2,1,0:T(8,128)(2,1)S(1)}, u32[]{:S(2)}, u32[]{:S(2)}) collective-permute-start(bf16[4,128,128]{2,1,0:T(8,128)(2,1)S(1)} %get-tuple-element.29), channel_id=1, source_target_pairs={{0,192},{8,200},{16,208},{24,216},{32,224},{40,232},{48,240},{56,2... | collective-permute-start | bytes 393224 | tf_op jit(solution)/shard_map/ppermute | solution.py:187
  23.8 1.4 %collective-permute-start.7 = (bf16[4,128,128]{2,1,0:T(8,128)(2,1)S(1)}, bf16[4,128,128]{2,1,0:T(8,128)(2,1)S(1)}, u32[]{:S(2)}, u32[]{:S(2)}) collective-permute-start(bf16[4,128,128]{2,1,0:T(8,128)(2,1)S(1)} %get-tuple-element.25), channel_id=1, source_target_pairs={{0,192},{8,200},{16,208},{24,216},{32,224},{40,232},{48,240},{56,2... | collective-permute-start | bytes 393224 | tf_op jit(solution)/shard_map/ppermute | solution.py:187
  25.2 0.1 collective-permute-start.11
  25.3 1.9 %collective-permute-done.8.far_up = bf16[4,128,128]{2,1,0:T(8,128)(2,1)S(1)} collective-permute-done((bf16[4,128,128]{2,1,0:T(8,128)(2,1)S(1)}, bf16[4,128,128]{2,1,0:T(8,128)(2,1)S(1)}, u32[]{:S(2)}, u32[]{:S(2)}) %collective-permute-start.8) | collective-permute-done | bytes 131104 | tf_op jit(solution)/shard_map/ppermute | solution.py:187
  27.2 1.1 %collective-permute-start.10 = (bf16[4,128,128]{2,1,0:T(8,128)(2,1)S(1)}, bf16[4,128,128]{2,1,0:T(8,128)(2,1)S(1)}, u32[]{:S(2)}, u32[]{:S(2)}) collective-permute-start(bf16[4,128,128]{2,1,0:T(8,128)(2,1)S(1)} %get-tuple-element.30), channel_id=1, source_target_pairs={{0,64},{8,72},{16,80},{24,88},{32,96},{40,104},{48,112},{56,120},{... | collective-permute-start | bytes 393224 | tf_op jit(solution)/shard_map/ppermute | solution.py:187
  28.3 1.7 %collective-permute-start.12 = (bf16[4,128,128]{2,1,0:T(8,128)(2,1)S(1)}, bf16[4,128,128]{2,1,0:T(8,128)(2,1)S(1)}, u32[]{:S(2)}, u32[]{:S(2)}) collective-permute-start(bf16[4,128,128]{2,1,0:T(8,128)(2,1)S(1)} %get-tuple-element.32), channel_id=1, source_target_pairs={{0,192},{8,200},{16,208},{24,216},{32,224},{40,232},{48,240},{56,2... | collective-permute-start | bytes 393224 | tf_op jit(solution)/shard_map/ppermute | solution.py:187
  30.0 0.2 collective-permute-done.11.high_below
  30.2 2.9 %collective-permute-done.10.low_below = bf16[4,128,128]{2,1,0:T(8,128)(2,1)S(1)} collective-permute-done((bf16[4,128,128]{2,1,0:T(8,128)(2,1)S(1)}, bf16[4,128,128]{2,1,0:T(8,128)(2,1)S(1)}, u32[]{:S(2)}, u32[]{:S(2)}) %collective-permute-start.10) | collective-permute-done | bytes 131104 | tf_op jit(solution)/shard_map/ppermute | solution.py:187
  33.1 0.1 shard_map.131
  33.2 17.4 %all_to_all.20.parts = bf16[8,128,128]{2,1,0:T(8,128)(2,1)S(1)} all-to-all(bf16[8,128,128]{2,1,0:T(8,128)(2,1)S(1)} %shard_map.131), channel_id=1, replica_groups={{0,8,16,24,32,40,48,56},{64,72,80,88,96,104,112,120},{128,136,144,152,1..., dimensions={0} | all-to-all | bytes 524288 | tf_op jit(solution)/shard_map/all_to_all | solution.py:52
  50.6 1.0 shard_map.132
  51.5 13.9 %all_to_all.21.packed = bf16[32,48,128]{2,1,0:T(8,128)(2,1)S(1)} all-to-all(bf16[32,48,128]{2,1,0:T(8,128)(2,1)S(1)} %get-tuple-element.36), channel_id=1, replica_groups=mesh['col'=32,'dom'=8] {'col'}, dimensions={0} | all-to-all | bytes 786432 | tf_op jit(solution)/shard_map/all_to_all | solution.py:52
  65.5 0.7 shard_map.133
  66.2 5.2 %all-to-all-start.2 = ((f32[32,8,128]{2,1,0:T(8,128)}), f32[32,8,128]{2,1,0:T(8,128)S(1)}, u32[]{:S(2)}, u32[]{:S(2)}) async-start(f32[32,8,128]{2,1,0:T(8,128)} %get-tuple-element.40), calls=%async_computation.2 | async-start | bytes 262144 | tf_op jit(solution)/shard_map/all_to_all | solution.py:52
  71.4 8.0 %shard_map.134 = (bf16[1040,128]{1,0:T(8,128)(2,1)S(1)}, bf16[1040,128]{1,0:T(8,128)(2,1)S(1)}) custom-call(s32[128]{0:T(128)S(1)} %get-tuple-element.34.pairs, bf16[168,128,128]{2,1,0:T(8,128)(2,1)} %get-tuple-element.35.kept, bf16[32,48,128]{2,1,0:T(8,128)(2,1)S(1)} %all_to_all.21.packed, f32[1,256]{1,0:T(1,128)S(1)} %get-tuple-element.37.bias), custom_call_target="tpu_custom_call" | custom-call | flops 671088640 | tf_op jit(solution)/shard_map/pallas_call | solution.py:407
  79.4 6.3 %collective-permute-start.13 = (bf16[1040,128]{1,0:T(8,128)(2,1)S(1)}, bf16[1040,128]{1,0:T(8,128)(2,1)S(1)}, u32[]{:S(2)}, u32[]{:S(2)}) collective-permute-start(bf16[1040,128]{1,0:T(8,128)(2,1)S(1)} %get-tuple-element.39), channel_id=1, source_target_pairs={{0,1},{1,0},{2,3},{3,2},{4,5},{5,4},{6,7},{7,6},{8,9},{9,8},{10,11... | collective-permute-start | bytes 798728 | tf_op jit(solution)/shard_map/ppermute | solution.py:48
  85.7 2.2 %collective-permute-start.14 = (f32[32,8,128]{2,1,0:T(8,128)S(1)}, f32[32,8,128]{2,1,0:T(8,128)S(1)}, u32[]{:S(2)}, u32[]{:S(2)}) collective-permute-start(f32[32,8,128]{2,1,0:T(8,128)S(1)} %all-to-all-done.2.grads), channel_id=1, source_target_pairs={{0,1},{1,0},{2,3},{3,2},{4,5},{5,4},{6,7},{7,6},{8,9},{9,8},{10,11... | collective-permute-start | bytes 393224 | tf_op jit(solution)/shard_map/ppermute | solution.py:48
  87.9 1.0 collective-permute-done.14.grads_got
  89.0 11.8 %all_to_all.22.parts = bf16[4,528,128]{2,1,0:T(8,128)(2,1)S(1)} all-to-all(bf16[4,528,128]{2,1,0:T(8,128)(2,1)S(1)} %shard_map.135), channel_id=1, replica_groups={{0,2,4,6},{1,3,5,7},{8,10,12,14},{9,11,13,15},{16,18,20,22},{17,19,21,2..., dimensions={0} | all-to-all | bytes 1081344 | tf_op jit(solution)/shard_map/all_to_all | solution.py:52
  100.7 0.8 shard_map.136
  (25 shorter events, 0.2 us)
Async XLA Ops:
  0.6 49.9 %copy-start.1 = (bf16[32,256]{1,0:T(8,128)(2,1)S(1)}, bf16[32,256]{1,0:T(8,128)(2,1)}, u32[]{:S(2)}) copy-start(bf16[32,256]{1,0:T(8,128)(2,1)} %upstream.1) | copy-start | bytes 49156
  0.6 49.9 %copy-start.5 = (s32[32]{0:T(128)S(1)}, s32[32]{0:T(128)}, u32[]{:S(2)}) copy-start(s32[32]{0:T(128)} %param.18) | copy-start | bytes 388
  0.7 49.9 %copy-start.3 = (f32[256]{0:T(256)S(1)}, f32[256]{0:T(256)}, u32[]{:S(2)}) copy-start(f32[256]{0:T(256)} %param.14) | copy-start | bytes 3076
  0.7 49.9 %copy-start = (bf16[128,256]{1,0:T(8,128)(2,1)S(1)}, bf16[128,256]{1,0:T(8,128)(2,1)}, u32[]{:S(2)}) copy-start(bf16[128,256]{1,0:T(8,128)(2,1)} %weight.1) | copy-start | bytes 196612
  0.7 49.9 %copy-start.4 = (f32[128]{0:T(128)S(1)}, f32[128]{0:T(128)}, u32[]{:S(2)}) copy-start(f32[128]{0:T(128)} %param.12) | copy-start | bytes 1540
  1.7 7.4 %collective-permute-start.5 = (bf16[256,128]{1,0:T(8,128)(2,1)S(1)}, bf16[256,128]{1,0:T(8,128)(2,1)S(1)}, u32[]{:S(2)}, u32[]{:S(2)}) collective-permute-start(bf16[256,128]{1,0:T(8,128)(2,1)S(1)} %multiply_convert_fusion.refs_0_), channel_id=1, source_target_pairs={{0,6},{1,7},{2,4},{3,5},{4,2},{5,3},{6,0},{7,1},{8,14},{9,15},{10,... | collective-permute-start | bytes 196616 | tf_op jit(solution)/shard_map/ppermute | solution.py:48
  5.1 6.0 %collective-permute-start.3 = (bf16[256,128]{1,0:T(8,128)(2,1)S(1)}, bf16[256,128]{1,0:T(8,128)(2,1)S(1)}, u32[]{:S(2)}, u32[]{:S(2)}) collective-permute-start(bf16[256,128]{1,0:T(8,128)(2,1)S(1)} %multiply_convert_fusion.refs_0_), channel_id=1, source_target_pairs={{0,4},{1,5},{2,6},{3,7},{4,0},{5,1},{6,2},{7,3},{8,12},{9,13},{10,... | collective-permute-start | bytes 196616 | tf_op jit(solution)/shard_map/ppermute | solution.py:48
  5.6 6.2 %collective-permute-start.1 = (bf16[256,128]{1,0:T(8,128)(2,1)S(1)}, bf16[256,128]{1,0:T(8,128)(2,1)S(1)}, u32[]{:S(2)}, u32[]{:S(2)}) collective-permute-start(bf16[256,128]{1,0:T(8,128)(2,1)S(1)} %multiply_convert_fusion.refs_0_), channel_id=1, source_target_pairs={{0,2},{1,3},{2,0},{3,1},{4,6},{5,7},{6,4},{7,5},{8,10},{9,11},{10,... | collective-permute-start | bytes 196616 | tf_op jit(solution)/shard_map/ppermute | solution.py:48
  5.7 7.0 %collective-permute-start = (bf16[256,128]{1,0:T(8,128)(2,1)S(1)}, bf16[256,128]{1,0:T(8,128)(2,1)S(1)}, u32[]{:S(2)}, u32[]{:S(2)}) collective-permute-start(bf16[256,128]{1,0:T(8,128)(2,1)S(1)} %multiply_convert_fusion.refs_0_), channel_id=1, source_target_pairs={{0,1},{1,0},{2,3},{3,2},{4,5},{5,4},{6,7},{7,6},{8,9},{9,8},{10,11... | collective-permute-start | bytes 196616 | tf_op jit(solution)/shard_map/ppermute | solution.py:48
  9.1 3.6 %collective-permute-start.6 = (bf16[256,128]{1,0:T(8,128)(2,1)S(1)}, bf16[256,128]{1,0:T(8,128)(2,1)S(1)}, u32[]{:S(2)}, u32[]{:S(2)}) collective-permute-start(bf16[256,128]{1,0:T(8,128)(2,1)S(1)} %collective-permute-done.5.refs_6_), channel_id=1, source_target_pairs={{0,1},{1,0},{2,3},{3,2},{4,5},{5,4},{6,7},{7,6},{8,9},{9,8},{10,11... | collective-permute-start | bytes 196616 | tf_op jit(solution)/shard_map/ppermute | solution.py:48
  11.1 1.7 %collective-permute-start.4 = (bf16[256,128]{1,0:T(8,128)(2,1)S(1)}, bf16[256,128]{1,0:T(8,128)(2,1)S(1)}, u32[]{:S(2)}, u32[]{:S(2)}) collective-permute-start(bf16[256,128]{1,0:T(8,128)(2,1)S(1)} %collective-permute-done.3.refs_4_), channel_id=1, source_target_pairs={{0,1},{1,0},{2,3},{3,2},{4,5},{5,4},{6,7},{7,6},{8,9},{9,8},{10,11... | collective-permute-start | bytes 196616 | tf_op jit(solution)/shard_map/ppermute | solution.py:48
  11.8 1.3 %collective-permute-start.2 = (bf16[256,128]{1,0:T(8,128)(2,1)S(1)}, bf16[256,128]{1,0:T(8,128)(2,1)S(1)}, u32[]{:S(2)}, u32[]{:S(2)}) collective-permute-start(bf16[256,128]{1,0:T(8,128)(2,1)S(1)} %collective-permute-done.1.refs_2_), channel_id=1, source_target_pairs={{0,1},{1,0},{2,3},{3,2},{4,5},{5,4},{6,7},{7,6},{8,9},{9,8},{10,11... | collective-permute-start | bytes 196616 | tf_op jit(solution)/shard_map/ppermute | solution.py:48
  12.7 88.0 %copy-start.2 = (f32[256]{0:T(256)S(1)}, f32[256]{0:T(256)}, u32[]{:S(2)}) copy-start(f32[256]{0:T(256)} %param.11) | copy-start | bytes 3076
  20.9 6.3 %collective-permute-start.8 = (bf16[4,128,128]{2,1,0:T(8,128)(2,1)S(1)}, bf16[4,128,128]{2,1,0:T(8,128)(2,1)S(1)}, u32[]{:S(2)}, u32[]{:S(2)}) collective-permute-start(bf16[4,128,128]{2,1,0:T(8,128)(2,1)S(1)} %get-tuple-element.27), channel_id=1, source_target_pairs={{0,64},{8,72},{16,80},{24,88},{32,96},{40,104},{48,112},{56,120},{... | collective-permute-start | bytes 393224 | tf_op jit(solution)/shard_map/ppermute | solution.py:187
  22.3 4.9 %collective-permute-start.9 = (bf16[4,128,128]{2,1,0:T(8,128)(2,1)S(1)}, bf16[4,128,128]{2,1,0:T(8,128)(2,1)S(1)}, u32[]{:S(2)}, u32[]{:S(2)}) collective-permute-start(bf16[4,128,128]{2,1,0:T(8,128)(2,1)S(1)} %get-tuple-element.29), channel_id=1, source_target_pairs={{0,192},{8,200},{16,208},{24,216},{32,224},{40,232},{48,240},{56,2... | collective-permute-start | bytes 393224 | tf_op jit(solution)/shard_map/ppermute | solution.py:187
  23.8 6.2 %collective-permute-start.7 = (bf16[4,128,128]{2,1,0:T(8,128)(2,1)S(1)}, bf16[4,128,128]{2,1,0:T(8,128)(2,1)S(1)}, u32[]{:S(2)}, u32[]{:S(2)}) collective-permute-start(bf16[4,128,128]{2,1,0:T(8,128)(2,1)S(1)} %get-tuple-element.25), channel_id=1, source_target_pairs={{0,192},{8,200},{16,208},{24,216},{32,224},{40,232},{48,240},{56,2... | collective-permute-start | bytes 393224 | tf_op jit(solution)/shard_map/ppermute | solution.py:187
  25.2 5.0 %collective-permute-start.11 = (bf16[4,128,128]{2,1,0:T(8,128)(2,1)S(1)}, bf16[4,128,128]{2,1,0:T(8,128)(2,1)S(1)}, u32[]{:S(2)}, u32[]{:S(2)}) collective-permute-start(bf16[4,128,128]{2,1,0:T(8,128)(2,1)S(1)} %get-tuple-element.31), channel_id=1, source_target_pairs={{0,64},{8,72},{16,80},{24,88},{32,96},{40,104},{48,112},{56,120},{... | collective-permute-start | bytes 393224 | tf_op jit(solution)/shard_map/ppermute | solution.py:187
  27.2 5.8 %collective-permute-start.10 = (bf16[4,128,128]{2,1,0:T(8,128)(2,1)S(1)}, bf16[4,128,128]{2,1,0:T(8,128)(2,1)S(1)}, u32[]{:S(2)}, u32[]{:S(2)}) collective-permute-start(bf16[4,128,128]{2,1,0:T(8,128)(2,1)S(1)} %get-tuple-element.30), channel_id=1, source_target_pairs={{0,64},{8,72},{16,80},{24,88},{32,96},{40,104},{48,112},{56,120},{... | collective-permute-start | bytes 393224 | tf_op jit(solution)/shard_map/ppermute | solution.py:187
  28.3 4.7 %collective-permute-start.12 = (bf16[4,128,128]{2,1,0:T(8,128)(2,1)S(1)}, bf16[4,128,128]{2,1,0:T(8,128)(2,1)S(1)}, u32[]{:S(2)}, u32[]{:S(2)}) collective-permute-start(bf16[4,128,128]{2,1,0:T(8,128)(2,1)S(1)} %get-tuple-element.32), channel_id=1, source_target_pairs={{0,192},{8,200},{16,208},{24,216},{32,224},{40,232},{48,240},{56,2... | collective-permute-start | bytes 393224 | tf_op jit(solution)/shard_map/ppermute | solution.py:187
  66.2 19.5 %all-to-all-start.2 = ((f32[32,8,128]{2,1,0:T(8,128)}), f32[32,8,128]{2,1,0:T(8,128)S(1)}, u32[]{:S(2)}, u32[]{:S(2)}) async-start(f32[32,8,128]{2,1,0:T(8,128)} %get-tuple-element.40), calls=%async_computation.2 | async-start | bytes 262144 | tf_op jit(solution)/shard_map/all_to_all | solution.py:52
  79.4 8.5 %collective-permute-start.13 = (bf16[1040,128]{1,0:T(8,128)(2,1)S(1)}, bf16[1040,128]{1,0:T(8,128)(2,1)S(1)}, u32[]{:S(2)}, u32[]{:S(2)}) collective-permute-start(bf16[1040,128]{1,0:T(8,128)(2,1)S(1)} %get-tuple-element.39), channel_id=1, source_target_pairs={{0,1},{1,0},{2,3},{3,2},{4,5},{5,4},{6,7},{7,6},{8,9},{9,8},{10,11... | collective-permute-start | bytes 798728 | tf_op jit(solution)/shard_map/ppermute | solution.py:48
  85.7 3.2 %collective-permute-start.14 = (f32[32,8,128]{2,1,0:T(8,128)S(1)}, f32[32,8,128]{2,1,0:T(8,128)S(1)}, u32[]{:S(2)}, u32[]{:S(2)}) collective-permute-start(f32[32,8,128]{2,1,0:T(8,128)S(1)} %all-to-all-done.2.grads), channel_id=1, source_target_pairs={{0,1},{1,0},{2,3},{3,2},{4,5},{5,4},{6,7},{7,6},{8,9},{9,8},{10,11... | collective-permute-start | bytes 393224 | tf_op jit(solution)/shard_map/ppermute | solution.py:48

commit v4 on v3

--- a/solution.py
+++ b/solution.py
@@ -15,11 +15,6 @@
 HBM = pl.BlockSpec(memory_space=pltpu.HBM)
 SMEM = pl.BlockSpec(memory_space=pltpu.SMEM)
 F32, BF16 = jnp.float32, jnp.bfloat16
-PAIRS = 96
-UNROLL = 4
-PHASES = 4
-COUNT_AT = 112
-EMPTY = 160
 STEP = 8
 GRADS = HID + 16
 PACK = TGT + 16
@@ -52,69 +47,49 @@
     return lax.all_to_all(value, axis, 0, 0, axis_index_groups=groups, tiled=True)
 
 
-def pair_of(pairs, edges, n):
-    word = pairs[n]
-    both = jnp.concatenate([edges[word & 255], edges[(word >> 8) & 255]], axis=1)
-    return both, (word >> 16) & 15, (word >> 20) & 15, word >> 24
-
-
-def forward_kernel(ids, mask, *refs):
-    pieces, (kept, pairs), outs = refs[:DOM], refs[DOM : DOM + 2], refs[DOM + 2 : DOM + 9]
-    sources, totals, staged, edges, waiting, mask_sems, kept_sems = refs[DOM + 9 :]
-    steps = mask.shape[0] // STEP
-
+def stream(ids, mask, numbers, staged, mask_sems, id_sem):
     def mask_copy(i):
         at = pl.ds(i * STEP, STEP)
         return pltpu.make_async_copy(mask.at[at], staged.at[at], mask_sems.at[i])
 
-    def kept_copy(i):
-        at = pl.ds(i * STEP, STEP)
-        return pltpu.make_async_copy(edges.at[at], kept.at[at], kept_sems.at[i])
-
-    for i in range(steps):
+    id_copy = pltpu.make_async_copy(ids, numbers, id_sem.at[0])
+    id_copy.start()
+    for i in range(mask.shape[0] // STEP):
         mask_copy(i).start()
+    return id_copy.wait, lambda i: mask_copy(i).wait()
+
+
+def stream_scratch(tile_mask):
+    return [
+        pltpu.SMEM((tile_mask.shape[0],), jnp.int32),
+        pltpu.VMEM(tile_mask.shape, jnp.int32),
+        pltpu.SemaphoreType.DMA((tile_mask.shape[0] // STEP,)),
+        pltpu.SemaphoreType.DMA((1,)),
+    ]
+
+
+def forward_kernel(ids, mask, *refs):
+    pieces, outs = refs[:DOM], refs[DOM : DOM + 7]
+    sources, totals, numbers, staged, mask_sems, id_sem = refs[DOM + 7 :]
+    wait_numbers, wait_tiles = stream(ids, mask, numbers, staged, mask_sems, id_sem)
     my_dom = lax.axis_index("dom")
     for k in range(DOM):
         at = my_dom ^ k
         sources[2 * at] = pieces[k][0:BLK, :]
         sources[2 * at + 1] = pieces[k][BLK:, :]
     totals[...] = jnp.zeros_like(totals)
-    edges[EMPTY:, :, :] = jnp.zeros((STEP, BLK, BLK), BF16)
-    kept_copy(steps).start()
-    for r in range(COL):
-        waiting[r] = -1
-
-    def step(i, n):
-        mask_copy(i).wait()
+    wait_numbers()
+
+    def step(i, carry):
+        wait_tiles(i)
         for u in range(STEP):
             t = i * STEP + u
-            r, c = ids[t] >> 4, ids[t] & 15
+            r, c = numbers[t] >> 4, numbers[t] & 15
             tile = staged[t].astype(F32).astype(BF16)
-            edges[t] = tile
             totals[r] = totals[r] + jnp.dot(tile, sources[c], preferred_element_type=F32)
-            first = waiting[r]
-            paired = first >= 0
-            pairs[n] = (first & 255) | (t << 8) | ((first >> 8) << 16) | (c << 20) | (r << 24)
-            waiting[r] = jnp.where(paired, -1, t | (c << 8))
-            n = n + jnp.where(paired, 1, 0)
-        kept_copy(i).start()
-        return n
-
-    n = 0
-    for phase in range(PHASES):
-        n = lax.fori_loop(phase * steps // PHASES, (phase + 1) * steps // PHASES, step, n)
-        pairs[COUNT_AT + phase] = n // UNROLL
-    for r in range(COL):
-        first = waiting[r]
-        pairs[n] = (first & 255) | (EMPTY << 8) | ((first >> 8) << 16) | (r << 24)
-        n = n + jnp.where(first >= 0, 1, 0)
-
-    def fill(at, carry):
-        pairs[at] = EMPTY | (EMPTY << 8)
         return carry
 
-    lax.fori_loop(n, PAIRS, fill, 0)
-    pairs[COUNT_AT + PHASES] = (n + UNROLL - 1) // UNROLL
+    lax.fori_loop(0, mask.shape[0] // STEP, step, 0)
     y = lax.axis_index("col") >> 3
     half = NZ // 2
     own, far_up, far_down, up_low, up_high, down_low, down_high = outs
@@ -129,32 +104,23 @@
     ):
         for z in range(count):
             out[z] = totals[((y + step_to) & 3) * NZ + first + z].astype(BF16)
-    for i in range(steps + 1):
-        kept_copy(i).wait()
 
 
 def forward(ids, tile_mask, pieces):
     tiles = tile_mask.shape[0]
-    steps = tiles // STEP
     return pl.pallas_call(
         forward_kernel,
-        out_shape=[sds((tiles + STEP, BLK, BLK), BF16), sds((BLK,), jnp.int32)]
-        + [sds((NZ, BLK, F), BF16)]
-        + [sds((NZ // 2, BLK, F), BF16)] * 6,
-        in_specs=[SMEM, HBM] + [VMEM] * DOM,
-        out_specs=[HBM, SMEM] + [VMEM] * 7,
+        out_shape=[sds((NZ, BLK, F), BF16)] + [sds((NZ // 2, BLK, F), BF16)] * 6,
+        in_specs=[HBM, HBM] + [VMEM] * DOM,
+        out_specs=[VMEM] * 7,
         scratch_shapes=[
             pltpu.VMEM((DOM * 2, BLK, F), BF16),
             pltpu.VMEM((COL, BLK, F), F32),
-            pltpu.VMEM(tile_mask.shape, jnp.int32),
-            pltpu.VMEM((tiles + STEP, BLK, BLK), BF16),
-            pltpu.SMEM((COL,), jnp.int32),
-            pltpu.SemaphoreType.DMA((steps,)),
-            pltpu.SemaphoreType.DMA((steps + 1,)),
-        ],
+        ]
+        + stream_scratch(tile_mask),
         compiler_params=pltpu.CompilerParams(vmem_limit_bytes=52 * 1024 * 1024),
         cost_estimate=pl.CostEstimate(
-            flops=2 * tiles * BLK**3, bytes_accessed=tiles * BLK * BLK * 6, transcendentals=0
+            flops=2 * tiles * BLK**3, bytes_accessed=tiles * BLK * BLK * 4, transcendentals=0
         ),
     )(ids, tile_mask, *pieces)
 
@@ -287,38 +253,26 @@
     return jnp.concatenate([rows[0:1] + rows[2:3], rows[1:2] + rows[3:4]], axis=1)
 
 
-def backward_kernel(pairs, kept, packed, bias, own, other, edges, returned, totals, sems):
+def backward_kernel(ids, mask, packed, bias, own, other, returned, totals, *work):
+    numbers, staged = work[:2]
+    wait_numbers, wait_tiles = stream(ids, mask, *work)
     my_core = lax.axis_index("dom") & 1
-    last = kept.shape[0] // STEP - 1
-
-    def kept_copy(i):
-        at = pl.ds(i * STEP, STEP)
-        return pltpu.make_async_copy(kept.at[at], edges.at[at], sems.at[i])
-
-    for i in range(last + 1):
-        kept_copy(i).start()
     for ref in (own, other):
         ref[NX * 256 :, :] = bias_rows(bias[...])
     unpack(packed, returned)
     totals[...] = jnp.zeros_like(totals)
-
-    def step(g, carry):
-        for u in range(UNROLL):
-            both, c1, c2, r = pair_of(pairs, edges, g * UNROLL + u)
-            product = jnp.dot(returned[r], both, preferred_element_type=F32)
-            totals[c1] = totals[c1] + product[:, :BLK]
-            totals[c2] = totals[c2] + product[:, BLK:]
+    wait_numbers()
+
+    def step(i, carry):
+        wait_tiles(i)
+        for u in range(STEP):
+            t = i * STEP + u
+            r, c = numbers[t] >> 4, numbers[t] & 15
+            tile = staged[t].astype(F32).astype(BF16)
+            totals[c] = totals[c] + jnp.dot(returned[r], tile, preferred_element_type=F32)
         return carry
 
-    done = 0
-    for phase in range(PHASES):
-        for i in range(phase * last // PHASES, (phase + 1) * last // PHASES):
-            kept_copy(i).wait()
-        until = pairs[COUNT_AT + phase]
-        lax.fori_loop(done, until, step, 0)
-        done = until
-    kept_copy(last).wait()
-    lax.fori_loop(done, pairs[COUNT_AT + PHASES], step, 0)
+    lax.fori_loop(0, mask.shape[0] // STEP, step, 0)
     for x in range(NX):
         for half in range(2):
             rows_at = pl.ds(x * 256 + half * BLK, BLK)
@@ -374,9 +328,8 @@
     along_x = [scaled] + [exchange_dom(scaled, NCORE * k) for k in range(1, NX)]
     pieces = [piece for held in along_x for piece in (held, exchange_dom(held, 1))]
     products = 2 * tile_mask.shape[0] * BLK**3
-    kept, pairs, own, far_up, far_down, up_low, up_high, down_low, down_high = forward(
-        tile_rows * 16 + tile_cols, tile_mask, pieces
-    )
+    ids = tile_rows * 16 + tile_cols
+    own, far_up, far_down, up_low, up_high, down_low, down_high = forward(ids, tile_mask, pieces)
     far_up, far_down = step_y(far_up, 1), step_y(far_down, -1)
     high_below, low_above = step_y(up_high, 1), step_y(down_low, -1)
     up, down = call(relay_kernel, [sds((NZ // 2, BLK, F), BF16)] * 2, [VMEM] * 4)(
@@ -407,16 +360,12 @@
     own, other = call(
         backward_kernel,
         [sds((NX * 256 + 16, F), BF16)] * 2,
-        [SMEM, HBM, VMEM, VMEM],
-        [
-            pltpu.VMEM(kept.shape, BF16),
-            pltpu.VMEM((COL, F, BLK), BF16),
-            pltpu.VMEM((DOM * 2, F, BLK), F32),
-            pltpu.SemaphoreType.DMA((kept.shape[0] // STEP,)),
-        ],
+        [HBM, HBM, VMEM, VMEM],
+        [pltpu.VMEM((COL, F, BLK), BF16), pltpu.VMEM((DOM * 2, F, BLK), F32)]
+        + stream_scratch(tile_mask),
         flops=products,
         limit=52,
-    )(pairs, kept, gathered, bias_sum)
+    )(ids, tile_mask, gathered, bias_sum)
     got = exchange_dom(other, 1)
     grads_got = exchange_dom(grads, 1)
     (by_x,) = call(core_sum_kernel, [sds((NX, 256 + GRADS, F), BF16)], [VMEM] * 4)(

time: 102 us -> 100 us (0.980)
  Pallas kernels: 18.5 us -> 15.2 us
  starting transfers between devices: 31.2 us -> 32.7 us
    pallas_call x2, Pallas kernels: 15.8 us -> 12.5 us  [the longest x1 6.46 us: body(): call(backward_kernel, [sds((NX * 256 + 16, F), BF16)] * 2, [HBM, HBM, VME...]
    ppermute x9, starting transfers between devices: 18.9 us -> 20.4 us  [exchange_dom(): return lax.ppermute(value, 'dom', pairs)]
  transfers between devices with their start and end apart: 16 -> 16, of which waited for: 5 -> 5; matrix products, arithmetic and copies ran while one was open for 1% -> 1% of each run, Pallas kernels for 8% -> 7%
where the time goes in v4:
time: 100 us; the launch traced here: 99.7 us
  blocking collectives  43.1 us (43%)
  starting transfers between devices  32.7 us (33%)
  Pallas kernels  15.2 us (15%)
  waiting for transfers between devices  6.29 us (6%)
  other arithmetic  1.68 us (2%)
    all_to_all x3, blocking collectives, swap(): lax.all_to_all(value, axis, 0, 0, axis_index_groups=groups, tiled=True)  43.1 us
    ppermute x9, starting transfers between devices, exchange_dom(): return lax.ppermute(value, 'dom', pairs)  20.4 us
    ppermute x6, starting transfers between devices, step_y(): return lax.ppermute(value, 'col', pairs)  7.12 us
    pallas_call x1, Pallas kernels, body(): call(backward_kernel, [sds((NX * 256 + 16, F), BF16)] * 2, [HBM, HBM, VME...  6.46 us
    pallas_call x1, Pallas kernels, forward(): pl.pallas_call(forward_kernel, out_shape=[sds((NZ, BLK, F), BF16)] + [sds...  6.06 us
    all_to_all x1, starting transfers between devices, swap(): lax.all_to_all(value, axis, 0, 0, axis_index_groups=groups, tiled=True)  5.22 us
    ppermute x6, waiting for transfers between devices, step_y(): return lax.ppermute(value, 'col', pairs)  4.99 us
  transfers between devices with their start and end apart: 16, of which 5 were waited for; matrix products, arithmetic and copies ran while one was open for 1% of the time, Pallas kernels for 7%

profile of v4, /device:TPU:1, one launch (start us, length us, event | category | flops | bytes accessed | tf_op | source)
XLA Modules:
  0.0 99.7 jit_solution(8463416001649470483)
XLA Ops:
  0.7 1.0 multiply_convert_fusion.refs_0_
  1.7 3.4 %collective-permute-start.5 = (bf16[256,128]{1,0:T(8,128)(2,1)S(1)}, bf16[256,128]{1,0:T(8,128)(2,1)S(1)}, u32[]{:S(2)}, u32[]{:S(2)}) collective-permute-start(bf16[256,128]{1,0:T(8,128)(2,1)S(1)} %multiply_convert_fusion.refs_0_), channel_id=1, source_target_pairs={{0,6},{1,7},{2,4},{3,5},{4,2},{5,3},{6,0},{7,1},{8,14},{9,15},{10,... | collective-permute-start | bytes 196616 | tf_op jit(solution)/shard_map/ppermute | solution.py:43
  5.1 0.5 collective-permute-start.3
  5.6 0.2 collective-permute-start.1
  5.7 3.3 %collective-permute-start = (bf16[256,128]{1,0:T(8,128)(2,1)S(1)}, bf16[256,128]{1,0:T(8,128)(2,1)S(1)}, u32[]{:S(2)}, u32[]{:S(2)}) collective-permute-start(bf16[256,128]{1,0:T(8,128)(2,1)S(1)} %multiply_convert_fusion.refs_0_), channel_id=1, source_target_pairs={{0,1},{1,0},{2,3},{3,2},{4,5},{5,4},{6,7},{7,6},{8,9},{9,8},{10,11... | collective-permute-start | bytes 196616 | tf_op jit(solution)/shard_map/ppermute | solution.py:43
  9.1 2.0 %collective-permute-start.6 = (bf16[256,128]{1,0:T(8,128)(2,1)S(1)}, bf16[256,128]{1,0:T(8,128)(2,1)S(1)}, u32[]{:S(2)}, u32[]{:S(2)}) collective-permute-start(bf16[256,128]{1,0:T(8,128)(2,1)S(1)} %collective-permute-done.5.refs_6_), channel_id=1, source_target_pairs={{0,1},{1,0},{2,3},{3,2},{4,5},{5,4},{6,7},{7,6},{8,9},{9,8},{10,11... | collective-permute-start | bytes 196616 | tf_op jit(solution)/shard_map/ppermute | solution.py:43
  11.1 0.7 collective-permute-start.4
  11.8 0.2 collective-permute-start.2
  12.0 0.7 multiply_add_fusion.ids
  12.8 0.3 collective-permute-done.2.refs_3_
  13.1 6.1 %shard_map.129 = (bf16[8,128,128]{2,1,0:T(8,128)(2,1)S(1)}, bf16[4,128,128]{2,1,0:T(8,128)(2,1)S(1)}, bf16[4,128,128]{2,1,0:T(8,128)(2,1)S(1)}, bf16[4,128,128]{...) custom-call(s32[160]{0:T(256)S(1)} %multiply_add_fusion.ids, ...), custom_call_target="tpu_custom_call" | custom-call | flops 671088640 | bytes 10485760 | tf_op jit(solution)/shard_map/pallas_call | solution.py:111
  19.1 1.4 %collective-permute-start.8 = (bf16[4,128,128]{2,1,0:T(8,128)(2,1)S(1)}, bf16[4,128,128]{2,1,0:T(8,128)(2,1)S(1)}, u32[]{:S(2)}, u32[]{:S(2)}) collective-permute-start(bf16[4,128,128]{2,1,0:T(8,128)(2,1)S(1)} %get-tuple-element.25), channel_id=1, source_target_pairs={{0,64},{8,72},{16,80},{24,88},{32,96},{40,104},{48,112},{56,120},{... | collective-permute-start | bytes 393224 | tf_op jit(solution)/shard_map/ppermute | solution.py:153
  20.5 1.5 %collective-permute-start.9 = (bf16[4,128,128]{2,1,0:T(8,128)(2,1)S(1)}, bf16[4,128,128]{2,1,0:T(8,128)(2,1)S(1)}, u32[]{:S(2)}, u32[]{:S(2)}) collective-permute-start(bf16[4,128,128]{2,1,0:T(8,128)(2,1)S(1)} %get-tuple-element.27), channel_id=1, source_target_pairs={{0,192},{8,200},{16,208},{24,216},{32,224},{40,232},{48,240},{56,2... | collective-permute-start | bytes 393224 | tf_op jit(solution)/shard_map/ppermute | solution.py:153
  22.0 1.4 %collective-permute-start.7 = (bf16[4,128,128]{2,1,0:T(8,128)(2,1)S(1)}, bf16[4,128,128]{2,1,0:T(8,128)(2,1)S(1)}, u32[]{:S(2)}, u32[]{:S(2)}) collective-permute-start(bf16[4,128,128]{2,1,0:T(8,128)(2,1)S(1)} %get-tuple-element.23), channel_id=1, source_target_pairs={{0,192},{8,200},{16,208},{24,216},{32,224},{40,232},{48,240},{56,2... | collective-permute-start | bytes 393224 | tf_op jit(solution)/shard_map/ppermute | solution.py:153
  23.4 0.1 collective-permute-start.11
  23.5 1.9 %collective-permute-done.8.far_up = bf16[4,128,128]{2,1,0:T(8,128)(2,1)S(1)} collective-permute-done((bf16[4,128,128]{2,1,0:T(8,128)(2,1)S(1)}, bf16[4,128,128]{2,1,0:T(8,128)(2,1)S(1)}, u32[]{:S(2)}, u32[]{:S(2)}) %collective-permute-start.8) | collective-permute-done | bytes 131104 | tf_op jit(solution)/shard_map/ppermute | solution.py:153
  25.5 1.1 %collective-permute-start.10 = (bf16[4,128,128]{2,1,0:T(8,128)(2,1)S(1)}, bf16[4,128,128]{2,1,0:T(8,128)(2,1)S(1)}, u32[]{:S(2)}, u32[]{:S(2)}) collective-permute-start(bf16[4,128,128]{2,1,0:T(8,128)(2,1)S(1)} %get-tuple-element.28), channel_id=1, source_target_pairs={{0,64},{8,72},{16,80},{24,88},{32,96},{40,104},{48,112},{56,120},{... | collective-permute-start | bytes 393224 | tf_op jit(solution)/shard_map/ppermute | solution.py:153
  26.6 1.7 %collective-permute-start.12 = (bf16[4,128,128]{2,1,0:T(8,128)(2,1)S(1)}, bf16[4,128,128]{2,1,0:T(8,128)(2,1)S(1)}, u32[]{:S(2)}, u32[]{:S(2)}) collective-permute-start(bf16[4,128,128]{2,1,0:T(8,128)(2,1)S(1)} %get-tuple-element.30), channel_id=1, source_target_pairs={{0,192},{8,200},{16,208},{24,216},{32,224},{40,232},{48,240},{56,2... | collective-permute-start | bytes 393224 | tf_op jit(solution)/shard_map/ppermute | solution.py:153
  28.2 0.2 collective-permute-done.11.high_below
  28.4 2.9 %collective-permute-done.10.low_below = bf16[4,128,128]{2,1,0:T(8,128)(2,1)S(1)} collective-permute-done((bf16[4,128,128]{2,1,0:T(8,128)(2,1)S(1)}, bf16[4,128,128]{2,1,0:T(8,128)(2,1)S(1)}, u32[]{:S(2)}, u32[]{:S(2)}) %collective-permute-start.10) | collective-permute-done | bytes 131104 | tf_op jit(solution)/shard_map/ppermute | solution.py:153
  31.3 0.1 shard_map.131
  31.4 17.4 %all_to_all.20.parts = bf16[8,128,128]{2,1,0:T(8,128)(2,1)S(1)} all-to-all(bf16[8,128,128]{2,1,0:T(8,128)(2,1)S(1)} %shard_map.131), channel_id=1, replica_groups={{0,8,16,24,32,40,48,56},{64,72,80,88,96,104,112,120},{128,136,144,152,1..., dimensions={0} | all-to-all | bytes 524288 | tf_op jit(solution)/shard_map/all_to_all | solution.py:47
  48.8 1.0 shard_map.132
  49.8 13.9 %all_to_all.21.packed = bf16[32,48,128]{2,1,0:T(8,128)(2,1)S(1)} all-to-all(bf16[32,48,128]{2,1,0:T(8,128)(2,1)S(1)} %get-tuple-element.32), channel_id=1, replica_groups=mesh['col'=32,'dom'=8] {'col'}, dimensions={0} | all-to-all | bytes 786432 | tf_op jit(solution)/shard_map/all_to_all | solution.py:47
  63.7 0.7 shard_map.133
  64.4 5.2 %all-to-all-start.2 = ((f32[32,8,128]{2,1,0:T(8,128)}), f32[32,8,128]{2,1,0:T(8,128)S(1)}, u32[]{:S(2)}, u32[]{:S(2)}) async-start(f32[32,8,128]{2,1,0:T(8,128)} %get-tuple-element.36), calls=%async_computation.2 | async-start | bytes 262144 | tf_op jit(solution)/shard_map/all_to_all | solution.py:47
  69.7 6.5 %shard_map.134 = (bf16[1040,128]{1,0:T(8,128)(2,1)S(1)}, bf16[1040,128]{1,0:T(8,128)(2,1)S(1)}) custom-call(s32[160]{0:T(256)S(1)} %multiply_add_fusion.ids, s32[160,128,128]{2,1,0:T(8,128)} %mask.3, bf16[32,48,128]{2,1,0:T(8,128)(2,1)S(1)} %all_to_all.21.packed, f32[1,256]{1,0:T(1,128)S(1)} %get-tuple-element.33.bias), custom_call_target="tpu_custom_call" | custom-call | flops 671088640 | tf_op jit(solution)/shard_map/pallas_call | solution.py:360
  76.1 6.3 %collective-permute-start.13 = (bf16[1040,128]{1,0:T(8,128)(2,1)S(1)}, bf16[1040,128]{1,0:T(8,128)(2,1)S(1)}, u32[]{:S(2)}, u32[]{:S(2)}) collective-permute-start(bf16[1040,128]{1,0:T(8,128)(2,1)S(1)} %get-tuple-element.35), channel_id=1, source_target_pairs={{0,1},{1,0},{2,3},{3,2},{4,5},{5,4},{6,7},{7,6},{8,9},{9,8},{10,11... | collective-permute-start | bytes 798728 | tf_op jit(solution)/shard_map/ppermute | solution.py:43
  82.4 3.7 %collective-permute-start.14 = (f32[32,8,128]{2,1,0:T(8,128)S(1)}, f32[32,8,128]{2,1,0:T(8,128)S(1)}, u32[]{:S(2)}, u32[]{:S(2)}) collective-permute-start(f32[32,8,128]{2,1,0:T(8,128)S(1)} %all-to-all-done.2.grads), channel_id=1, source_target_pairs={{0,1},{1,0},{2,3},{3,2},{4,5},{5,4},{6,7},{7,6},{8,9},{9,8},{10,11... | collective-permute-start | bytes 393224 | tf_op jit(solution)/shard_map/ppermute | solution.py:43
  86.2 1.0 collective-permute-done.14.grads_got
  87.2 11.8 %all_to_all.22.parts = bf16[4,528,128]{2,1,0:T(8,128)(2,1)S(1)} all-to-all(bf16[4,528,128]{2,1,0:T(8,128)(2,1)S(1)} %shard_map.135), channel_id=1, replica_groups={{0,2,4,6},{1,3,5,7},{8,10,12,14},{9,11,13,15},{16,18,20,22},{17,19,21,2..., dimensions={0} | all-to-all | bytes 1081344 | tf_op jit(solution)/shard_map/all_to_all | solution.py:47
  99.0 0.8 shard_map.136
  (25 shorter events, 0.2 us)
Async XLA Ops:
  0.6 48.2 %copy-start.1 = (bf16[32,256]{1,0:T(8,128)(2,1)S(1)}, bf16[32,256]{1,0:T(8,128)(2,1)}, u32[]{:S(2)}) copy-start(bf16[32,256]{1,0:T(8,128)(2,1)} %upstream.1) | copy-start | bytes 49156
  0.6 48.2 %copy-start.5 = (s32[32]{0:T(128)S(1)}, s32[32]{0:T(128)}, u32[]{:S(2)}) copy-start(s32[32]{0:T(128)} %param.18) | copy-start | bytes 388
  0.7 48.1 %copy-start.3 = (f32[256]{0:T(256)S(1)}, f32[256]{0:T(256)}, u32[]{:S(2)}) copy-start(f32[256]{0:T(256)} %param.14) | copy-start | bytes 3076
  0.7 48.1 %copy-start = (bf16[128,256]{1,0:T(8,128)(2,1)S(1)}, bf16[128,256]{1,0:T(8,128)(2,1)}, u32[]{:S(2)}) copy-start(bf16[128,256]{1,0:T(8,128)(2,1)} %weight.1) | copy-start | bytes 196612
  0.7 48.1 %copy-start.4 = (f32[128]{0:T(128)S(1)}, f32[128]{0:T(128)}, u32[]{:S(2)}) copy-start(f32[128]{0:T(128)} %param.12) | copy-start | bytes 1540
  1.7 7.4 %collective-permute-start.5 = (bf16[256,128]{1,0:T(8,128)(2,1)S(1)}, bf16[256,128]{1,0:T(8,128)(2,1)S(1)}, u32[]{:S(2)}, u32[]{:S(2)}) collective-permute-start(bf16[256,128]{1,0:T(8,128)(2,1)S(1)} %multiply_convert_fusion.refs_0_), channel_id=1, source_target_pairs={{0,6},{1,7},{2,4},{3,5},{4,2},{5,3},{6,0},{7,1},{8,14},{9,15},{10,... | collective-permute-start | bytes 196616 | tf_op jit(solution)/shard_map/ppermute | solution.py:43
  5.1 6.0 %collective-permute-start.3 = (bf16[256,128]{1,0:T(8,128)(2,1)S(1)}, bf16[256,128]{1,0:T(8,128)(2,1)S(1)}, u32[]{:S(2)}, u32[]{:S(2)}) collective-permute-start(bf16[256,128]{1,0:T(8,128)(2,1)S(1)} %multiply_convert_fusion.refs_0_), channel_id=1, source_target_pairs={{0,4},{1,5},{2,6},{3,7},{4,0},{5,1},{6,2},{7,3},{8,12},{9,13},{10,... | collective-permute-start | bytes 196616 | tf_op jit(solution)/shard_map/ppermute | solution.py:43
  5.6 6.2 %collective-permute-start.1 = (bf16[256,128]{1,0:T(8,128)(2,1)S(1)}, bf16[256,128]{1,0:T(8,128)(2,1)S(1)}, u32[]{:S(2)}, u32[]{:S(2)}) collective-permute-start(bf16[256,128]{1,0:T(8,128)(2,1)S(1)} %multiply_convert_fusion.refs_0_), channel_id=1, source_target_pairs={{0,2},{1,3},{2,0},{3,1},{4,6},{5,7},{6,4},{7,5},{8,10},{9,11},{10,... | collective-permute-start | bytes 196616 | tf_op jit(solution)/shard_map/ppermute | solution.py:43
  5.7 7.0 %collective-permute-start = (bf16[256,128]{1,0:T(8,128)(2,1)S(1)}, bf16[256,128]{1,0:T(8,128)(2,1)S(1)}, u32[]{:S(2)}, u32[]{:S(2)}) collective-permute-start(bf16[256,128]{1,0:T(8,128)(2,1)S(1)} %multiply_convert_fusion.refs_0_), channel_id=1, source_target_pairs={{0,1},{1,0},{2,3},{3,2},{4,5},{5,4},{6,7},{7,6},{8,9},{9,8},{10,11... | collective-permute-start | bytes 196616 | tf_op jit(solution)/shard_map/ppermute | solution.py:43
  9.1 3.6 %collective-permute-start.6 = (bf16[256,128]{1,0:T(8,128)(2,1)S(1)}, bf16[256,128]{1,0:T(8,128)(2,1)S(1)}, u32[]{:S(2)}, u32[]{:S(2)}) collective-permute-start(bf16[256,128]{1,0:T(8,128)(2,1)S(1)} %collective-permute-done.5.refs_6_), channel_id=1, source_target_pairs={{0,1},{1,0},{2,3},{3,2},{4,5},{5,4},{6,7},{7,6},{8,9},{9,8},{10,11... | collective-permute-start | bytes 196616 | tf_op jit(solution)/shard_map/ppermute | solution.py:43
  11.1 1.7 %collective-permute-start.4 = (bf16[256,128]{1,0:T(8,128)(2,1)S(1)}, bf16[256,128]{1,0:T(8,128)(2,1)S(1)}, u32[]{:S(2)}, u32[]{:S(2)}) collective-permute-start(bf16[256,128]{1,0:T(8,128)(2,1)S(1)} %collective-permute-done.3.refs_4_), channel_id=1, source_target_pairs={{0,1},{1,0},{2,3},{3,2},{4,5},{5,4},{6,7},{7,6},{8,9},{9,8},{10,11... | collective-permute-start | bytes 196616 | tf_op jit(solution)/shard_map/ppermute | solution.py:43
  11.8 1.3 %collective-permute-start.2 = (bf16[256,128]{1,0:T(8,128)(2,1)S(1)}, bf16[256,128]{1,0:T(8,128)(2,1)S(1)}, u32[]{:S(2)}, u32[]{:S(2)}) collective-permute-start(bf16[256,128]{1,0:T(8,128)(2,1)S(1)} %collective-permute-done.1.refs_2_), channel_id=1, source_target_pairs={{0,1},{1,0},{2,3},{3,2},{4,5},{5,4},{6,7},{7,6},{8,9},{9,8},{10,11... | collective-permute-start | bytes 196616 | tf_op jit(solution)/shard_map/ppermute | solution.py:43
  19.1 79.9 %copy-start.2 = (f32[256]{0:T(256)S(1)}, f32[256]{0:T(256)}, u32[]{:S(2)}) copy-start(f32[256]{0:T(256)} %param.11) | copy-start | bytes 3076
  19.1 6.3 %collective-permute-start.8 = (bf16[4,128,128]{2,1,0:T(8,128)(2,1)S(1)}, bf16[4,128,128]{2,1,0:T(8,128)(2,1)S(1)}, u32[]{:S(2)}, u32[]{:S(2)}) collective-permute-start(bf16[4,128,128]{2,1,0:T(8,128)(2,1)S(1)} %get-tuple-element.25), channel_id=1, source_target_pairs={{0,64},{8,72},{16,80},{24,88},{32,96},{40,104},{48,112},{56,120},{... | collective-permute-start | bytes 393224 | tf_op jit(solution)/shard_map/ppermute | solution.py:153
  20.5 4.9 %collective-permute-start.9 = (bf16[4,128,128]{2,1,0:T(8,128)(2,1)S(1)}, bf16[4,128,128]{2,1,0:T(8,128)(2,1)S(1)}, u32[]{:S(2)}, u32[]{:S(2)}) collective-permute-start(bf16[4,128,128]{2,1,0:T(8,128)(2,1)S(1)} %get-tuple-element.27), channel_id=1, source_target_pairs={{0,192},{8,200},{16,208},{24,216},{32,224},{40,232},{48,240},{56,2... | collective-permute-start | bytes 393224 | tf_op jit(solution)/shard_map/ppermute | solution.py:153
  22.0 6.2 %collective-permute-start.7 = (bf16[4,128,128]{2,1,0:T(8,128)(2,1)S(1)}, bf16[4,128,128]{2,1,0:T(8,128)(2,1)S(1)}, u32[]{:S(2)}, u32[]{:S(2)}) collective-permute-start(bf16[4,128,128]{2,1,0:T(8,128)(2,1)S(1)} %get-tuple-element.23), channel_id=1, source_target_pairs={{0,192},{8,200},{16,208},{24,216},{32,224},{40,232},{48,240},{56,2... | collective-permute-start | bytes 393224 | tf_op jit(solution)/shard_map/ppermute | solution.py:153
  23.4 5.0 %collective-permute-start.11 = (bf16[4,128,128]{2,1,0:T(8,128)(2,1)S(1)}, bf16[4,128,128]{2,1,0:T(8,128)(2,1)S(1)}, u32[]{:S(2)}, u32[]{:S(2)}) collective-permute-start(bf16[4,128,128]{2,1,0:T(8,128)(2,1)S(1)} %get-tuple-element.29), channel_id=1, source_target_pairs={{0,64},{8,72},{16,80},{24,88},{32,96},{40,104},{48,112},{56,120},{... | collective-permute-start | bytes 393224 | tf_op jit(solution)/shard_map/ppermute | solution.py:153
  25.5 5.8 %collective-permute-start.10 = (bf16[4,128,128]{2,1,0:T(8,128)(2,1)S(1)}, bf16[4,128,128]{2,1,0:T(8,128)(2,1)S(1)}, u32[]{:S(2)}, u32[]{:S(2)}) collective-permute-start(bf16[4,128,128]{2,1,0:T(8,128)(2,1)S(1)} %get-tuple-element.28), channel_id=1, source_target_pairs={{0,64},{8,72},{16,80},{24,88},{32,96},{40,104},{48,112},{56,120},{... | collective-permute-start | bytes 393224 | tf_op jit(solution)/shard_map/ppermute | solution.py:153
  26.6 4.7 %collective-permute-start.12 = (bf16[4,128,128]{2,1,0:T(8,128)(2,1)S(1)}, bf16[4,128,128]{2,1,0:T(8,128)(2,1)S(1)}, u32[]{:S(2)}, u32[]{:S(2)}) collective-permute-start(bf16[4,128,128]{2,1,0:T(8,128)(2,1)S(1)} %get-tuple-element.30), channel_id=1, source_target_pairs={{0,192},{8,200},{16,208},{24,216},{32,224},{40,232},{48,240},{56,2... | collective-permute-start | bytes 393224 | tf_op jit(solution)/shard_map/ppermute | solution.py:153
  64.4 18.0 %all-to-all-start.2 = ((f32[32,8,128]{2,1,0:T(8,128)}), f32[32,8,128]{2,1,0:T(8,128)S(1)}, u32[]{:S(2)}, u32[]{:S(2)}) async-start(f32[32,8,128]{2,1,0:T(8,128)} %get-tuple-element.36), calls=%async_computation.2 | async-start | bytes 262144 | tf_op jit(solution)/shard_map/all_to_all | solution.py:47
  76.1 10.0 %collective-permute-start.13 = (bf16[1040,128]{1,0:T(8,128)(2,1)S(1)}, bf16[1040,128]{1,0:T(8,128)(2,1)S(1)}, u32[]{:S(2)}, u32[]{:S(2)}) collective-permute-start(bf16[1040,128]{1,0:T(8,128)(2,1)S(1)} %get-tuple-element.35), channel_id=1, source_target_pairs={{0,1},{1,0},{2,3},{3,2},{4,5},{5,4},{6,7},{7,6},{8,9},{9,8},{10,11... | collective-permute-start | bytes 798728 | tf_op jit(solution)/shard_map/ppermute | solution.py:43
  82.4 4.7 %collective-permute-start.14 = (f32[32,8,128]{2,1,0:T(8,128)S(1)}, f32[32,8,128]{2,1,0:T(8,128)S(1)}, u32[]{:S(2)}, u32[]{:S(2)}) collective-permute-start(f32[32,8,128]{2,1,0:T(8,128)S(1)} %all-to-all-done.2.grads), channel_id=1, source_target_pairs={{0,1},{1,0},{2,3},{3,2},{4,5},{5,4},{6,7},{7,6},{8,9},{9,8},{10,11... | collective-permute-start | bytes 393224 | tf_op jit(solution)/shard_map/ppermute | solution.py:43

commit v5 on v4

--- a/solution.py
+++ b/solution.py
@@ -15,7 +15,7 @@
 HBM = pl.BlockSpec(memory_space=pltpu.HBM)
 SMEM = pl.BlockSpec(memory_space=pltpu.SMEM)
 F32, BF16 = jnp.float32, jnp.bfloat16
-STEP = 8
+STEP = 16
 GRADS = HID + 16
 PACK = TGT + 16
 Z_GROUPS = [[y * NZ + z for z in range(NZ)] for y in range(NY)]

time: 100 us -> 98.6 us (0.986)
  Pallas kernels: 15.2 us -> 12.2 us
  starting transfers between devices: 32.7 us -> 34.2 us
    pallas_call x1, Pallas kernels: 6.46 us -> 4.93 us  [body(): call(backward_kernel, [sds((NX * 256 + 16, F), BF16)] * 2, [HBM, HBM, VME...]
    ppermute x9, starting transfers between devices: 20.4 us -> 21.9 us  [exchange_dom(): return lax.ppermute(value, 'dom', pairs)]
    pallas_call x1, Pallas kernels: 6.06 us -> 4.57 us  [forward(): pl.pallas_call(forward_kernel, out_shape=[sds((NZ, BLK, F), BF16)] + [sds...]
  transfers between devices with their start and end apart: 16 -> 16, of which waited for: 5 -> 5; matrix products, arithmetic and copies ran while one was open for 1% -> 1% of each run, Pallas kernels for 7% -> 5%
where the time goes in v5:
time: 98.6 us; the launch traced here: 98.3 us
  blocking collectives  43.1 us (44%)
  starting transfers between devices  34.2 us (35%)
  Pallas kernels  12.2 us (12%)
  waiting for transfers between devices  6.31 us (6%)
  other arithmetic  1.68 us (2%)
    all_to_all x3, blocking collectives, swap(): lax.all_to_all(value, axis, 0, 0, axis_index_groups=groups, tiled=True)  43.1 us
    ppermute x9, starting transfers between devices, exchange_dom(): return lax.ppermute(value, 'dom', pairs)  21.9 us
    ppermute x6, starting transfers between devices, step_y(): return lax.ppermute(value, 'col', pairs)  7.12 us
    all_to_all x1, starting transfers between devices, swap(): lax.all_to_all(value, axis, 0, 0, axis_index_groups=groups, tiled=True)  5.22 us
    ppermute x6, waiting for transfers between devices, step_y(): return lax.ppermute(value, 'col', pairs)  5.01 us
    pallas_call x1, Pallas kernels, body(): call(backward_kernel, [sds((NX * 256 + 16, F), BF16)] * 2, [HBM, HBM, VME...  4.93 us
    pallas_call x1, Pallas kernels, forward(): pl.pallas_call(forward_kernel, out_shape=[sds((NZ, BLK, F), BF16)] + [sds...  4.57 us
  transfers between devices with their start and end apart: 16, of which 5 were waited for; matrix products, arithmetic and copies ran while one was open for 1% of the time, Pallas kernels for 5%

profile of v5, /device:TPU:1, one launch (start us, length us, event | category | flops | bytes accessed | tf_op | source)
XLA Modules:
  0.0 98.3 jit_solution(8426792906360517295)
XLA Ops:
  0.7 1.0 %multiply_convert_fusion.refs_0_ = bf16[256,128]{1,0:T(8,128)(2,1)S(1)} fusion(bf16[256,128]{1,0:T(8,128)(2,1)} %param.10, f32[256]{0:T(256)} %param.11), kind=kLoop, calls=%fused_computation | loop fusion | flops 98304 | bytes 132096 | tf_op jit(solution)/shard_map/convert_element_type | solution.py:327
  1.7 3.4 %collective-permute-start.5 = (bf16[256,128]{1,0:T(8,128)(2,1)S(1)}, bf16[256,128]{1,0:T(8,128)(2,1)S(1)}, u32[]{:S(2)}, u32[]{:S(2)}) collective-permute-start(bf16[256,128]{1,0:T(8,128)(2,1)S(1)} %multiply_convert_fusion.refs_0_), channel_id=1, source_target_pairs={{0,6},{1,7},{2,4},{3,5},{4,2},{5,3},{6,0},{7,1},{8,14},{9,15},{10,... | collective-permute-start | bytes 196616 | tf_op jit(solution)/shard_map/ppermute | solution.py:43
  5.1 0.5 collective-permute-start.3
  5.6 0.2 collective-permute-start.1
  5.7 3.3 %collective-permute-start = (bf16[256,128]{1,0:T(8,128)(2,1)S(1)}, bf16[256,128]{1,0:T(8,128)(2,1)S(1)}, u32[]{:S(2)}, u32[]{:S(2)}) collective-permute-start(bf16[256,128]{1,0:T(8,128)(2,1)S(1)} %multiply_convert_fusion.refs_0_), channel_id=1, source_target_pairs={{0,1},{1,0},{2,3},{3,2},{4,5},{5,4},{6,7},{7,6},{8,9},{9,8},{10,11... | collective-permute-start | bytes 196616 | tf_op jit(solution)/shard_map/ppermute | solution.py:43
  9.1 2.0 %collective-permute-start.6 = (bf16[256,128]{1,0:T(8,128)(2,1)S(1)}, bf16[256,128]{1,0:T(8,128)(2,1)S(1)}, u32[]{:S(2)}, u32[]{:S(2)}) collective-permute-start(bf16[256,128]{1,0:T(8,128)(2,1)S(1)} %collective-permute-done.5.refs_6_), channel_id=1, source_target_pairs={{0,1},{1,0},{2,3},{3,2},{4,5},{5,4},{6,7},{7,6},{8,9},{9,8},{10,11... | collective-permute-start | bytes 196616 | tf_op jit(solution)/shard_map/ppermute | solution.py:43
  11.1 0.7 collective-permute-start.4
  11.8 0.2 collective-permute-start.2
  12.0 0.7 multiply_add_fusion.ids
  12.8 0.3 collective-permute-done.2.refs_3_
  13.1 4.6 %shard_map.129 = (bf16[8,128,128]{2,1,0:T(8,128)(2,1)S(1)}, bf16[4,128,128]{2,1,0:T(8,128)(2,1)S(1)}, bf16[4,128,128]{2,1,0:T(8,128)(2,1)S(1)}, bf16[4,128,128]{...) custom-call(s32[160]{0:T(256)S(1)} %multiply_add_fusion.ids, ...), custom_call_target="tpu_custom_call" | custom-call | flops 671088640 | bytes 10485760 | tf_op jit(solution)/shard_map/pallas_call | solution.py:111
  17.6 1.4 %collective-permute-start.8 = (bf16[4,128,128]{2,1,0:T(8,128)(2,1)S(1)}, bf16[4,128,128]{2,1,0:T(8,128)(2,1)S(1)}, u32[]{:S(2)}, u32[]{:S(2)}) collective-permute-start(bf16[4,128,128]{2,1,0:T(8,128)(2,1)S(1)} %get-tuple-element.25), channel_id=1, source_target_pairs={{0,64},{8,72},{16,80},{24,88},{32,96},{40,104},{48,112},{56,120},{... | collective-permute-start | bytes 393224 | tf_op jit(solution)/shard_map/ppermute | solution.py:153
  19.0 1.5 %collective-permute-start.9 = (bf16[4,128,128]{2,1,0:T(8,128)(2,1)S(1)}, bf16[4,128,128]{2,1,0:T(8,128)(2,1)S(1)}, u32[]{:S(2)}, u32[]{:S(2)}) collective-permute-start(bf16[4,128,128]{2,1,0:T(8,128)(2,1)S(1)} %get-tuple-element.27), channel_id=1, source_target_pairs={{0,192},{8,200},{16,208},{24,216},{32,224},{40,232},{48,240},{56,2... | collective-permute-start | bytes 393224 | tf_op jit(solution)/shard_map/ppermute | solution.py:153
  20.5 1.4 %collective-permute-start.7 = (bf16[4,128,128]{2,1,0:T(8,128)(2,1)S(1)}, bf16[4,128,128]{2,1,0:T(8,128)(2,1)S(1)}, u32[]{:S(2)}, u32[]{:S(2)}) collective-permute-start(bf16[4,128,128]{2,1,0:T(8,128)(2,1)S(1)} %get-tuple-element.23), channel_id=1, source_target_pairs={{0,192},{8,200},{16,208},{24,216},{32,224},{40,232},{48,240},{56,2... | collective-permute-start | bytes 393224 | tf_op jit(solution)/shard_map/ppermute | solution.py:153
  21.9 0.1 collective-permute-start.11
  22.0 1.9 %collective-permute-done.8.far_up = bf16[4,128,128]{2,1,0:T(8,128)(2,1)S(1)} collective-permute-done((bf16[4,128,128]{2,1,0:T(8,128)(2,1)S(1)}, bf16[4,128,128]{2,1,0:T(8,128)(2,1)S(1)}, u32[]{:S(2)}, u32[]{:S(2)}) %collective-permute-start.8) | collective-permute-done | bytes 131104 | tf_op jit(solution)/shard_map/ppermute | solution.py:153
  24.0 1.2 %collective-permute-start.10 = (bf16[4,128,128]{2,1,0:T(8,128)(2,1)S(1)}, bf16[4,128,128]{2,1,0:T(8,128)(2,1)S(1)}, u32[]{:S(2)}, u32[]{:S(2)}) collective-permute-start(bf16[4,128,128]{2,1,0:T(8,128)(2,1)S(1)} %get-tuple-element.28), channel_id=1, source_target_pairs={{0,64},{8,72},{16,80},{24,88},{32,96},{40,104},{48,112},{56,120},{... | collective-permute-start | bytes 393224 | tf_op jit(solution)/shard_map/ppermute | solution.py:153
  25.1 1.6 %collective-permute-start.12 = (bf16[4,128,128]{2,1,0:T(8,128)(2,1)S(1)}, bf16[4,128,128]{2,1,0:T(8,128)(2,1)S(1)}, u32[]{:S(2)}, u32[]{:S(2)}) collective-permute-start(bf16[4,128,128]{2,1,0:T(8,128)(2,1)S(1)} %get-tuple-element.30), channel_id=1, source_target_pairs={{0,192},{8,200},{16,208},{24,216},{32,224},{40,232},{48,240},{56,2... | collective-permute-start | bytes 393224 | tf_op jit(solution)/shard_map/ppermute | solution.py:153
  26.7 0.2 collective-permute-done.11.high_below
  26.9 2.9 %collective-permute-done.10.low_below = bf16[4,128,128]{2,1,0:T(8,128)(2,1)S(1)} collective-permute-done((bf16[4,128,128]{2,1,0:T(8,128)(2,1)S(1)}, bf16[4,128,128]{2,1,0:T(8,128)(2,1)S(1)}, u32[]{:S(2)}, u32[]{:S(2)}) %collective-permute-start.10) | collective-permute-done | bytes 131104 | tf_op jit(solution)/shard_map/ppermute | solution.py:153
  29.8 0.1 shard_map.131
  29.9 17.4 %all_to_all.20.parts = bf16[8,128,128]{2,1,0:T(8,128)(2,1)S(1)} all-to-all(bf16[8,128,128]{2,1,0:T(8,128)(2,1)S(1)} %shard_map.131), channel_id=1, replica_groups={{0,8,16,24,32,40,48,56},{64,72,80,88,96,104,112,120},{128,136,144,152,1..., dimensions={0} | all-to-all | bytes 524288 | tf_op jit(solution)/shard_map/all_to_all | solution.py:47
  47.3 1.0 shard_map.132
  48.3 13.9 %all_to_all.21.packed = bf16[32,48,128]{2,1,0:T(8,128)(2,1)S(1)} all-to-all(bf16[32,48,128]{2,1,0:T(8,128)(2,1)S(1)} %get-tuple-element.32), channel_id=1, replica_groups=mesh['col'=32,'dom'=8] {'col'}, dimensions={0} | all-to-all | bytes 786432 | tf_op jit(solution)/shard_map/all_to_all | solution.py:47
  62.3 0.7 shard_map.133
  63.0 5.2 %all-to-all-start.2 = ((f32[32,8,128]{2,1,0:T(8,128)}), f32[32,8,128]{2,1,0:T(8,128)S(1)}, u32[]{:S(2)}, u32[]{:S(2)}) async-start(f32[32,8,128]{2,1,0:T(8,128)} %get-tuple-element.36), calls=%async_computation.2 | async-start | bytes 262144 | tf_op jit(solution)/shard_map/all_to_all | solution.py:47
  68.2 4.9 %shard_map.134 = (bf16[1040,128]{1,0:T(8,128)(2,1)S(1)}, bf16[1040,128]{1,0:T(8,128)(2,1)S(1)}) custom-call(s32[160]{0:T(256)S(1)} %multiply_add_fusion.ids, s32[160,128,128]{2,1,0:T(8,128)} %mask.3, bf16[32,48,128]{2,1,0:T(8,128)(2,1)S(1)} %all_to_all.21.packed, f32[1,256]{1,0:T(1,128)S(1)} %get-tuple-element.33.bias), custom_call_target="tpu_custom_call" | custom-call | flops 671088640 | tf_op jit(solution)/shard_map/pallas_call | solution.py:360
  73.1 6.3 %collective-permute-start.13 = (bf16[1040,128]{1,0:T(8,128)(2,1)S(1)}, bf16[1040,128]{1,0:T(8,128)(2,1)S(1)}, u32[]{:S(2)}, u32[]{:S(2)}) collective-permute-start(bf16[1040,128]{1,0:T(8,128)(2,1)S(1)} %get-tuple-element.35), channel_id=1, source_target_pairs={{0,1},{1,0},{2,3},{3,2},{4,5},{5,4},{6,7},{7,6},{8,9},{9,8},{10,11... | collective-permute-start | bytes 798728 | tf_op jit(solution)/shard_map/ppermute | solution.py:43
  79.4 5.3 %collective-permute-start.14 = (f32[32,8,128]{2,1,0:T(8,128)S(1)}, f32[32,8,128]{2,1,0:T(8,128)S(1)}, u32[]{:S(2)}, u32[]{:S(2)}) collective-permute-start(f32[32,8,128]{2,1,0:T(8,128)S(1)} %all-to-all-done.2.grads), channel_id=1, source_target_pairs={{0,1},{1,0},{2,3},{3,2},{4,5},{5,4},{6,7},{7,6},{8,9},{9,8},{10,11... | collective-permute-start | bytes 393224 | tf_op jit(solution)/shard_map/ppermute | solution.py:43
  84.7 1.0 %collective-permute-done.14.grads_got = f32[32,8,128]{2,1,0:T(8,128)S(1)} collective-permute-done((f32[32,8,128]{2,1,0:T(8,128)S(1)}, f32[32,8,128]{2,1,0:T(8,128)S(1)}, u32[]{:S(2)}, u32[]{:S(2)}) %collective-permute-start.14) | collective-permute-done | bytes 131104 | tf_op jit(solution)/shard_map/ppermute | solution.py:43
  85.8 11.8 %all_to_all.22.parts = bf16[4,528,128]{2,1,0:T(8,128)(2,1)S(1)} all-to-all(bf16[4,528,128]{2,1,0:T(8,128)(2,1)S(1)} %shard_map.135), channel_id=1, replica_groups={{0,2,4,6},{1,3,5,7},{8,10,12,14},{9,11,13,15},{16,18,20,22},{17,19,21,2..., dimensions={0} | all-to-all | bytes 1081344 | tf_op jit(solution)/shard_map/all_to_all | solution.py:47
  97.5 0.8 shard_map.136
  (25 shorter events, 0.2 us)
Async XLA Ops:
  0.6 46.7 %copy-start.1 = (bf16[32,256]{1,0:T(8,128)(2,1)S(1)}, bf16[32,256]{1,0:T(8,128)(2,1)}, u32[]{:S(2)}) copy-start(bf16[32,256]{1,0:T(8,128)(2,1)} %upstream.1) | copy-start | bytes 49156
  0.6 46.7 %copy-start.5 = (s32[32]{0:T(128)S(1)}, s32[32]{0:T(128)}, u32[]{:S(2)}) copy-start(s32[32]{0:T(128)} %param.18) | copy-start | bytes 388
  0.7 46.7 %copy-start.3 = (f32[256]{0:T(256)S(1)}, f32[256]{0:T(256)}, u32[]{:S(2)}) copy-start(f32[256]{0:T(256)} %param.14) | copy-start | bytes 3076
  0.7 46.7 %copy-start = (bf16[128,256]{1,0:T(8,128)(2,1)S(1)}, bf16[128,256]{1,0:T(8,128)(2,1)}, u32[]{:S(2)}) copy-start(bf16[128,256]{1,0:T(8,128)(2,1)} %weight.1) | copy-start | bytes 196612
  0.7 46.7 %copy-start.4 = (f32[128]{0:T(128)S(1)}, f32[128]{0:T(128)}, u32[]{:S(2)}) copy-start(f32[128]{0:T(128)} %param.12) | copy-start | bytes 1540
  1.7 7.4 %collective-permute-start.5 = (bf16[256,128]{1,0:T(8,128)(2,1)S(1)}, bf16[256,128]{1,0:T(8,128)(2,1)S(1)}, u32[]{:S(2)}, u32[]{:S(2)}) collective-permute-start(bf16[256,128]{1,0:T(8,128)(2,1)S(1)} %multiply_convert_fusion.refs_0_), channel_id=1, source_target_pairs={{0,6},{1,7},{2,4},{3,5},{4,2},{5,3},{6,0},{7,1},{8,14},{9,15},{10,... | collective-permute-start | bytes 196616 | tf_op jit(solution)/shard_map/ppermute | solution.py:43
  5.1 6.0 %collective-permute-start.3 = (bf16[256,128]{1,0:T(8,128)(2,1)S(1)}, bf16[256,128]{1,0:T(8,128)(2,1)S(1)}, u32[]{:S(2)}, u32[]{:S(2)}) collective-permute-start(bf16[256,128]{1,0:T(8,128)(2,1)S(1)} %multiply_convert_fusion.refs_0_), channel_id=1, source_target_pairs={{0,4},{1,5},{2,6},{3,7},{4,0},{5,1},{6,2},{7,3},{8,12},{9,13},{10,... | collective-permute-start | bytes 196616 | tf_op jit(solution)/shard_map/ppermute | solution.py:43
  5.6 6.2 %collective-permute-start.1 = (bf16[256,128]{1,0:T(8,128)(2,1)S(1)}, bf16[256,128]{1,0:T(8,128)(2,1)S(1)}, u32[]{:S(2)}, u32[]{:S(2)}) collective-permute-start(bf16[256,128]{1,0:T(8,128)(2,1)S(1)} %multiply_convert_fusion.refs_0_), channel_id=1, source_target_pairs={{0,2},{1,3},{2,0},{3,1},{4,6},{5,7},{6,4},{7,5},{8,10},{9,11},{10,... | collective-permute-start | bytes 196616 | tf_op jit(solution)/shard_map/ppermute | solution.py:43
  5.7 7.0 %collective-permute-start = (bf16[256,128]{1,0:T(8,128)(2,1)S(1)}, bf16[256,128]{1,0:T(8,128)(2,1)S(1)}, u32[]{:S(2)}, u32[]{:S(2)}) collective-permute-start(bf16[256,128]{1,0:T(8,128)(2,1)S(1)} %multiply_convert_fusion.refs_0_), channel_id=1, source_target_pairs={{0,1},{1,0},{2,3},{3,2},{4,5},{5,4},{6,7},{7,6},{8,9},{9,8},{10,11... | collective-permute-start | bytes 196616 | tf_op jit(solution)/shard_map/ppermute | solution.py:43
  9.1 3.6 %collective-permute-start.6 = (bf16[256,128]{1,0:T(8,128)(2,1)S(1)}, bf16[256,128]{1,0:T(8,128)(2,1)S(1)}, u32[]{:S(2)}, u32[]{:S(2)}) collective-permute-start(bf16[256,128]{1,0:T(8,128)(2,1)S(1)} %collective-permute-done.5.refs_6_), channel_id=1, source_target_pairs={{0,1},{1,0},{2,3},{3,2},{4,5},{5,4},{6,7},{7,6},{8,9},{9,8},{10,11... | collective-permute-start | bytes 196616 | tf_op jit(solution)/shard_map/ppermute | solution.py:43
  11.1 1.7 %collective-permute-start.4 = (bf16[256,128]{1,0:T(8,128)(2,1)S(1)}, bf16[256,128]{1,0:T(8,128)(2,1)S(1)}, u32[]{:S(2)}, u32[]{:S(2)}) collective-permute-start(bf16[256,128]{1,0:T(8,128)(2,1)S(1)} %collective-permute-done.3.refs_4_), channel_id=1, source_target_pairs={{0,1},{1,0},{2,3},{3,2},{4,5},{5,4},{6,7},{7,6},{8,9},{9,8},{10,11... | collective-permute-start | bytes 196616 | tf_op jit(solution)/shard_map/ppermute | solution.py:43
  11.8 1.3 %collective-permute-start.2 = (bf16[256,128]{1,0:T(8,128)(2,1)S(1)}, bf16[256,128]{1,0:T(8,128)(2,1)S(1)}, u32[]{:S(2)}, u32[]{:S(2)}) collective-permute-start(bf16[256,128]{1,0:T(8,128)(2,1)S(1)} %collective-permute-done.1.refs_2_), channel_id=1, source_target_pairs={{0,1},{1,0},{2,3},{3,2},{4,5},{5,4},{6,7},{7,6},{8,9},{9,8},{10,11... | collective-permute-start | bytes 196616 | tf_op jit(solution)/shard_map/ppermute | solution.py:43
  17.6 79.9 %copy-start.2 = (f32[256]{0:T(256)S(1)}, f32[256]{0:T(256)}, u32[]{:S(2)}) copy-start(f32[256]{0:T(256)} %param.11) | copy-start | bytes 3076
  17.6 6.2 %collective-permute-start.8 = (bf16[4,128,128]{2,1,0:T(8,128)(2,1)S(1)}, bf16[4,128,128]{2,1,0:T(8,128)(2,1)S(1)}, u32[]{:S(2)}, u32[]{:S(2)}) collective-permute-start(bf16[4,128,128]{2,1,0:T(8,128)(2,1)S(1)} %get-tuple-element.25), channel_id=1, source_target_pairs={{0,64},{8,72},{16,80},{24,88},{32,96},{40,104},{48,112},{56,120},{... | collective-permute-start | bytes 393224 | tf_op jit(solution)/shard_map/ppermute | solution.py:153
  19.0 4.9 %collective-permute-start.9 = (bf16[4,128,128]{2,1,0:T(8,128)(2,1)S(1)}, bf16[4,128,128]{2,1,0:T(8,128)(2,1)S(1)}, u32[]{:S(2)}, u32[]{:S(2)}) collective-permute-start(bf16[4,128,128]{2,1,0:T(8,128)(2,1)S(1)} %get-tuple-element.27), channel_id=1, source_target_pairs={{0,192},{8,200},{16,208},{24,216},{32,224},{40,232},{48,240},{56,2... | collective-permute-start | bytes 393224 | tf_op jit(solution)/shard_map/ppermute | solution.py:153
  20.5 6.2 %collective-permute-start.7 = (bf16[4,128,128]{2,1,0:T(8,128)(2,1)S(1)}, bf16[4,128,128]{2,1,0:T(8,128)(2,1)S(1)}, u32[]{:S(2)}, u32[]{:S(2)}) collective-permute-start(bf16[4,128,128]{2,1,0:T(8,128)(2,1)S(1)} %get-tuple-element.23), channel_id=1, source_target_pairs={{0,192},{8,200},{16,208},{24,216},{32,224},{40,232},{48,240},{56,2... | collective-permute-start | bytes 393224 | tf_op jit(solution)/shard_map/ppermute | solution.py:153
  21.9 5.0 %collective-permute-start.11 = (bf16[4,128,128]{2,1,0:T(8,128)(2,1)S(1)}, bf16[4,128,128]{2,1,0:T(8,128)(2,1)S(1)}, u32[]{:S(2)}, u32[]{:S(2)}) collective-permute-start(bf16[4,128,128]{2,1,0:T(8,128)(2,1)S(1)} %get-tuple-element.29), channel_id=1, source_target_pairs={{0,64},{8,72},{16,80},{24,88},{32,96},{40,104},{48,112},{56,120},{... | collective-permute-start | bytes 393224 | tf_op jit(solution)/shard_map/ppermute | solution.py:153
  24.0 5.9 %collective-permute-start.10 = (bf16[4,128,128]{2,1,0:T(8,128)(2,1)S(1)}, bf16[4,128,128]{2,1,0:T(8,128)(2,1)S(1)}, u32[]{:S(2)}, u32[]{:S(2)}) collective-permute-start(bf16[4,128,128]{2,1,0:T(8,128)(2,1)S(1)} %get-tuple-element.28), channel_id=1, source_target_pairs={{0,64},{8,72},{16,80},{24,88},{32,96},{40,104},{48,112},{56,120},{... | collective-permute-start | bytes 393224 | tf_op jit(solution)/shard_map/ppermute | solution.py:153
  25.1 4.7 %collective-permute-start.12 = (bf16[4,128,128]{2,1,0:T(8,128)(2,1)S(1)}, bf16[4,128,128]{2,1,0:T(8,128)(2,1)S(1)}, u32[]{:S(2)}, u32[]{:S(2)}) collective-permute-start(bf16[4,128,128]{2,1,0:T(8,128)(2,1)S(1)} %get-tuple-element.30), channel_id=1, source_target_pairs={{0,192},{8,200},{16,208},{24,216},{32,224},{40,232},{48,240},{56,2... | collective-permute-start | bytes 393224 | tf_op jit(solution)/shard_map/ppermute | solution.py:153
  63.0 16.5 %all-to-all-start.2 = ((f32[32,8,128]{2,1,0:T(8,128)}), f32[32,8,128]{2,1,0:T(8,128)S(1)}, u32[]{:S(2)}, u32[]{:S(2)}) async-start(f32[32,8,128]{2,1,0:T(8,128)} %get-tuple-element.36), calls=%async_computation.2 | async-start | bytes 262144 | tf_op jit(solution)/shard_map/all_to_all | solution.py:47
  73.1 11.6 %collective-permute-start.13 = (bf16[1040,128]{1,0:T(8,128)(2,1)S(1)}, bf16[1040,128]{1,0:T(8,128)(2,1)S(1)}, u32[]{:S(2)}, u32[]{:S(2)}) collective-permute-start(bf16[1040,128]{1,0:T(8,128)(2,1)S(1)} %get-tuple-element.35), channel_id=1, source_target_pairs={{0,1},{1,0},{2,3},{3,2},{4,5},{5,4},{6,7},{7,6},{8,9},{9,8},{10,11... | collective-permute-start | bytes 798728 | tf_op jit(solution)/shard_map/ppermute | solution.py:43
  79.4 6.3 %collective-permute-start.14 = (f32[32,8,128]{2,1,0:T(8,128)S(1)}, f32[32,8,128]{2,1,0:T(8,128)S(1)}, u32[]{:S(2)}, u32[]{:S(2)}) collective-permute-start(f32[32,8,128]{2,1,0:T(8,128)S(1)} %all-to-all-done.2.grads), channel_id=1, source_target_pairs={{0,1},{1,0},{2,3},{3,2},{4,5},{5,4},{6,7},{7,6},{8,9},{9,8},{10,11... | collective-permute-start | bytes 393224 | tf_op jit(solution)/shard_map/ppermute | solution.py:43

commit v6 on v5

--- a/solution.py
+++ b/solution.py
@@ -153,6 +153,13 @@
     return lax.ppermute(value, "col", pairs)
 
 
+def thirds(value):
+    high = value.astype(BF16)
+    rest = value - high.astype(F32)
+    middle = rest.astype(BF16)
+    return high, middle, (rest - middle.astype(F32)).astype(BF16)
+
+
 def dense_kernel(parts, dest_scale, weight, bias, targets, upstream, hidden, packed):
     summed = parts[0].astype(F32)
     for z in range(1, NZ):
@@ -164,10 +171,9 @@
     hidden[...] = (preact * sigmoid(preact)).astype(BF16)
     wanted = targets[...]
     row_ids = lax.broadcasted_iota(jnp.int32, (BLK, TGT), 0)
-    chosen = (row_ids == wanted).astype(F32)
-    chosen_b = chosen.astype(BF16)
+    chosen = (row_ids == wanted).astype(BF16)
     agg_t = lax.dot_general(
-        chosen_b, aggregated, (((0,), (0,)), ((), ())), preferred_element_type=F32
+        chosen, aggregated, (((0,), (0,)), ((), ())), preferred_element_type=F32
     ).astype(BF16)
     pre_t = jnp.dot(agg_t, w, preferred_element_type=F32) + bias[...]
     s = sigmoid(pre_t)
@@ -180,14 +186,14 @@
         slope, w, (((1,), (1,)), ((), ())), preferred_element_type=F32
     )
     same = lax.dot_general(
-        chosen_b, chosen_b, (((0,), (0,)), ((), ())), preferred_element_type=F32
-    )
-    collected = jnp.dot(
-        same, term, preferred_element_type=F32, precision=lax.Precision.HIGHEST
-    )
-    scale_t = lax.dot_general(
-        chosen, scale, (((0,), (0,)), ((), ())), preferred_element_type=F32,
-        precision=lax.Precision.HIGHEST,
+        chosen, chosen, (((0,), (0,)), ((), ())), preferred_element_type=F32
+    )
+    collected = sum(
+        jnp.dot(same.astype(BF16), third, preferred_element_type=F32) for third in thirds(term)
+    )
+    scale_t = sum(
+        lax.dot_general(chosen, third, (((0,), (0,)), ((), ())), preferred_element_type=F32)
+        for third in thirds(scale)
     )
     k_row = lax.broadcasted_iota(jnp.int32, (TGT, TGT), 0)
     k_col = lax.broadcasted_iota(jnp.int32, (TGT, TGT), 1)

time: 98.6 us -> 98.5 us (level)
  no operation moved by 1% of the time
where the time goes in v6:
time: 98.5 us; the launch traced here: 98.2 us
  blocking collectives  43.1 us (44%)
  starting transfers between devices  34.2 us (35%)
  Pallas kernels  12.1 us (12%)
  waiting for transfers between devices  6.31 us (6%)
  other arithmetic  1.68 us (2%)
    all_to_all x3, blocking collectives, swap(): lax.all_to_all(value, axis, 0, 0, axis_index_groups=groups, tiled=True)  43.1 us
    ppermute x9, starting transfers between devices, exchange_dom(): return lax.ppermute(value, 'dom', pairs)  21.9 us
    ppermute x6, starting transfers between devices, step_y(): return lax.ppermute(value, 'col', pairs)  7.13 us
    all_to_all x1, starting transfers between devices, swap(): lax.all_to_all(value, axis, 0, 0, axis_index_groups=groups, tiled=True)  5.22 us
    ppermute x6, waiting for transfers between devices, step_y(): return lax.ppermute(value, 'col', pairs)  5.01 us
    pallas_call x1, Pallas kernels, body(): call(backward_kernel, [sds((NX * 256 + 16, F), BF16)] * 2, [HBM, HBM, VME...  4.97 us
    pallas_call x1, Pallas kernels, forward(): pl.pallas_call(forward_kernel, out_shape=[sds((NZ, BLK, F), BF16)] + [sds...  4.57 us
  transfers between devices with their start and end apart: 16, of which 5 were waited for; matrix products, arithmetic and copies ran while one was open for 1% of the time, Pallas kernels for 5%

profile of v6, /device:TPU:1, one launch (start us, length us, event | category | flops | bytes accessed | tf_op | source)
XLA Modules:
  0.0 98.2 jit_solution(17676194960249578332)
XLA Ops:
  0.7 1.0 %multiply_convert_fusion.refs_0_ = bf16[256,128]{1,0:T(8,128)(2,1)S(1)} fusion(bf16[256,128]{1,0:T(8,128)(2,1)} %param.10, f32[256]{0:T(256)} %param.11), kind=kLoop, calls=%fused_computation | loop fusion | flops 98304 | bytes 132096 | tf_op jit(solution)/shard_map/convert_element_type | solution.py:333
  1.7 3.4 %collective-permute-start.5 = (bf16[256,128]{1,0:T(8,128)(2,1)S(1)}, bf16[256,128]{1,0:T(8,128)(2,1)S(1)}, u32[]{:S(2)}, u32[]{:S(2)}) collective-permute-start(bf16[256,128]{1,0:T(8,128)(2,1)S(1)} %multiply_convert_fusion.refs_0_), channel_id=1, source_target_pairs={{0,6},{1,7},{2,4},{3,5},{4,2},{5,3},{6,0},{7,1},{8,14},{9,15},{10,... | collective-permute-start | bytes 196616 | tf_op jit(solution)/shard_map/ppermute | solution.py:43
  5.1 0.5 collective-permute-start.3
  5.6 0.2 collective-permute-start.1
  5.7 3.3 %collective-permute-start = (bf16[256,128]{1,0:T(8,128)(2,1)S(1)}, bf16[256,128]{1,0:T(8,128)(2,1)S(1)}, u32[]{:S(2)}, u32[]{:S(2)}) collective-permute-start(bf16[256,128]{1,0:T(8,128)(2,1)S(1)} %multiply_convert_fusion.refs_0_), channel_id=1, source_target_pairs={{0,1},{1,0},{2,3},{3,2},{4,5},{5,4},{6,7},{7,6},{8,9},{9,8},{10,11... | collective-permute-start | bytes 196616 | tf_op jit(solution)/shard_map/ppermute | solution.py:43
  9.1 2.0 %collective-permute-start.6 = (bf16[256,128]{1,0:T(8,128)(2,1)S(1)}, bf16[256,128]{1,0:T(8,128)(2,1)S(1)}, u32[]{:S(2)}, u32[]{:S(2)}) collective-permute-start(bf16[256,128]{1,0:T(8,128)(2,1)S(1)} %collective-permute-done.5.refs_6_), channel_id=1, source_target_pairs={{0,1},{1,0},{2,3},{3,2},{4,5},{5,4},{6,7},{7,6},{8,9},{9,8},{10,11... | collective-permute-start | bytes 196616 | tf_op jit(solution)/shard_map/ppermute | solution.py:43
  11.1 0.7 collective-permute-start.4
  11.8 0.2 collective-permute-start.2
  12.0 0.7 multiply_add_fusion.ids
  12.8 0.3 collective-permute-done.2.refs_3_
  13.1 4.6 %shard_map.129 = (bf16[8,128,128]{2,1,0:T(8,128)(2,1)S(1)}, bf16[4,128,128]{2,1,0:T(8,128)(2,1)S(1)}, bf16[4,128,128]{2,1,0:T(8,128)(2,1)S(1)}, bf16[4,128,128]{...) custom-call(s32[160]{0:T(256)S(1)} %multiply_add_fusion.ids, ...), custom_call_target="tpu_custom_call" | custom-call | flops 671088640 | bytes 10485760 | tf_op jit(solution)/shard_map/pallas_call | solution.py:111
  17.6 1.4 %collective-permute-start.8 = (bf16[4,128,128]{2,1,0:T(8,128)(2,1)S(1)}, bf16[4,128,128]{2,1,0:T(8,128)(2,1)S(1)}, u32[]{:S(2)}, u32[]{:S(2)}) collective-permute-start(bf16[4,128,128]{2,1,0:T(8,128)(2,1)S(1)} %get-tuple-element.25), channel_id=1, source_target_pairs={{0,64},{8,72},{16,80},{24,88},{32,96},{40,104},{48,112},{56,120},{... | collective-permute-start | bytes 393224 | tf_op jit(solution)/shard_map/ppermute | solution.py:153
  19.0 1.5 %collective-permute-start.9 = (bf16[4,128,128]{2,1,0:T(8,128)(2,1)S(1)}, bf16[4,128,128]{2,1,0:T(8,128)(2,1)S(1)}, u32[]{:S(2)}, u32[]{:S(2)}) collective-permute-start(bf16[4,128,128]{2,1,0:T(8,128)(2,1)S(1)} %get-tuple-element.27), channel_id=1, source_target_pairs={{0,192},{8,200},{16,208},{24,216},{32,224},{40,232},{48,240},{56,2... | collective-permute-start | bytes 393224 | tf_op jit(solution)/shard_map/ppermute | solution.py:153
  20.5 1.4 %collective-permute-start.7 = (bf16[4,128,128]{2,1,0:T(8,128)(2,1)S(1)}, bf16[4,128,128]{2,1,0:T(8,128)(2,1)S(1)}, u32[]{:S(2)}, u32[]{:S(2)}) collective-permute-start(bf16[4,128,128]{2,1,0:T(8,128)(2,1)S(1)} %get-tuple-element.23), channel_id=1, source_target_pairs={{0,192},{8,200},{16,208},{24,216},{32,224},{40,232},{48,240},{56,2... | collective-permute-start | bytes 393224 | tf_op jit(solution)/shard_map/ppermute | solution.py:153
  21.9 0.1 collective-permute-start.11
  22.0 1.9 %collective-permute-done.8.far_up = bf16[4,128,128]{2,1,0:T(8,128)(2,1)S(1)} collective-permute-done((bf16[4,128,128]{2,1,0:T(8,128)(2,1)S(1)}, bf16[4,128,128]{2,1,0:T(8,128)(2,1)S(1)}, u32[]{:S(2)}, u32[]{:S(2)}) %collective-permute-start.8) | collective-permute-done | bytes 131104 | tf_op jit(solution)/shard_map/ppermute | solution.py:153
  24.0 1.1 %collective-permute-start.10 = (bf16[4,128,128]{2,1,0:T(8,128)(2,1)S(1)}, bf16[4,128,128]{2,1,0:T(8,128)(2,1)S(1)}, u32[]{:S(2)}, u32[]{:S(2)}) collective-permute-start(bf16[4,128,128]{2,1,0:T(8,128)(2,1)S(1)} %get-tuple-element.28), channel_id=1, source_target_pairs={{0,64},{8,72},{16,80},{24,88},{32,96},{40,104},{48,112},{56,120},{... | collective-permute-start | bytes 393224 | tf_op jit(solution)/shard_map/ppermute | solution.py:153
  25.1 1.7 %collective-permute-start.12 = (bf16[4,128,128]{2,1,0:T(8,128)(2,1)S(1)}, bf16[4,128,128]{2,1,0:T(8,128)(2,1)S(1)}, u32[]{:S(2)}, u32[]{:S(2)}) collective-permute-start(bf16[4,128,128]{2,1,0:T(8,128)(2,1)S(1)} %get-tuple-element.30), channel_id=1, source_target_pairs={{0,192},{8,200},{16,208},{24,216},{32,224},{40,232},{48,240},{56,2... | collective-permute-start | bytes 393224 | tf_op jit(solution)/shard_map/ppermute | solution.py:153
  26.7 0.2 collective-permute-done.11.high_below
  27.0 2.9 %collective-permute-done.10.low_below = bf16[4,128,128]{2,1,0:T(8,128)(2,1)S(1)} collective-permute-done((bf16[4,128,128]{2,1,0:T(8,128)(2,1)S(1)}, bf16[4,128,128]{2,1,0:T(8,128)(2,1)S(1)}, u32[]{:S(2)}, u32[]{:S(2)}) %collective-permute-start.10) | collective-permute-done | bytes 131104 | tf_op jit(solution)/shard_map/ppermute | solution.py:153
  29.8 0.1 shard_map.131
  29.9 17.4 %all_to_all.20.parts = bf16[8,128,128]{2,1,0:T(8,128)(2,1)S(1)} all-to-all(bf16[8,128,128]{2,1,0:T(8,128)(2,1)S(1)} %shard_map.131), channel_id=1, replica_groups={{0,8,16,24,32,40,48,56},{64,72,80,88,96,104,112,120},{128,136,144,152,1..., dimensions={0} | all-to-all | bytes 524288 | tf_op jit(solution)/shard_map/all_to_all | solution.py:47
  47.3 0.9 shard_map.132
  48.2 13.9 %all_to_all.21.packed = bf16[32,48,128]{2,1,0:T(8,128)(2,1)S(1)} all-to-all(bf16[32,48,128]{2,1,0:T(8,128)(2,1)S(1)} %get-tuple-element.32), channel_id=1, replica_groups=mesh['col'=32,'dom'=8] {'col'}, dimensions={0} | all-to-all | bytes 786432 | tf_op jit(solution)/shard_map/all_to_all | solution.py:47
  62.1 0.7 shard_map.133
  62.8 5.2 %all-to-all-start.2 = ((f32[32,8,128]{2,1,0:T(8,128)}), f32[32,8,128]{2,1,0:T(8,128)S(1)}, u32[]{:S(2)}, u32[]{:S(2)}) async-start(f32[32,8,128]{2,1,0:T(8,128)} %get-tuple-element.36), calls=%async_computation.2 | async-start | bytes 262144 | tf_op jit(solution)/shard_map/all_to_all | solution.py:47
  68.1 5.0 %shard_map.134 = (bf16[1040,128]{1,0:T(8,128)(2,1)S(1)}, bf16[1040,128]{1,0:T(8,128)(2,1)S(1)}) custom-call(s32[160]{0:T(256)S(1)} %multiply_add_fusion.ids, s32[160,128,128]{2,1,0:T(8,128)} %mask.3, bf16[32,48,128]{2,1,0:T(8,128)(2,1)S(1)} %all_to_all.21.packed, f32[1,256]{1,0:T(1,128)S(1)} %get-tuple-element.33.bias), custom_call_target="tpu_custom_call" | custom-call | flops 671088640 | tf_op jit(solution)/shard_map/pallas_call | solution.py:366
  73.0 6.3 %collective-permute-start.13 = (bf16[1040,128]{1,0:T(8,128)(2,1)S(1)}, bf16[1040,128]{1,0:T(8,128)(2,1)S(1)}, u32[]{:S(2)}, u32[]{:S(2)}) collective-permute-start(bf16[1040,128]{1,0:T(8,128)(2,1)S(1)} %get-tuple-element.35), channel_id=1, source_target_pairs={{0,1},{1,0},{2,3},{3,2},{4,5},{5,4},{6,7},{7,6},{8,9},{9,8},{10,11... | collective-permute-start | bytes 798728 | tf_op jit(solution)/shard_map/ppermute | solution.py:43
  79.3 5.2 %collective-permute-start.14 = (f32[32,8,128]{2,1,0:T(8,128)S(1)}, f32[32,8,128]{2,1,0:T(8,128)S(1)}, u32[]{:S(2)}, u32[]{:S(2)}) collective-permute-start(f32[32,8,128]{2,1,0:T(8,128)S(1)} %all-to-all-done.2.grads), channel_id=1, source_target_pairs={{0,1},{1,0},{2,3},{3,2},{4,5},{5,4},{6,7},{7,6},{8,9},{9,8},{10,11... | collective-permute-start | bytes 393224 | tf_op jit(solution)/shard_map/ppermute | solution.py:43
  84.6 1.0 %collective-permute-done.14.grads_got = f32[32,8,128]{2,1,0:T(8,128)S(1)} collective-permute-done((f32[32,8,128]{2,1,0:T(8,128)S(1)}, f32[32,8,128]{2,1,0:T(8,128)S(1)}, u32[]{:S(2)}, u32[]{:S(2)}) %collective-permute-start.14) | collective-permute-done | bytes 131104 | tf_op jit(solution)/shard_map/ppermute | solution.py:43
  85.6 11.8 %all_to_all.22.parts = bf16[4,528,128]{2,1,0:T(8,128)(2,1)S(1)} all-to-all(bf16[4,528,128]{2,1,0:T(8,128)(2,1)S(1)} %shard_map.135), channel_id=1, replica_groups={{0,2,4,6},{1,3,5,7},{8,10,12,14},{9,11,13,15},{16,18,20,22},{17,19,21,2..., dimensions={0} | all-to-all | bytes 1081344 | tf_op jit(solution)/shard_map/all_to_all | solution.py:47
  97.4 0.8 shard_map.136
  (25 shorter events, 0.2 us)
Async XLA Ops:
  0.6 46.7 %copy-start.1 = (bf16[32,256]{1,0:T(8,128)(2,1)S(1)}, bf16[32,256]{1,0:T(8,128)(2,1)}, u32[]{:S(2)}) copy-start(bf16[32,256]{1,0:T(8,128)(2,1)} %upstream.1) | copy-start | bytes 49156
  0.6 46.7 %copy-start.5 = (s32[32]{0:T(128)S(1)}, s32[32]{0:T(128)}, u32[]{:S(2)}) copy-start(s32[32]{0:T(128)} %param.18) | copy-start | bytes 388
  0.7 46.7 %copy-start.3 = (f32[256]{0:T(256)S(1)}, f32[256]{0:T(256)}, u32[]{:S(2)}) copy-start(f32[256]{0:T(256)} %param.14) | copy-start | bytes 3076
  0.7 46.7 %copy-start = (bf16[128,256]{1,0:T(8,128)(2,1)S(1)}, bf16[128,256]{1,0:T(8,128)(2,1)}, u32[]{:S(2)}) copy-start(bf16[128,256]{1,0:T(8,128)(2,1)} %weight.1) | copy-start | bytes 196612
  0.7 46.7 %copy-start.4 = (f32[128]{0:T(128)S(1)}, f32[128]{0:T(128)}, u32[]{:S(2)}) copy-start(f32[128]{0:T(128)} %param.12) | copy-start | bytes 1540
  1.7 7.4 %collective-permute-start.5 = (bf16[256,128]{1,0:T(8,128)(2,1)S(1)}, bf16[256,128]{1,0:T(8,128)(2,1)S(1)}, u32[]{:S(2)}, u32[]{:S(2)}) collective-permute-start(bf16[256,128]{1,0:T(8,128)(2,1)S(1)} %multiply_convert_fusion.refs_0_), channel_id=1, source_target_pairs={{0,6},{1,7},{2,4},{3,5},{4,2},{5,3},{6,0},{7,1},{8,14},{9,15},{10,... | collective-permute-start | bytes 196616 | tf_op jit(solution)/shard_map/ppermute | solution.py:43
  5.1 6.0 %collective-permute-start.3 = (bf16[256,128]{1,0:T(8,128)(2,1)S(1)}, bf16[256,128]{1,0:T(8,128)(2,1)S(1)}, u32[]{:S(2)}, u32[]{:S(2)}) collective-permute-start(bf16[256,128]{1,0:T(8,128)(2,1)S(1)} %multiply_convert_fusion.refs_0_), channel_id=1, source_target_pairs={{0,4},{1,5},{2,6},{3,7},{4,0},{5,1},{6,2},{7,3},{8,12},{9,13},{10,... | collective-permute-start | bytes 196616 | tf_op jit(solution)/shard_map/ppermute | solution.py:43
  5.6 6.2 %collective-permute-start.1 = (bf16[256,128]{1,0:T(8,128)(2,1)S(1)}, bf16[256,128]{1,0:T(8,128)(2,1)S(1)}, u32[]{:S(2)}, u32[]{:S(2)}) collective-permute-start(bf16[256,128]{1,0:T(8,128)(2,1)S(1)} %multiply_convert_fusion.refs_0_), channel_id=1, source_target_pairs={{0,2},{1,3},{2,0},{3,1},{4,6},{5,7},{6,4},{7,5},{8,10},{9,11},{10,... | collective-permute-start | bytes 196616 | tf_op jit(solution)/shard_map/ppermute | solution.py:43
  5.7 7.0 %collective-permute-start = (bf16[256,128]{1,0:T(8,128)(2,1)S(1)}, bf16[256,128]{1,0:T(8,128)(2,1)S(1)}, u32[]{:S(2)}, u32[]{:S(2)}) collective-permute-start(bf16[256,128]{1,0:T(8,128)(2,1)S(1)} %multiply_convert_fusion.refs_0_), channel_id=1, source_target_pairs={{0,1},{1,0},{2,3},{3,2},{4,5},{5,4},{6,7},{7,6},{8,9},{9,8},{10,11... | collective-permute-start | bytes 196616 | tf_op jit(solution)/shard_map/ppermute | solution.py:43
  9.1 3.6 %collective-permute-start.6 = (bf16[256,128]{1,0:T(8,128)(2,1)S(1)}, bf16[256,128]{1,0:T(8,128)(2,1)S(1)}, u32[]{:S(2)}, u32[]{:S(2)}) collective-permute-start(bf16[256,128]{1,0:T(8,128)(2,1)S(1)} %collective-permute-done.5.refs_6_), channel_id=1, source_target_pairs={{0,1},{1,0},{2,3},{3,2},{4,5},{5,4},{6,7},{7,6},{8,9},{9,8},{10,11... | collective-permute-start | bytes 196616 | tf_op jit(solution)/shard_map/ppermute | solution.py:43
  11.1 1.7 %collective-permute-start.4 = (bf16[256,128]{1,0:T(8,128)(2,1)S(1)}, bf16[256,128]{1,0:T(8,128)(2,1)S(1)}, u32[]{:S(2)}, u32[]{:S(2)}) collective-permute-start(bf16[256,128]{1,0:T(8,128)(2,1)S(1)} %collective-permute-done.3.refs_4_), channel_id=1, source_target_pairs={{0,1},{1,0},{2,3},{3,2},{4,5},{5,4},{6,7},{7,6},{8,9},{9,8},{10,11... | collective-permute-start | bytes 196616 | tf_op jit(solution)/shard_map/ppermute | solution.py:43
  11.8 1.3 %collective-permute-start.2 = (bf16[256,128]{1,0:T(8,128)(2,1)S(1)}, bf16[256,128]{1,0:T(8,128)(2,1)S(1)}, u32[]{:S(2)}, u32[]{:S(2)}) collective-permute-start(bf16[256,128]{1,0:T(8,128)(2,1)S(1)} %collective-permute-done.1.refs_2_), channel_id=1, source_target_pairs={{0,1},{1,0},{2,3},{3,2},{4,5},{5,4},{6,7},{7,6},{8,9},{9,8},{10,11... | collective-permute-start | bytes 196616 | tf_op jit(solution)/shard_map/ppermute | solution.py:43
  17.6 79.8 %copy-start.2 = (f32[256]{0:T(256)S(1)}, f32[256]{0:T(256)}, u32[]{:S(2)}) copy-start(f32[256]{0:T(256)} %param.11) | copy-start | bytes 3076
  17.6 6.3 %collective-permute-start.8 = (bf16[4,128,128]{2,1,0:T(8,128)(2,1)S(1)}, bf16[4,128,128]{2,1,0:T(8,128)(2,1)S(1)}, u32[]{:S(2)}, u32[]{:S(2)}) collective-permute-start(bf16[4,128,128]{2,1,0:T(8,128)(2,1)S(1)} %get-tuple-element.25), channel_id=1, source_target_pairs={{0,64},{8,72},{16,80},{24,88},{32,96},{40,104},{48,112},{56,120},{... | collective-permute-start | bytes 393224 | tf_op jit(solution)/shard_map/ppermute | solution.py:153
  19.0 4.9 %collective-permute-start.9 = (bf16[4,128,128]{2,1,0:T(8,128)(2,1)S(1)}, bf16[4,128,128]{2,1,0:T(8,128)(2,1)S(1)}, u32[]{:S(2)}, u32[]{:S(2)}) collective-permute-start(bf16[4,128,128]{2,1,0:T(8,128)(2,1)S(1)} %get-tuple-element.27), channel_id=1, source_target_pairs={{0,192},{8,200},{16,208},{24,216},{32,224},{40,232},{48,240},{56,2... | collective-permute-start | bytes 393224 | tf_op jit(solution)/shard_map/ppermute | solution.py:153
  20.5 6.2 %collective-permute-start.7 = (bf16[4,128,128]{2,1,0:T(8,128)(2,1)S(1)}, bf16[4,128,128]{2,1,0:T(8,128)(2,1)S(1)}, u32[]{:S(2)}, u32[]{:S(2)}) collective-permute-start(bf16[4,128,128]{2,1,0:T(8,128)(2,1)S(1)} %get-tuple-element.23), channel_id=1, source_target_pairs={{0,192},{8,200},{16,208},{24,216},{32,224},{40,232},{48,240},{56,2... | collective-permute-start | bytes 393224 | tf_op jit(solution)/shard_map/ppermute | solution.py:153
  21.9 5.0 %collective-permute-start.11 = (bf16[4,128,128]{2,1,0:T(8,128)(2,1)S(1)}, bf16[4,128,128]{2,1,0:T(8,128)(2,1)S(1)}, u32[]{:S(2)}, u32[]{:S(2)}) collective-permute-start(bf16[4,128,128]{2,1,0:T(8,128)(2,1)S(1)} %get-tuple-element.29), channel_id=1, source_target_pairs={{0,64},{8,72},{16,80},{24,88},{32,96},{40,104},{48,112},{56,120},{... | collective-permute-start | bytes 393224 | tf_op jit(solution)/shard_map/ppermute | solution.py:153
  24.0 5.9 %collective-permute-start.10 = (bf16[4,128,128]{2,1,0:T(8,128)(2,1)S(1)}, bf16[4,128,128]{2,1,0:T(8,128)(2,1)S(1)}, u32[]{:S(2)}, u32[]{:S(2)}) collective-permute-start(bf16[4,128,128]{2,1,0:T(8,128)(2,1)S(1)} %get-tuple-element.28), channel_id=1, source_target_pairs={{0,64},{8,72},{16,80},{24,88},{32,96},{40,104},{48,112},{56,120},{... | collective-permute-start | bytes 393224 | tf_op jit(solution)/shard_map/ppermute | solution.py:153
  25.1 4.8 %collective-permute-start.12 = (bf16[4,128,128]{2,1,0:T(8,128)(2,1)S(1)}, bf16[4,128,128]{2,1,0:T(8,128)(2,1)S(1)}, u32[]{:S(2)}, u32[]{:S(2)}) collective-permute-start(bf16[4,128,128]{2,1,0:T(8,128)(2,1)S(1)} %get-tuple-element.30), channel_id=1, source_target_pairs={{0,192},{8,200},{16,208},{24,216},{32,224},{40,232},{48,240},{56,2... | collective-permute-start | bytes 393224 | tf_op jit(solution)/shard_map/ppermute | solution.py:153
  62.8 16.5 %all-to-all-start.2 = ((f32[32,8,128]{2,1,0:T(8,128)}), f32[32,8,128]{2,1,0:T(8,128)S(1)}, u32[]{:S(2)}, u32[]{:S(2)}) async-start(f32[32,8,128]{2,1,0:T(8,128)} %get-tuple-element.36), calls=%async_computation.2 | async-start | bytes 262144 | tf_op jit(solution)/shard_map/all_to_all | solution.py:47
  73.0 11.5 %collective-permute-start.13 = (bf16[1040,128]{1,0:T(8,128)(2,1)S(1)}, bf16[1040,128]{1,0:T(8,128)(2,1)S(1)}, u32[]{:S(2)}, u32[]{:S(2)}) collective-permute-start(bf16[1040,128]{1,0:T(8,128)(2,1)S(1)} %get-tuple-element.35), channel_id=1, source_target_pairs={{0,1},{1,0},{2,3},{3,2},{4,5},{5,4},{6,7},{7,6},{8,9},{9,8},{10,11... | collective-permute-start | bytes 798728 | tf_op jit(solution)/shard_map/ppermute | solution.py:43
  79.3 6.2 %collective-permute-start.14 = (f32[32,8,128]{2,1,0:T(8,128)S(1)}, f32[32,8,128]{2,1,0:T(8,128)S(1)}, u32[]{:S(2)}, u32[]{:S(2)}) collective-permute-start(f32[32,8,128]{2,1,0:T(8,128)S(1)} %all-to-all-done.2.grads), channel_id=1, source_target_pairs={{0,1},{1,0},{2,3},{3,2},{4,5},{5,4},{6,7},{7,6},{8,9},{9,8},{10,11... | collective-permute-start | bytes 393224 | tf_op jit(solution)/shard_map/ppermute | solution.py:43
